TPU v7x, 256 devices: a whole 4x4x8 slice. The times are simulated.
256 devices in a mesh: blk: 256 (over x, y, z, core).
Axes of the slice: x: 4, y: 4, z: 8, core: 2. Of those that a mesh axis runs over, the one named last changes fastest.
Arguments:
- tracers: float32 [1024, 2, 2, 128, 128], P('blk'), may hold values from -6 to 6
- velocity: float32 [1024, 2, 2, 128, 128], P('blk'), may hold values from -5 to 5
- block_counts: int32 [256], replicated, may hold values from 1 to 4, as said below
- land_mask: int32 [26, 34], replicated, may hold values from 0 to 1, as said below
Outputs:
- tracers_out: float32 [1024, 2, 2, 128, 128], P('blk')
- velocity_out: float32 [1024, 2, 2, 128, 128], P('blk')
Inputs may be any that keep to these rules, and one draw needn't show every extreme that they name: `block_counts`: they sum to 538; the first 68 entries are 1. `land_mask`: exactly 538 ocean blocks; the first 68 blocks in row-major order are ocean.
All inputs are finite; a program needn't handle non-finite values.
Results may differ from a plain program's by a relative error of at most 0.00002.
Values sent between devices are 32-bit elements; how exact they have to be, the bound alone decides.
No kernel may reach another device: no remote copies, remote signals or barrier semaphores. Data moves between devices by JAX's collectives and lax.ppermute only.
A program may use at most 128 MiB of HBM per device.

v0:
```python
import jax
import jax.numpy as jnp
from jax import lax
from jax.sharding import PartitionSpec as P

SUBSTEPS = 2


TIME_STEP = 0.1
DIFFUSIVITY = 0.5
VISCOSITY = 0.5
GRAVITY_SCALE = 0.5
CORIOLIS_MEAN = 1.0
CORIOLIS_SLOPE = 2.0


def from_behind(block, axis, distance):
    devices = range(lax.axis_size(axis))
    route = [(i - distance, i) for i in devices if i - distance in devices]
    return lax.ppermute(block, axis, route)


def sea_density(temper, salty):
    return -0.3 * temper + 0.6 * salty - 0.08 * temper * temper + 0.05 * temper * salty


def hydro_pressure(density_now):
    return GRAVITY_SCALE * (jnp.cumsum(density_now, axis=0) - 0.5 * density_now)


def neighbours(field, halo_south, halo_north, halo_west, halo_east):
    north_val = jnp.concatenate([field[:, 1:, :], halo_north[:, None, :]], axis=1)
    south_val = jnp.concatenate([halo_south[:, None, :], field[:, :-1, :]], axis=1)
    east_val = jnp.concatenate([field[:, :, 1:], halo_east[:, :, None]], axis=2)
    west_val = jnp.concatenate([halo_west[:, :, None], field[:, :, :-1]], axis=2)
    return (north_val, south_val, east_val, west_val)


def advance_substep(ocean_fields, halos, opens, first_row, rows_total):
    width = ocean_fields.shape[-1]
    spots = jnp.arange(width)
    open_n = jnp.where(spots == width - 1, opens[1], 1.0)[None, :, None]
    open_s = jnp.where(spots == 0, opens[0], 1.0)[None, :, None]
    open_e = jnp.where(spots == width - 1, opens[3], 1.0)[None, None, :]
    open_w = jnp.where(spots == 0, opens[2], 1.0)[None, None, :]

    def beside_all(index):
        return neighbours(
            ocean_fields[index], halos[0, index], halos[1, index], halos[2, index], halos[3, index]
        )

    east_vel = ocean_fields[2]
    north_vel = ocean_fields[3]
    un_val, us_val, ue_val, uw_val = beside_all(2)
    vn_val, vs_val, ve_val, vw_val = beside_all(3)
    face_e = 0.5 * (east_vel + ue_val)
    face_w = 0.5 * (uw_val + east_vel)
    face_n = 0.5 * (north_vel + vn_val)
    face_s = 0.5 * (vs_val + north_vel)
    results = []
    for index in range(2):
        value = ocean_fields[index]
        cn_val, cs_val, east_center_value, cw_val = beside_all(index)
        flux_e = open_e * face_e * 0.5 * (value + east_center_value)
        flux_w = open_w * face_w * 0.5 * (cw_val + value)
        flux_n = open_n * face_n * 0.5 * (value + cn_val)
        flux_s = open_s * face_s * 0.5 * (cs_val + value)
        laplace = (
            open_e * (east_center_value - value)
            + open_w * (cw_val - value)
            + open_n * (cn_val - value)
            + open_s * (cs_val - value)
        )
        results.append(
            value + TIME_STEP * (-(flux_e - flux_w + flux_n - flux_s) + DIFFUSIVITY * laplace)
        )
    press = hydro_pressure(sea_density(ocean_fields[0], ocean_fields[1]))
    halo_press = [hydro_pressure(sea_density(halos[side, 0], halos[side, 1])) for side in range(4)]
    pn_val, ps_val, pe_val, pw_val = neighbours(
        press, halo_press[0], halo_press[1], halo_press[2], halo_press[3]
    )
    grad_x = 0.5 * (open_e * (pe_val - press) + open_w * (press - pw_val))
    grad_y = 0.5 * (open_n * (pn_val - press) + open_s * (press - ps_val))
    latitude = (first_row + spots.astype(jnp.float32) + 0.5) / rows_total
    coriolis = (CORIOLIS_MEAN + CORIOLIS_SLOPE * (latitude - 0.5))[None, :, None]
    lap_u = (
        open_e * (ue_val - east_vel)
        + open_w * (uw_val - east_vel)
        + open_n * (un_val - east_vel)
        + open_s * (us_val - east_vel)
    )
    lap_v = (
        open_e * (ve_val - north_vel)
        + open_w * (vw_val - north_vel)
        + open_n * (vn_val - north_vel)
        + open_s * (vs_val - north_vel)
    )
    results.append(east_vel + TIME_STEP * (coriolis * north_vel - grad_x + VISCOSITY * lap_u))
    results.append(north_vel + TIME_STEP * (-coriolis * east_vel - grad_y + VISCOSITY * lap_v))
    return jnp.stack(results)


def block_tables(block_counts, land_mask, device, slot_id):
    grid_rows, grid_cols = land_mask.shape
    flat_land = land_mask.reshape(-1)
    sea_flag = 1 - flat_land
    ordering = jnp.argsort(flat_land, stable=True)
    position = jnp.cumsum(sea_flag) - sea_flag
    run_ends = jnp.cumsum(block_counts)
    run_starts = run_ends - block_counts
    list_pos = run_starts[device] + slot_id
    is_live = slot_id < block_counts[device]
    block_in_grid = ordering[jnp.clip(list_pos, 0, grid_rows * grid_cols - 1)]
    block_row = block_in_grid // grid_cols
    block_col = block_in_grid % grid_cols
    at_top = block_row == grid_rows - 1
    mirror_col = grid_cols - 1 - block_col
    nb_row = jnp.stack(
        [block_row - 1, jnp.where(at_top, block_row, block_row + 1), block_row, block_row], axis=-1
    )
    nb_col = jnp.stack(
        [
            block_col,
            jnp.where(at_top, mirror_col, block_col),
            (block_col + grid_cols - 1) % grid_cols,
            (block_col + 1) % grid_cols,
        ],
        axis=-1,
    )
    exists = jnp.stack([block_row > 0, at_top | True, at_top | True, at_top | True], axis=-1)
    nb_grid = jnp.clip(nb_row, 0, grid_rows - 1) * grid_cols + nb_col
    is_wet = exists & (sea_flag[nb_grid] == 1)
    nb_pos = position[nb_grid]
    nb_owner = jnp.clip(
        jnp.searchsorted(run_ends, nb_pos, side="right"), 0, block_counts.shape[0] - 1
    )
    nb_slot = nb_pos - run_starts[nb_owner]
    edge_id = jnp.stack(
        [
            jnp.ones_like(block_row),
            jnp.where(at_top, 1, 0).astype(jnp.int32),
            jnp.full_like(block_row, 3),
            jnp.full_like(block_row, 2),
        ],
        axis=-1,
    )
    is_fold = jnp.stack([at_top & False, at_top, at_top & False, at_top & False], axis=-1)
    return (is_live, block_row, nb_owner, nb_slot, edge_id, is_fold, is_wet)


def edge_rims(ocean_fields):
    return jnp.stack(
        [
            ocean_fields[:, :, :, 0, :],
            ocean_fields[:, :, :, -1, :],
            ocean_fields[:, :, :, :, 0],
            ocean_fields[:, :, :, :, -1],
        ],
        axis=1,
    )


def per_device(tracers, velocity, block_counts, land_mask):
    slots = tracers.shape[0]
    width = tracers.shape[-1]
    reach = min(land_mask.shape[1], lax.axis_size("blk") - 1)
    myself = lax.axis_index("blk")
    slot_id = jnp.arange(slots, dtype=jnp.int32)
    device = jnp.full((slots,), myself, dtype=jnp.int32)
    is_live, block_row, nb_owner, nb_slot, edge_id, is_fold, is_wet = block_tables(
        block_counts, land_mask, device, slot_id
    )
    neighbour_distance = jnp.clip(nb_owner - myself, -reach, reach)
    take_at = (
        ((neighbour_distance + reach) * slots + jnp.clip(nb_slot, 0, slots - 1)) * 4 + edge_id
    ).reshape(-1)
    opens = is_wet.astype(jnp.float32)
    first_row = (block_row * width).astype(jnp.float32)
    rows_total = float(land_mask.shape[0] * width)
    signs = jnp.array([1.0, 1.0, -1.0, -1.0], dtype=jnp.float32)[:, None, None]
    ocean_fields = jnp.concatenate([tracers, velocity], axis=1)
    for step in range(SUBSTEPS):
        rims = edge_rims(ocean_fields)
        pieces = []
        for window_pos in range(2 * reach + 1):
            offset = window_pos - reach
            pieces.append(rims if offset == 0 else from_behind(rims, "blk", -offset))
        window = jnp.stack(pieces)
        flat = window.reshape((window.shape[0] * slots * 4,) + rims.shape[2:])
        halos = flat[take_at].reshape((slots, 4) + rims.shape[2:])
        flipped = halos[..., ::-1] * signs
        halos = jnp.where(is_fold[:, :, None, None, None], flipped, halos)
        updated = jax.vmap(advance_substep, in_axes=(0, 0, 0, 0, None))(
            ocean_fields, halos, opens, first_row, rows_total
        )
        ocean_fields = jnp.where(
            is_live[:, None, None, None, None], updated, jnp.zeros_like(updated)
        )
    return (ocean_fields[:, :2], ocean_fields[:, 2:])


def solution(mesh):
    placed = (P("blk", None, None, None, None), P("blk", None, None, None, None), P(), P())
    return jax.shard_map(
        per_device,
        mesh=mesh,
        in_specs=placed,
        out_specs=(P("blk", None, None, None, None), P("blk", None, None, None, None)),
        check_vma=False,
    )
```

profile of v0, /device:TPU:3, one launch (start us, length us, event | category | flops | bytes accessed | tf_op | source)
XLA Modules:
  0.0 1250.4 jit_solution(8976966182868602691)
XLA Ops:
  130.7 13.1 %collective-permute-start.19 = (f32[4,4,4,2,128]{4,3,2,0,1:T(2,128)S(1)}, f32[4,4,4,2,128]{4,3,2,0,1:T(2,128)S(1)}, u32[]{:S(2)}, u32[]{:S(2)}) collective-permute-start(f32[4,4,4,2,128]{4,3,2,0,1:T(2,128)S(1)} %pad_maximum_fusion.24), channel_id=1, source_target_pairs={{0,15},{1,16},{2,17},{3,18},{4,19},{5,20},{6,21},{7,22},{8,23},{9,... | collective-permute-start | bytes 196616 | tf_op jit(solution)/shard_map/ppermute | solution.py:20
  143.9 13.1 %collective-permute-start.20 = (f32[4,4,4,2,128]{4,3,2,0,1:T(2,128)S(1)}, f32[4,4,4,2,128]{4,3,2,0,1:T(2,128)S(1)}, u32[]{:S(2)}, u32[]{:S(2)}) collective-permute-start(f32[4,4,4,2,128]{4,3,2,0,1:T(2,128)S(1)} %pad_maximum_fusion.24), channel_id=1, source_target_pairs={{0,14},{1,15},{2,16},{3,17},{4,18},{5,19},{6,20},{7,21},{8,22},{9,... | collective-permute-start | bytes 196616 | tf_op jit(solution)/shard_map/ppermute | solution.py:20
  157.0 13.1 %collective-permute-start.21 = (f32[4,4,4,2,128]{4,3,2,0,1:T(2,128)S(1)}, f32[4,4,4,2,128]{4,3,2,0,1:T(2,128)S(1)}, u32[]{:S(2)}, u32[]{:S(2)}) collective-permute-start(f32[4,4,4,2,128]{4,3,2,0,1:T(2,128)S(1)} %pad_maximum_fusion.24), channel_id=1, source_target_pairs={{0,13},{1,14},{2,15},{3,16},{4,17},{5,18},{6,19},{7,20},{8,21},{9,... | collective-permute-start | bytes 196616 | tf_op jit(solution)/shard_map/ppermute | solution.py:20
  170.2 13.1 %collective-permute-start.22 = (f32[4,4,4,2,128]{4,3,2,0,1:T(2,128)S(1)}, f32[4,4,4,2,128]{4,3,2,0,1:T(2,128)S(1)}, u32[]{:S(2)}, u32[]{:S(2)}) collective-permute-start(f32[4,4,4,2,128]{4,3,2,0,1:T(2,128)S(1)} %pad_maximum_fusion.24), channel_id=1, source_target_pairs={{0,12},{1,13},{2,14},{3,15},{4,16},{5,17},{6,18},{7,19},{8,20},{9,... | collective-permute-start | bytes 196616 | tf_op jit(solution)/shard_map/ppermute | solution.py:20
  183.4 13.1 %collective-permute-start.23 = (f32[4,4,4,2,128]{4,3,2,0,1:T(2,128)S(1)}, f32[4,4,4,2,128]{4,3,2,0,1:T(2,128)S(1)}, u32[]{:S(2)}, u32[]{:S(2)}) collective-permute-start(f32[4,4,4,2,128]{4,3,2,0,1:T(2,128)S(1)} %pad_maximum_fusion.24), channel_id=1, source_target_pairs={{0,11},{1,12},{2,13},{3,14},{4,15},{5,16},{6,17},{7,18},{8,19},{9,... | collective-permute-start | bytes 196616 | tf_op jit(solution)/shard_map/ppermute | solution.py:20
  196.5 13.1 %collective-permute-start.24 = (f32[4,4,4,2,128]{4,3,2,0,1:T(2,128)S(1)}, f32[4,4,4,2,128]{4,3,2,0,1:T(2,128)S(1)}, u32[]{:S(2)}, u32[]{:S(2)}) collective-permute-start(f32[4,4,4,2,128]{4,3,2,0,1:T(2,128)S(1)} %pad_maximum_fusion.24), channel_id=1, source_target_pairs={{0,10},{1,11},{2,12},{3,13},{4,14},{5,15},{6,16},{7,17},{8,18},{9,... | collective-permute-start | bytes 196616 | tf_op jit(solution)/shard_map/ppermute | solution.py:20
  209.7 13.1 %collective-permute-start.25 = (f32[4,4,4,2,128]{4,3,2,0,1:T(2,128)S(1)}, f32[4,4,4,2,128]{4,3,2,0,1:T(2,128)S(1)}, u32[]{:S(2)}, u32[]{:S(2)}) collective-permute-start(f32[4,4,4,2,128]{4,3,2,0,1:T(2,128)S(1)} %pad_maximum_fusion.24), channel_id=1, source_target_pairs={{0,9},{1,10},{2,11},{3,12},{4,13},{5,14},{6,15},{7,16},{8,17},{9,1... | collective-permute-start | bytes 196616 | tf_op jit(solution)/shard_map/ppermute | solution.py:20
  222.8 13.1 %collective-permute-start.26 = (f32[4,4,4,2,128]{4,3,2,0,1:T(2,128)S(1)}, f32[4,4,4,2,128]{4,3,2,0,1:T(2,128)S(1)}, u32[]{:S(2)}, u32[]{:S(2)}) collective-permute-start(f32[4,4,4,2,128]{4,3,2,0,1:T(2,128)S(1)} %pad_maximum_fusion.24), channel_id=1, source_target_pairs={{0,8},{1,9},{2,10},{3,11},{4,12},{5,13},{6,14},{7,15},{8,16},{9,17... | collective-permute-start | bytes 196616 | tf_op jit(solution)/shard_map/ppermute | solution.py:20
  236.0 13.1 %collective-permute-start.27 = (f32[4,4,4,2,128]{4,3,2,0,1:T(2,128)S(1)}, f32[4,4,4,2,128]{4,3,2,0,1:T(2,128)S(1)}, u32[]{:S(2)}, u32[]{:S(2)}) collective-permute-start(f32[4,4,4,2,128]{4,3,2,0,1:T(2,128)S(1)} %pad_maximum_fusion.24), channel_id=1, source_target_pairs={{0,7},{1,8},{2,9},{3,10},{4,11},{5,12},{6,13},{7,14},{8,15},{9,16}... | collective-permute-start | bytes 196616 | tf_op jit(solution)/shard_map/ppermute | solution.py:20
  249.2 13.1 %collective-permute-start.28 = (f32[4,4,4,2,128]{4,3,2,0,1:T(2,128)S(1)}, f32[4,4,4,2,128]{4,3,2,0,1:T(2,128)S(1)}, u32[]{:S(2)}, u32[]{:S(2)}) collective-permute-start(f32[4,4,4,2,128]{4,3,2,0,1:T(2,128)S(1)} %pad_maximum_fusion.24), channel_id=1, source_target_pairs={{0,6},{1,7},{2,8},{3,9},{4,10},{5,11},{6,12},{7,13},{8,14},{9,15},... | collective-permute-start | bytes 196616 | tf_op jit(solution)/shard_map/ppermute | solution.py:20
  262.3 13.1 %collective-permute-start.29 = (f32[4,4,4,2,128]{4,3,2,0,1:T(2,128)S(1)}, f32[4,4,4,2,128]{4,3,2,0,1:T(2,128)S(1)}, u32[]{:S(2)}, u32[]{:S(2)}) collective-permute-start(f32[4,4,4,2,128]{4,3,2,0,1:T(2,128)S(1)} %pad_maximum_fusion.24), channel_id=1, source_target_pairs={{0,5},{1,6},{2,7},{3,8},{4,9},{5,10},{6,11},{7,12},{8,13},{9,14},{... | collective-permute-start | bytes 196616 | tf_op jit(solution)/shard_map/ppermute | solution.py:20
  288.6 13.1 %collective-permute-start.31 = (f32[4,4,4,2,128]{4,3,2,0,1:T(2,128)S(1)}, f32[4,4,4,2,128]{4,3,2,0,1:T(2,128)S(1)}, u32[]{:S(2)}, u32[]{:S(2)}) collective-permute-start(f32[4,4,4,2,128]{4,3,2,0,1:T(2,128)S(1)} %pad_maximum_fusion.24), channel_id=1, source_target_pairs={{0,3},{1,4},{2,5},{3,6},{4,7},{5,8},{6,9},{7,10},{8,11},{9,12},{10... | collective-permute-start | bytes 196616 | tf_op jit(solution)/shard_map/ppermute | solution.py:20
  301.8 13.1 %collective-permute-start.32 = (f32[4,4,4,2,128]{4,3,2,0,1:T(2,128)S(1)}, f32[4,4,4,2,128]{4,3,2,0,1:T(2,128)S(1)}, u32[]{:S(2)}, u32[]{:S(2)}) collective-permute-start(f32[4,4,4,2,128]{4,3,2,0,1:T(2,128)S(1)} %pad_maximum_fusion.24), channel_id=1, source_target_pairs={{0,2},{1,3},{2,4},{3,5},{4,6},{5,7},{6,8},{7,9},{8,10},{9,11},{10,... | collective-permute-start | bytes 196616 | tf_op jit(solution)/shard_map/ppermute | solution.py:20
  315.0 13.1 %collective-permute-start.33 = (f32[4,4,4,2,128]{4,3,2,0,1:T(2,128)S(1)}, f32[4,4,4,2,128]{4,3,2,0,1:T(2,128)S(1)}, u32[]{:S(2)}, u32[]{:S(2)}) collective-permute-start(f32[4,4,4,2,128]{4,3,2,0,1:T(2,128)S(1)} %pad_maximum_fusion.24), channel_id=1, source_target_pairs={{0,1},{1,2},{2,3},{3,4},{4,5},{5,6},{6,7},{7,8},{8,9},{9,10},{10,1... | collective-permute-start | bytes 196616 | tf_op jit(solution)/shard_map/ppermute | solution.py:20
  328.1 13.1 %collective-permute-start.34 = (f32[4,4,4,2,128]{4,3,2,0,1:T(2,128)S(1)}, f32[4,4,4,2,128]{4,3,2,0,1:T(2,128)S(1)}, u32[]{:S(2)}, u32[]{:S(2)}) collective-permute-start(f32[4,4,4,2,128]{4,3,2,0,1:T(2,128)S(1)} %pad_maximum_fusion.24), channel_id=1, source_target_pairs={{1,0},{2,1},{3,2},{4,3},{5,4},{6,5},{7,6},{8,7},{9,8},{10,9},{11,1... | collective-permute-start | bytes 196616 | tf_op jit(solution)/shard_map/ppermute | solution.py:20
  341.3 13.1 %collective-permute-start.35 = (f32[4,4,4,2,128]{4,3,2,0,1:T(2,128)S(1)}, f32[4,4,4,2,128]{4,3,2,0,1:T(2,128)S(1)}, u32[]{:S(2)}, u32[]{:S(2)}) collective-permute-start(f32[4,4,4,2,128]{4,3,2,0,1:T(2,128)S(1)} %pad_maximum_fusion.24), channel_id=1, source_target_pairs={{2,0},{3,1},{4,2},{5,3},{6,4},{7,5},{8,6},{9,7},{10,8},{11,9},{12,... | collective-permute-start | bytes 196616 | tf_op jit(solution)/shard_map/ppermute | solution.py:20
  354.4 13.1 %collective-permute-start.36 = (f32[4,4,4,2,128]{4,3,2,0,1:T(2,128)S(1)}, f32[4,4,4,2,128]{4,3,2,0,1:T(2,128)S(1)}, u32[]{:S(2)}, u32[]{:S(2)}) collective-permute-start(f32[4,4,4,2,128]{4,3,2,0,1:T(2,128)S(1)} %pad_maximum_fusion.24), channel_id=1, source_target_pairs={{3,0},{4,1},{5,2},{6,3},{7,4},{8,5},{9,6},{10,7},{11,8},{12,9},{13... | collective-permute-start | bytes 196616 | tf_op jit(solution)/shard_map/ppermute | solution.py:20
  367.6 13.1 %collective-permute-start.37 = (f32[4,4,4,2,128]{4,3,2,0,1:T(2,128)S(1)}, f32[4,4,4,2,128]{4,3,2,0,1:T(2,128)S(1)}, u32[]{:S(2)}, u32[]{:S(2)}) collective-permute-start(f32[4,4,4,2,128]{4,3,2,0,1:T(2,128)S(1)} %pad_maximum_fusion.24), channel_id=1, source_target_pairs={{4,0},{5,1},{6,2},{7,3},{8,4},{9,5},{10,6},{11,7},{12,8},{13,9},{1... | collective-permute-start | bytes 196616 | tf_op jit(solution)/shard_map/ppermute | solution.py:20
  380.8 13.1 %collective-permute-start.38 = (f32[4,4,4,2,128]{4,3,2,0,1:T(2,128)S(1)}, f32[4,4,4,2,128]{4,3,2,0,1:T(2,128)S(1)}, u32[]{:S(2)}, u32[]{:S(2)}) collective-permute-start(f32[4,4,4,2,128]{4,3,2,0,1:T(2,128)S(1)} %pad_maximum_fusion.24), channel_id=1, source_target_pairs={{5,0},{6,1},{7,2},{8,3},{9,4},{10,5},{11,6},{12,7},{13,8},{14,9},{... | collective-permute-start | bytes 196616 | tf_op jit(solution)/shard_map/ppermute | solution.py:20
  394.0 13.1 %collective-permute-start.39 = (f32[4,4,4,2,128]{4,3,2,0,1:T(2,128)S(1)}, f32[4,4,4,2,128]{4,3,2,0,1:T(2,128)S(1)}, u32[]{:S(2)}, u32[]{:S(2)}) collective-permute-start(f32[4,4,4,2,128]{4,3,2,0,1:T(2,128)S(1)} %pad_maximum_fusion.24), channel_id=1, source_target_pairs={{6,0},{7,1},{8,2},{9,3},{10,4},{11,5},{12,6},{13,7},{14,8},{15,9},... | collective-permute-start | bytes 196616 | tf_op jit(solution)/shard_map/ppermute | solution.py:20
  420.3 13.1 %collective-permute-start.41 = (f32[4,4,4,2,128]{4,3,2,0,1:T(2,128)S(1)}, f32[4,4,4,2,128]{4,3,2,0,1:T(2,128)S(1)}, u32[]{:S(2)}, u32[]{:S(2)}) collective-permute-start(f32[4,4,4,2,128]{4,3,2,0,1:T(2,128)S(1)} %pad_maximum_fusion.24), channel_id=1, source_target_pairs={{8,0},{9,1},{10,2},{11,3},{12,4},{13,5},{14,6},{15,7},{16,8},{17,9... | collective-permute-start | bytes 196616 | tf_op jit(solution)/shard_map/ppermute | solution.py:20
  433.4 13.1 %collective-permute-start.42 = (f32[4,4,4,2,128]{4,3,2,0,1:T(2,128)S(1)}, f32[4,4,4,2,128]{4,3,2,0,1:T(2,128)S(1)}, u32[]{:S(2)}, u32[]{:S(2)}) collective-permute-start(f32[4,4,4,2,128]{4,3,2,0,1:T(2,128)S(1)} %pad_maximum_fusion.24), channel_id=1, source_target_pairs={{9,0},{10,1},{11,2},{12,3},{13,4},{14,5},{15,6},{16,7},{17,8},{18,... | collective-permute-start | bytes 196616 | tf_op jit(solution)/shard_map/ppermute | solution.py:20
  446.6 13.1 %collective-permute-start.43 = (f32[4,4,4,2,128]{4,3,2,0,1:T(2,128)S(1)}, f32[4,4,4,2,128]{4,3,2,0,1:T(2,128)S(1)}, u32[]{:S(2)}, u32[]{:S(2)}) collective-permute-start(f32[4,4,4,2,128]{4,3,2,0,1:T(2,128)S(1)} %pad_maximum_fusion.24), channel_id=1, source_target_pairs={{10,0},{11,1},{12,2},{13,3},{14,4},{15,5},{16,6},{17,7},{18,8},{19... | collective-permute-start | bytes 196616 | tf_op jit(solution)/shard_map/ppermute | solution.py:20
  459.8 13.1 %collective-permute-start.44 = (f32[4,4,4,2,128]{4,3,2,0,1:T(2,128)S(1)}, f32[4,4,4,2,128]{4,3,2,0,1:T(2,128)S(1)}, u32[]{:S(2)}, u32[]{:S(2)}) collective-permute-start(f32[4,4,4,2,128]{4,3,2,0,1:T(2,128)S(1)} %pad_maximum_fusion.24), channel_id=1, source_target_pairs={{11,0},{12,1},{13,2},{14,3},{15,4},{16,5},{17,6},{18,7},{19,8},{20... | collective-permute-start | bytes 196616 | tf_op jit(solution)/shard_map/ppermute | solution.py:20
  (758 shorter events, 938.7 us)
Async XLA Ops:
  130.7 65.8 %collective-permute-start.19 = (f32[4,4,4,2,128]{4,3,2,0,1:T(2,128)S(1)}, f32[4,4,4,2,128]{4,3,2,0,1:T(2,128)S(1)}, u32[]{:S(2)}, u32[]{:S(2)}) collective-permute-start(f32[4,4,4,2,128]{4,3,2,0,1:T(2,128)S(1)} %pad_maximum_fusion.24), channel_id=1, source_target_pairs={{0,15},{1,16},{2,17},{3,18},{4,19},{5,20},{6,21},{7,22},{8,23},{9,... | collective-permute-start | bytes 196616 | tf_op jit(solution)/shard_map/ppermute | solution.py:20
  157.0 65.8 %collective-permute-start.21 = (f32[4,4,4,2,128]{4,3,2,0,1:T(2,128)S(1)}, f32[4,4,4,2,128]{4,3,2,0,1:T(2,128)S(1)}, u32[]{:S(2)}, u32[]{:S(2)}) collective-permute-start(f32[4,4,4,2,128]{4,3,2,0,1:T(2,128)S(1)} %pad_maximum_fusion.24), channel_id=1, source_target_pairs={{0,13},{1,14},{2,15},{3,16},{4,17},{5,18},{6,19},{7,20},{8,21},{9,... | collective-permute-start | bytes 196616 | tf_op jit(solution)/shard_map/ppermute | solution.py:20
  170.2 65.8 %collective-permute-start.22 = (f32[4,4,4,2,128]{4,3,2,0,1:T(2,128)S(1)}, f32[4,4,4,2,128]{4,3,2,0,1:T(2,128)S(1)}, u32[]{:S(2)}, u32[]{:S(2)}) collective-permute-start(f32[4,4,4,2,128]{4,3,2,0,1:T(2,128)S(1)} %pad_maximum_fusion.24), channel_id=1, source_target_pairs={{0,12},{1,13},{2,14},{3,15},{4,16},{5,17},{6,18},{7,19},{8,20},{9,... | collective-permute-start | bytes 196616 | tf_op jit(solution)/shard_map/ppermute | solution.py:20
  196.5 65.8 %collective-permute-start.24 = (f32[4,4,4,2,128]{4,3,2,0,1:T(2,128)S(1)}, f32[4,4,4,2,128]{4,3,2,0,1:T(2,128)S(1)}, u32[]{:S(2)}, u32[]{:S(2)}) collective-permute-start(f32[4,4,4,2,128]{4,3,2,0,1:T(2,128)S(1)} %pad_maximum_fusion.24), channel_id=1, source_target_pairs={{0,10},{1,11},{2,12},{3,13},{4,14},{5,15},{6,16},{7,17},{8,18},{9,... | collective-permute-start | bytes 196616 | tf_op jit(solution)/shard_map/ppermute | solution.py:20
  209.7 65.8 %collective-permute-start.25 = (f32[4,4,4,2,128]{4,3,2,0,1:T(2,128)S(1)}, f32[4,4,4,2,128]{4,3,2,0,1:T(2,128)S(1)}, u32[]{:S(2)}, u32[]{:S(2)}) collective-permute-start(f32[4,4,4,2,128]{4,3,2,0,1:T(2,128)S(1)} %pad_maximum_fusion.24), channel_id=1, source_target_pairs={{0,9},{1,10},{2,11},{3,12},{4,13},{5,14},{6,15},{7,16},{8,17},{9,1... | collective-permute-start | bytes 196616 | tf_op jit(solution)/shard_map/ppermute | solution.py:20
  236.0 65.8 %collective-permute-start.27 = (f32[4,4,4,2,128]{4,3,2,0,1:T(2,128)S(1)}, f32[4,4,4,2,128]{4,3,2,0,1:T(2,128)S(1)}, u32[]{:S(2)}, u32[]{:S(2)}) collective-permute-start(f32[4,4,4,2,128]{4,3,2,0,1:T(2,128)S(1)} %pad_maximum_fusion.24), channel_id=1, source_target_pairs={{0,7},{1,8},{2,9},{3,10},{4,11},{5,12},{6,13},{7,14},{8,15},{9,16}... | collective-permute-start | bytes 196616 | tf_op jit(solution)/shard_map/ppermute | solution.py:20
  249.2 65.8 %collective-permute-start.28 = (f32[4,4,4,2,128]{4,3,2,0,1:T(2,128)S(1)}, f32[4,4,4,2,128]{4,3,2,0,1:T(2,128)S(1)}, u32[]{:S(2)}, u32[]{:S(2)}) collective-permute-start(f32[4,4,4,2,128]{4,3,2,0,1:T(2,128)S(1)} %pad_maximum_fusion.24), channel_id=1, source_target_pairs={{0,6},{1,7},{2,8},{3,9},{4,10},{5,11},{6,12},{7,13},{8,14},{9,15},... | collective-permute-start | bytes 196616 | tf_op jit(solution)/shard_map/ppermute | solution.py:20
  262.3 65.8 %collective-permute-start.29 = (f32[4,4,4,2,128]{4,3,2,0,1:T(2,128)S(1)}, f32[4,4,4,2,128]{4,3,2,0,1:T(2,128)S(1)}, u32[]{:S(2)}, u32[]{:S(2)}) collective-permute-start(f32[4,4,4,2,128]{4,3,2,0,1:T(2,128)S(1)} %pad_maximum_fusion.24), channel_id=1, source_target_pairs={{0,5},{1,6},{2,7},{3,8},{4,9},{5,10},{6,11},{7,12},{8,13},{9,14},{... | collective-permute-start | bytes 196616 | tf_op jit(solution)/shard_map/ppermute | solution.py:20
  288.6 65.8 %collective-permute-start.31 = (f32[4,4,4,2,128]{4,3,2,0,1:T(2,128)S(1)}, f32[4,4,4,2,128]{4,3,2,0,1:T(2,128)S(1)}, u32[]{:S(2)}, u32[]{:S(2)}) collective-permute-start(f32[4,4,4,2,128]{4,3,2,0,1:T(2,128)S(1)} %pad_maximum_fusion.24), channel_id=1, source_target_pairs={{0,3},{1,4},{2,5},{3,6},{4,7},{5,8},{6,9},{7,10},{8,11},{9,12},{10... | collective-permute-start | bytes 196616 | tf_op jit(solution)/shard_map/ppermute | solution.py:20
  301.8 65.8 %collective-permute-start.32 = (f32[4,4,4,2,128]{4,3,2,0,1:T(2,128)S(1)}, f32[4,4,4,2,128]{4,3,2,0,1:T(2,128)S(1)}, u32[]{:S(2)}, u32[]{:S(2)}) collective-permute-start(f32[4,4,4,2,128]{4,3,2,0,1:T(2,128)S(1)} %pad_maximum_fusion.24), channel_id=1, source_target_pairs={{0,2},{1,3},{2,4},{3,5},{4,6},{5,7},{6,8},{7,9},{8,10},{9,11},{10,... | collective-permute-start | bytes 196616 | tf_op jit(solution)/shard_map/ppermute | solution.py:20
  328.1 65.8 %collective-permute-start.34 = (f32[4,4,4,2,128]{4,3,2,0,1:T(2,128)S(1)}, f32[4,4,4,2,128]{4,3,2,0,1:T(2,128)S(1)}, u32[]{:S(2)}, u32[]{:S(2)}) collective-permute-start(f32[4,4,4,2,128]{4,3,2,0,1:T(2,128)S(1)} %pad_maximum_fusion.24), channel_id=1, source_target_pairs={{1,0},{2,1},{3,2},{4,3},{5,4},{6,5},{7,6},{8,7},{9,8},{10,9},{11,1... | collective-permute-start | bytes 196616 | tf_op jit(solution)/shard_map/ppermute | solution.py:20
  341.3 65.8 %collective-permute-start.35 = (f32[4,4,4,2,128]{4,3,2,0,1:T(2,128)S(1)}, f32[4,4,4,2,128]{4,3,2,0,1:T(2,128)S(1)}, u32[]{:S(2)}, u32[]{:S(2)}) collective-permute-start(f32[4,4,4,2,128]{4,3,2,0,1:T(2,128)S(1)} %pad_maximum_fusion.24), channel_id=1, source_target_pairs={{2,0},{3,1},{4,2},{5,3},{6,4},{7,5},{8,6},{9,7},{10,8},{11,9},{12,... | collective-permute-start | bytes 196616 | tf_op jit(solution)/shard_map/ppermute | solution.py:20
  354.4 65.8 %collective-permute-start.36 = (f32[4,4,4,2,128]{4,3,2,0,1:T(2,128)S(1)}, f32[4,4,4,2,128]{4,3,2,0,1:T(2,128)S(1)}, u32[]{:S(2)}, u32[]{:S(2)}) collective-permute-start(f32[4,4,4,2,128]{4,3,2,0,1:T(2,128)S(1)} %pad_maximum_fusion.24), channel_id=1, source_target_pairs={{3,0},{4,1},{5,2},{6,3},{7,4},{8,5},{9,6},{10,7},{11,8},{12,9},{13... | collective-permute-start | bytes 196616 | tf_op jit(solution)/shard_map/ppermute | solution.py:20
  367.6 65.8 %collective-permute-start.37 = (f32[4,4,4,2,128]{4,3,2,0,1:T(2,128)S(1)}, f32[4,4,4,2,128]{4,3,2,0,1:T(2,128)S(1)}, u32[]{:S(2)}, u32[]{:S(2)}) collective-permute-start(f32[4,4,4,2,128]{4,3,2,0,1:T(2,128)S(1)} %pad_maximum_fusion.24), channel_id=1, source_target_pairs={{4,0},{5,1},{6,2},{7,3},{8,4},{9,5},{10,6},{11,7},{12,8},{13,9},{1... | collective-permute-start | bytes 196616 | tf_op jit(solution)/shard_map/ppermute | solution.py:20
  380.8 65.8 %collective-permute-start.38 = (f32[4,4,4,2,128]{4,3,2,0,1:T(2,128)S(1)}, f32[4,4,4,2,128]{4,3,2,0,1:T(2,128)S(1)}, u32[]{:S(2)}, u32[]{:S(2)}) collective-permute-start(f32[4,4,4,2,128]{4,3,2,0,1:T(2,128)S(1)} %pad_maximum_fusion.24), channel_id=1, source_target_pairs={{5,0},{6,1},{7,2},{8,3},{9,4},{10,5},{11,6},{12,7},{13,8},{14,9},{... | collective-permute-start | bytes 196616 | tf_op jit(solution)/shard_map/ppermute | solution.py:20
  394.0 65.8 %collective-permute-start.39 = (f32[4,4,4,2,128]{4,3,2,0,1:T(2,128)S(1)}, f32[4,4,4,2,128]{4,3,2,0,1:T(2,128)S(1)}, u32[]{:S(2)}, u32[]{:S(2)}) collective-permute-start(f32[4,4,4,2,128]{4,3,2,0,1:T(2,128)S(1)} %pad_maximum_fusion.24), channel_id=1, source_target_pairs={{6,0},{7,1},{8,2},{9,3},{10,4},{11,5},{12,6},{13,7},{14,8},{15,9},... | collective-permute-start | bytes 196616 | tf_op jit(solution)/shard_map/ppermute | solution.py:20
  420.3 65.8 %collective-permute-start.41 = (f32[4,4,4,2,128]{4,3,2,0,1:T(2,128)S(1)}, f32[4,4,4,2,128]{4,3,2,0,1:T(2,128)S(1)}, u32[]{:S(2)}, u32[]{:S(2)}) collective-permute-start(f32[4,4,4,2,128]{4,3,2,0,1:T(2,128)S(1)} %pad_maximum_fusion.24), channel_id=1, source_target_pairs={{8,0},{9,1},{10,2},{11,3},{12,4},{13,5},{14,6},{15,7},{16,8},{17,9... | collective-permute-start | bytes 196616 | tf_op jit(solution)/shard_map/ppermute | solution.py:20
  433.4 65.8 %collective-permute-start.42 = (f32[4,4,4,2,128]{4,3,2,0,1:T(2,128)S(1)}, f32[4,4,4,2,128]{4,3,2,0,1:T(2,128)S(1)}, u32[]{:S(2)}, u32[]{:S(2)}) collective-permute-start(f32[4,4,4,2,128]{4,3,2,0,1:T(2,128)S(1)} %pad_maximum_fusion.24), channel_id=1, source_target_pairs={{9,0},{10,1},{11,2},{12,3},{13,4},{14,5},{15,6},{16,7},{17,8},{18,... | collective-permute-start | bytes 196616 | tf_op jit(solution)/shard_map/ppermute | solution.py:20
  459.8 65.8 %collective-permute-start.44 = (f32[4,4,4,2,128]{4,3,2,0,1:T(2,128)S(1)}, f32[4,4,4,2,128]{4,3,2,0,1:T(2,128)S(1)}, u32[]{:S(2)}, u32[]{:S(2)}) collective-permute-start(f32[4,4,4,2,128]{4,3,2,0,1:T(2,128)S(1)} %pad_maximum_fusion.24), channel_id=1, source_target_pairs={{11,0},{12,1},{13,2},{14,3},{15,4},{16,5},{17,6},{18,7},{19,8},{20... | collective-permute-start | bytes 196616 | tf_op jit(solution)/shard_map/ppermute | solution.py:20
  939.7 65.8 %collective-permute-start.102 = (f32[4,4,4,2,128]{4,3,2,0,1:T(2,128)S(1)}, f32[4,4,4,2,128]{4,3,2,0,1:T(2,128)S(1)}, u32[]{:S(2)}, u32[]{:S(2)}) collective-permute-start(f32[4,4,4,2,128]{4,3,2,0,1:T(2,128)S(1)} %pad_maximum_fusion.25), channel_id=1, source_target_pairs={{1,0},{2,1},{3,2},{4,3},{5,4},{6,5},{7,6},{8,7},{9,8},{10,9},{11,1... | collective-permute-start | bytes 196616 | tf_op jit(solution)/shard_map/ppermute | solution.py:20
  952.9 65.8 %collective-permute-start.103 = (f32[4,4,4,2,128]{4,3,2,0,1:T(2,128)S(1)}, f32[4,4,4,2,128]{4,3,2,0,1:T(2,128)S(1)}, u32[]{:S(2)}, u32[]{:S(2)}) collective-permute-start(f32[4,4,4,2,128]{4,3,2,0,1:T(2,128)S(1)} %pad_maximum_fusion.25), channel_id=1, source_target_pairs={{2,0},{3,1},{4,2},{5,3},{6,4},{7,5},{8,6},{9,7},{10,8},{11,9},{12,... | collective-permute-start | bytes 196616 | tf_op jit(solution)/shard_map/ppermute | solution.py:20
  966.0 65.8 %collective-permute-start.104 = (f32[4,4,4,2,128]{4,3,2,0,1:T(2,128)S(1)}, f32[4,4,4,2,128]{4,3,2,0,1:T(2,128)S(1)}, u32[]{:S(2)}, u32[]{:S(2)}) collective-permute-start(f32[4,4,4,2,128]{4,3,2,0,1:T(2,128)S(1)} %pad_maximum_fusion.25), channel_id=1, source_target_pairs={{3,0},{4,1},{5,2},{6,3},{7,4},{8,5},{9,6},{10,7},{11,8},{12,9},{13... | collective-permute-start | bytes 196616 | tf_op jit(solution)/shard_map/ppermute | solution.py:20
  979.2 65.8 %collective-permute-start.105 = (f32[4,4,4,2,128]{4,3,2,0,1:T(2,128)S(1)}, f32[4,4,4,2,128]{4,3,2,0,1:T(2,128)S(1)}, u32[]{:S(2)}, u32[]{:S(2)}) collective-permute-start(f32[4,4,4,2,128]{4,3,2,0,1:T(2,128)S(1)} %pad_maximum_fusion.25), channel_id=1, source_target_pairs={{4,0},{5,1},{6,2},{7,3},{8,4},{9,5},{10,6},{11,7},{12,8},{13,9},{1... | collective-permute-start | bytes 196616 | tf_op jit(solution)/shard_map/ppermute | solution.py:20
  992.3 65.8 %collective-permute-start.106 = (f32[4,4,4,2,128]{4,3,2,0,1:T(2,128)S(1)}, f32[4,4,4,2,128]{4,3,2,0,1:T(2,128)S(1)}, u32[]{:S(2)}, u32[]{:S(2)}) collective-permute-start(f32[4,4,4,2,128]{4,3,2,0,1:T(2,128)S(1)} %pad_maximum_fusion.25), channel_id=1, source_target_pairs={{5,0},{6,1},{7,2},{8,3},{9,4},{10,5},{11,6},{12,7},{13,8},{14,9},{... | collective-permute-start | bytes 196616 | tf_op jit(solution)/shard_map/ppermute | solution.py:20
  (176 other events, 4944.4 us)
where the time goes:
time: 1270 us; the launch traced here: 1250 us
  starting transfers between devices  1090 us (86%)
  local copies, waits for them, and re-layouts  108 us (9%)
  other arithmetic  32 us (3%)
  waiting for transfers between devices  16.2 us (1%)
    ppermute x136, starting transfers between devices, from_behind(): return lax.ppermute(block, axis, route)  1090 us
  transfers between devices with their start and end apart: 136, of which 9 were waited for; matrix products, arithmetic and copies ran while one was open for 4% of the time, Pallas kernels for 0%

commit v1 on v0

v1 whole, which is shorter than its diff:
```python
import jax
import jax.numpy as jnp
from jax import lax
from jax.experimental import pallas as pl
from jax.experimental.pallas import tpu as pltpu
from jax.sharding import PartitionSpec as P

DEVICES = 256
ROWS, COLS = 26, 34
WIDTH = 128
CAP = 8
MORE = 10
EDGE = 16
MSG_EDGES = 18
MSG = MSG_EDGES * EDGE + 8
CHUNK = CAP * EDGE + 16
SWAP = 16 * EDGE + 8
F32 = jnp.float32
I32 = jnp.int32


def params(mib):
    return pltpu.CompilerParams(vmem_limit_bytes=mib * 1024 * 1024)


VM = pl.BlockSpec(memory_space=pltpu.VMEM)
SM = pl.BlockSpec(memory_space=pltpu.SMEM)
HB = pl.BlockSpec(memory_space=pl.ANY)


def grid_ids(block_counts, land):
    sea = 1 - land.reshape(-1).astype(I32)
    cells = jnp.arange(ROWS * COLS, dtype=I32)
    pos = jnp.sum(jnp.where(cells[None, :] < cells[:, None], sea[None, :], 0), axis=1)
    devs = jnp.arange(DEVICES, dtype=I32)
    ends = jnp.sum(jnp.where(devs[None, :] <= devs[:, None], block_counts[None, :], 0), axis=1)
    past = ends[None, :] <= pos[:, None]
    owner = jnp.sum(past.astype(I32), axis=1)
    start = jnp.max(jnp.where(past, ends[None, :], 0), axis=1)
    ids = jnp.where(sea == 1, owner * 4 + pos - start, -1)
    return ids.reshape(ROWS, COLS)


def neighbour_ids(ids):
    none = jnp.full((1, COLS), -1, I32)
    south = jnp.concatenate([none, ids[:-1]], axis=0)
    north = jnp.concatenate([ids[1:], ids[-1:, ::-1]], axis=0)

    def west(x):
        return jnp.concatenate([x[:, -1:], x[:, :-1]], axis=1)

    def east(x):
        return jnp.concatenate([x[:, 1:], x[:, :1]], axis=1)

    sides = [south, north, west(ids), east(ids), west(south), east(south), west(north), east(north)]
    return jnp.stack([x.reshape(-1) for x in sides])


def exclusive_count(mask):
    n = mask.shape[-1]
    i = jnp.arange(n)
    return jnp.sum(mask[..., None, :] & (i[None, :] < i[:, None]), axis=-1).astype(I32)


def make_tables(block_counts, land, me):
    column, zed, core = me >> 4, (me >> 1) & 7, me & 1
    ids = grid_ids(block_counts, land)
    near = neighbour_ids(ids)
    flat = ids.reshape(-1)
    chip_d = flat >> 3
    chip_s = near[:4] >> 3
    away = (near[:4] >= 0) & (flat >= 0) & (chip_s != chip_d)
    kind = jnp.where(away, (chip_s & 7) + 8 * (chip_s > chip_d), -1)
    kinds = jnp.sum(kind[:, :, None] == jnp.arange(16), axis=0).astype(jnp.bfloat16)
    chips = (chip_d[None, :] == jnp.arange(DEVICES // 2)[:, None]).astype(jnp.bfloat16)
    loads = jnp.dot(chips, kinds, preferred_element_type=F32)
    overflow = jnp.max(loads) > CAP + 0.5

    want = column * 64 + jnp.arange(64, dtype=I32)
    hit = flat[None, :] == want[:, None]
    cell = jnp.arange(ROWS * COLS, dtype=I32)
    mine = jnp.sum(jnp.where(hit[:, None, :], near[None] + 1, 0), axis=-1) - 1
    place = jnp.sum(jnp.where(hit, cell[None, :] + 1, 0), axis=-1) - 1
    live = place >= 0
    row = place // COLS
    col = place % COLS
    top = live & (row == ROWS - 1)

    chip_s = mine >> 3
    t_s = mine & 7
    z_s = chip_s & 7
    delta = jnp.abs((chip_s >> 3) - column)
    chip_d = column * 8 + jnp.arange(64, dtype=I32)[:, None] // 8
    valid = mine >= 0
    down = core == 1
    flow = valid & jnp.where(down, chip_s > chip_d, chip_s < chip_d)
    fold = top[:, None] & jnp.array([False, True, False, False])
    up_edge = jnp.stack([t_s[:, 0], t_s[:, 1], jnp.full((64,), 8, I32), jnp.full((64,), 9, I32)], axis=1)
    down_edge = jnp.stack(
        [t_s[:, 0], t_s[:, 1] + jnp.where(top, 10, 0), jnp.full((64,), 9, I32), jnp.full((64,), 8, I32)], axis=1
    )
    edge = jnp.where(down, down_edge, up_edge)
    at = (delta[:, :4] * MSG + edge * EDGE).reshape(8, 32)
    send = (flow[:, :4] & (z_s[:, :4] == zed)).reshape(8, 32)
    rank = exclusive_count(send)
    ranks = jnp.arange(CAP + MORE)
    picks = jnp.sum(jnp.where(send[:, None, :] & (rank[:, None, :] == ranks[None, :, None]), at[:, None, :], 0), axis=-1)

    def my_chip(x):
        x = lax.dynamic_slice_in_dim(x, zed * 8, 8, axis=0)
        return jnp.where(down, jnp.concatenate([x[4:], x[:4]]), x)

    got = my_chip(flow[:, :4]).reshape(32)
    got_z = my_chip(z_s[:, :4]).reshape(32)
    chip_flow = lax.dynamic_slice_in_dim(flow[:, :4], zed * 8, 8, axis=0).reshape(32)
    chip_z = lax.dynamic_slice_in_dim(z_s[:, :4], zed * 8, 8, axis=0).reshape(32)
    i32 = jnp.arange(32)
    before = chip_flow[None, :] & (chip_z[None, :] == chip_z[:, None]) & (i32[None, :] < i32[:, None])
    got_rank = jnp.sum(before, axis=1).astype(I32)
    got_rank = jnp.where(down, jnp.concatenate([got_rank[16:], got_rank[:16]]), got_rank)
    first = got & (got_rank < CAP)
    take = jnp.where(first, got_z * CHUNK + got_rank * EDGE, 0)

    same = chip_s == chip_d
    c_flow = my_chip((flow | (valid & same & (core == 0)))[:, 4:])
    hi = jnp.array([0, 1, 0, 1], I32)
    lane = jnp.where(
        (jnp.array([False, False, True, True])[None, :] & ~top[:, None]),
        16 + 2 * t_s[:, 4:] + hi,
        2 * t_s[:, 4:] + jnp.where(top[:, None] & jnp.array([False, False, True, True]), 1 - hi, hi),
    )
    lane = my_chip(lane + 32 * (delta[:, 4:] & 3))
    c_row = my_chip(z_s[:, 4:] * CHUNK + CAP * EDGE + 8 * (delta[:, 4:] >> 2))
    dst = (jnp.arange(8)[:, None] & 3) * 4 + jnp.arange(4)[None, :]
    c_take = jnp.where(c_flow, c_row, 0).reshape(32)
    c_turn = jnp.where(c_flow, (dst - lane) & 127, 0).reshape(32)
    c_dst = jnp.where(c_flow, dst, 999).reshape(32).astype(I32)

    def own(x):
        return my_chip(x)[:4]

    o_id, o_row, o_top, o_live = own(mine), own(row), own(top), own(live)
    o_chip, o_t = o_id[:, :4] >> 3, o_id[:, :4] & 7
    chip = me >> 1
    from_edge = jnp.stack([jnp.full((4,), 1, I32), jnp.where(o_top, 1, 0), jnp.full((4,), 3, I32), jnp.full((4,), 2, I32)], axis=1)
    here = (o_t * 4 + from_edge) * EDGE
    there = jnp.arange(16, dtype=I32).reshape(4, 4) * EDGE
    own_base, other_base = 8 * 4 * EDGE, 8 * 4 * EDGE + SWAP
    lower = o_chip < chip
    flown = there + jnp.where(lower == (core == 0), own_base, other_base)
    source = jnp.where(o_chip == chip, here, flown)
    source = jnp.where(o_id[:, :4] >= 0, source, 8 * 4 * EDGE + 2 * SWAP)

    c_live = lax.dynamic_slice_in_dim(live, zed * 8, 8, axis=0)
    c_col = lax.dynamic_slice_in_dim(col, zed * 8, 8, axis=0)
    t8 = jnp.arange(8, dtype=I32)
    last = jnp.max(jnp.where(c_live, t8, 0))
    zero_col = jnp.max(jnp.where(c_live & (c_col == 0), t8, 0))
    end_col = jnp.min(jnp.where(c_live & (c_col == COLS - 1), t8, 7))
    up = jnp.concatenate([t8 * 4 + 1, (last * 4 + 3)[None], (zero_col * 4 + 2)[None], t8 * 4 + 1])
    dn = jnp.concatenate([t8 * 4, jnp.array([2], I32), (end_col * 4 + 3)[None], t8 * 4 + 1])
    message = jnp.where(down, dn, up) * EDGE

    wet = (o_id >= 0).astype(F32)
    lanes = jnp.arange(WIDTH)
    low = jnp.stack([jnp.stack([wet[:, 6], wet[:, 4]], 1).reshape(8), jnp.stack([wet[:, 5], wet[:, 4]], 1).reshape(8)])
    high = jnp.stack([jnp.stack([wet[:, 7], wet[:, 5]], 1).reshape(8), jnp.stack([wet[:, 7], wet[:, 6]], 1).reshape(8)])
    low = jnp.where(lanes == 0, low[..., None], 1.0)
    high = jnp.where(lanes == WIDTH - 1, high[..., None], 1.0)
    rowf = o_row.astype(F32) * WIDTH
    y_n = jnp.where(o_top, rowf + (WIDTH - 1), rowf + WIDTH)
    y_row = jnp.stack([y_n, rowf - 1.0], axis=1).reshape(8, 1) + jnp.zeros((1, WIDTH), F32)
    y_col = jnp.repeat(rowf, 2)[:, None] + lanes.astype(F32)[None, :]
    cor = jnp.stack([y_row, y_col])
    cor = (cor + 0.5) * (2.0 / (ROWS * WIDTH))
    strips = jnp.stack([low, high, cor], axis=1)
    east = jnp.where(lanes == WIDTH - 1, wet[:, 3:4], 1.0)
    west = jnp.where(lanes == 0, wet[:, 2:3], 1.0)
    ones = jnp.ones((WIDTH,), F32)
    alive = o_live.astype(F32)
    faces = jnp.stack(
        [east, west, wet[:, 1:2] * ones, wet[:, 0:1] * ones, rowf[:, None] * ones, alive[:, None] * ones] + [jnp.zeros((4, WIDTH), F32)] * 2,
        axis=1,
    )

    final = jnp.concatenate([source.reshape(16), (o_top & (o_id[:, 1] >= 0)).astype(I32), core[None].astype(I32)])
    return {
        "overflow": overflow,
        "message": jnp.concatenate([message, core[None]]).astype(I32),
        "picks": picks.astype(I32),
        "take": jnp.concatenate([take, c_take, c_turn, c_dst]).astype(I32),
        "got": got,
        "got_z": got_z,
        "got_rank": got_rank,
        "final": final.astype(I32),
        "top": o_top.astype(I32),
        "strips": strips,
        "faces": faces,
    }


def rims_kernel(tr, ve, out, turned):
    lane = lax.broadcasted_iota(I32, (WIDTH, WIDTH), 1) // 4
    gathered = jnp.zeros((WIDTH, WIDTH), F32)
    for slot in range(4):
        for fl in range(8):
            ref, k = (tr, fl) if fl < 4 else (ve, fl - 4)
            for depth in range(2):
                out[slot, 0, pl.ds(depth * 8 + fl, 1), :] = ref[slot, k, pl.ds(depth, 1), :]
                out[slot, 1, pl.ds(depth * 8 + fl, 1), :] = ref[slot, k, pl.ds(127 - depth, 1), :]
            tile = slot * 8 + fl
            rolled = pltpu.roll(ref[slot, k], (4 * tile + 2) % WIDTH, 1)
            gathered = jnp.where(lane == tile, rolled, gathered)
    turned[...] = gathered.T
    for slot in range(4):
        for j, (side, depth) in enumerate([(3, 1), (3, 0), (2, 0), (2, 1)]):
            out[slot, side, pl.ds(depth * 8, 8), :] = turned[pl.ds(slot * 32 + j, 8, stride=4), :]


def message_kernel(table, mine, other, chip, out):
    core = table[MSG_EDGES]
    flag = core == 0
    for t in range(4):
        for side in range(4):
            at = (t * 4 + side) * EDGE
            a, b = mine[pl.ds(at, EDGE), :], other[pl.ds(at, EDGE), :]
            chip[pl.ds(at, EDGE), :] = jnp.where(flag, a, b)
            chip[pl.ds(16 * EDGE + at, EDGE), :] = jnp.where(flag, b, a)
    for e in range(MSG_EDGES):
        at = pl.multiple_of(table[e], EDGE)
        out[pl.ds(e * EDGE, EDGE), :] = chip[pl.ds(at, EDGE), :]
    lane = lax.broadcasted_iota(I32, (8, WIDTH), 1) // 2
    corners = jnp.zeros((8, WIDTH), F32)
    for t in range(8):
        for side, base in ((1, 0), (0, 8)):
            x = chip[pl.ds((t * 4 + side) * EDGE, 8), :]
            corners = jnp.where(lane == base + t, pltpu.roll(x, 2 * (base + t) + 1, 1), corners)
    out[pl.ds(MSG_EDGES * EDGE, 8), :] = corners


def pack_kernel(table, m0, m1, m2, m3, c4, c5, out, held, far, sem):
    copies = [pltpu.make_async_copy(m, held.at[pl.ds(i * MSG, MSG)], sem.at[i]) for i, m in enumerate((m0, m1, m2, m3))]
    copies += [pltpu.make_async_copy(m, far.at[pl.ds(i * 8, 8)], sem.at[4 + i]) for i, m in enumerate((c4, c5))]
    for copy in copies:
        copy.start()
    for copy in copies:
        copy.wait()
    lane = lax.broadcasted_iota(I32, (8, WIDTH), 1) // 32
    near_c = jnp.zeros((8, WIDTH), F32)
    for i in range(4):
        x = held[pl.ds(i * MSG + MSG_EDGES * EDGE, 8), :]
        near_c = jnp.where(lane == i, pltpu.roll(x, 32 * i, 1) if i else x, near_c)
    far_c = jnp.where(lane == 0, far[pl.ds(0, 8), :], pltpu.roll(far[pl.ds(8, 8), :], 32, 1))
    for z in range(8):
        for r in range(CAP):
            at = pl.multiple_of(table[z * CAP + r], 8)
            out[pl.ds(z * CHUNK + r * EDGE, EDGE), :] = held[pl.ds(at, EDGE), :]
        out[pl.ds(z * CHUNK + CAP * EDGE, 8), :] = near_c
        out[pl.ds(z * CHUNK + CAP * EDGE + 8, 8), :] = far_c


def sort_kernel(table, got, own, other):
    lane = lax.broadcasted_iota(I32, (8, WIDTH), 1)
    for half, out in enumerate((own, other)):
        for e in range(16):
            at = pl.multiple_of(table[half * 16 + e], 8)
            out[pl.ds(e * EDGE, EDGE), :] = got[pl.ds(at, EDGE), :]
        corners = jnp.zeros((8, WIDTH), F32)
        for e in range(16):
            i = half * 16 + e
            at = pl.multiple_of(table[32 + i], 8)
            x = pltpu.roll(got[pl.ds(at, 8), :], table[64 + i], 1)
            corners = jnp.where(lane == table[96 + i], x, corners)
        out[pl.ds(16 * EDGE, 8), :] = corners


def pressure(t0, t1, s0, s1):
    r0 = t0 * (-0.3 - 0.08 * t0 + 0.05 * s0) + 0.6 * s0
    r1 = t1 * (-0.3 - 0.08 * t1 + 0.05 * s1) + 0.6 * s1
    return 0.25 * r0, 0.5 * r0 + 0.25 * r1


def stencil(c, e, w, n, s, oe, ow, on, os, f):
    def times(o, x):
        return x if o is None else o * x

    ue, uw = 0.025 * (c[2] + e[2]), 0.025 * (w[2] + c[2])
    vn, vs = 0.025 * (c[3] + n[3]), 0.025 * (s[3] + c[3])
    ae, be = times(oe, 0.05 - ue), times(oe, 0.05 + ue)
    aw, bw = times(ow, 0.05 + uw), times(ow, 0.05 - uw)
    an, bn = times(on, 0.05 - vn), times(on, 0.05 + vn)
    as_, bs = times(os, 0.05 + vs), times(os, 0.05 - vs)
    mid = 1.0 - ((be + bw) + (bn + bs))
    out = []
    for i in range(2):
        out.append(mid * c[i] + ((ae * e[i] + aw * w[i]) + (an * n[i] + as_ * s[i])))
    for i, (lo, hi, olo, ohi) in ((2, (w, e, ow, oe)), (3, (s, n, os, on))):
        lap = (times(oe, e[i] - c[i]) + times(ow, w[i] - c[i])) + (times(on, n[i] - c[i]) + times(os, s[i] - c[i]))
        grad = times(ohi, hi[4] - c[4]) + times(olo, c[4] - lo[4])
        turn = f * c[3] if i == 2 else -(f * c[2])
        out.append(c[i] + (0.1 * turn + 0.05 * (lap - grad)))
    return out


def steps_kernel(table, chip, own, other, strips, faces, tr, ve, tr_out, ve_out, held, hx, inn, crv, upd, cols, xa, xb, sem):
    sizes = (8 * 4 * EDGE, SWAP, SWAP)
    starts = (0, sizes[0], sizes[0] + SWAP)
    copies = [
        pltpu.make_async_copy(x, held.at[pl.ds(at, n)], sem.at[i]) for i, (x, at, n) in enumerate(zip((chip, own, other), starts, sizes))
    ]
    for copy in copies:
        copy.start()
    held[pl.ds(starts[2] + SWAP, EDGE), :] = jnp.zeros((EDGE, WIDTH), F32)
    for copy in copies:
        copy.wait()
    core = table[20]
    i0 = lax.broadcasted_iota(I32, (WIDTH, WIDTH), 0)
    i1 = lax.broadcasted_iota(I32, (WIDTH, WIDTH), 1)
    mirror = (i0 + i1 == WIDTH - 1).astype(F32)
    sub16 = lax.broadcasted_iota(I32, (EDGE, WIDTH), 0)
    sign = jnp.where((sub16 & 7) >= 4, -1.0, 1.0)
    lane8 = lax.broadcasted_iota(I32, (8, WIDTH), 1)
    sub8 = lax.broadcasted_iota(I32, (8, WIDTH), 0)
    even = (sub8 & 1) == 0
    corners = held[pl.ds(starts[1] + 16 * EDGE, 8), :] + held[pl.ds(starts[2] + 16 * EDGE, 8), :]
    sign8 = jnp.where(sub8 >= 4, -1.0, 1.0)

    for slot in range(4):
        fold = table[16 + slot] == 1
        top = table[21 + slot] == 1
        for side in range(4):
            at = pl.multiple_of(table[slot * 4 + side], 8)
            x = held[pl.ds(at, EDGE), :]
            if side == 1:
                flipped = jnp.dot(x, mirror, preferred_element_type=F32, precision=lax.Precision.HIGHEST) * sign
                x = jnp.where(fold, flipped, x)
            group, row = (0, 1) if side == 0 else (0, 0) if side == 1 else (1, 1) if side == 2 else (1, 0)
            row += slot * 2
            hx[group, :, row, :] = x
            inner = held[pl.ds(pl.multiple_of(core * (16 * EDGE) + (slot * 4 + side) * EDGE, 8), 8), :]
            inn[group, :, row, :] = inner
        for group, odd, lo, hi in ((0, 0, 2, 3), (0, 1, 0, 1), (1, 0, 1, 3), (1, 1, 0, 2)):
            vals = []
            for which, lane in ((lo, 0), (hi, WIDTH - 1)):
                v = pltpu.roll(corners, (lane - (slot * 4 + which)) % WIDTH, 1)
                if which >= 2:
                    v = jnp.where(top, v * sign8, v)
                vals.append(v)
            crv[group, :, slot * 2 + odd, :] = jnp.where(lane8 == 0, vals[0], vals[1])

    for group in range(2):
        low_o, high_o, cor = strips[group, 0], strips[group, 1], strips[group, 2]
        at_c, at_p, at_m, at_h, at_l = [], [], [], [], []
        for q in range(8):
            c, outer, inner, k = hx[group, q], hx[group, 8 + q], inn[group, q], crv[group, q]
            at_c.append(c)
            at_p.append(jnp.where(even, outer, inner))
            at_m.append(jnp.where(even, inner, outer))
            at_h.append(jnp.where(lane8 == WIDTH - 1, k, pltpu.roll(c, WIDTH - 1, 1)))
            at_l.append(jnp.where(lane8 == 0, k, pltpu.roll(c, 1, 1)))
        five = [x + list(pressure(x[0], x[1], x[2], x[3])) for x in (at_c, at_p, at_m, at_h, at_l)]
        for level in range(2):
            c, p, m, h, l = [[x[2 * i + level] for i in range(5)] for x in five]
            if group == 0:
                new = stencil(c, h, l, p, m, high_o, low_o, None, None, cor)
            else:
                new = stencil(c, p, m, h, l, None, None, high_o, low_o, cor)
            for i in range(4):
                upd[group, 2 * i + level] = new[i]

    for step in range(2):
        parts = [(hx if step == 0 else upd)[1, q] for q in range(8)]
        parts += list(pressure(parts[0], parts[1], parts[2], parts[3]))
        parts += [jnp.zeros((WIDTH - 80, WIDTH), F32)]
        cols[step] = jnp.concatenate(parts, axis=0).T

    lane = lax.broadcasted_iota(I32, (EDGE, WIDTH), 1)
    y16 = lax.broadcasted_iota(I32, (EDGE, WIDTH), 0).astype(F32)
    at_lo, at_hi = sub16 == 0, sub16 == EDGE - 1

    def one_slot(slot, carry):
        oe, ow = faces[slot, pl.ds(0, 1), :], faces[slot, pl.ds(1, 1), :]
        on, os = faces[slot, pl.ds(2, 1), :], faces[slot, pl.ds(3, 1), :]
        base = faces[slot, pl.ds(4, 1), :]
        alive = faces[slot, pl.ds(5, 1), :] > 0.5
        on16 = jnp.where(at_hi, on, 1.0)
        os16 = jnp.where(at_lo, os, 1.0)
        for step in range(2):
            src = xa if step == 0 else xb
            halo = hx if step == 0 else upd
            for q in range(8):
                src[q, pl.ds(7, 1), :] = halo[0, q, pl.ds(slot * 2 + 1, 1), :]
                src[q, pl.ds(136, 1), :] = halo[0, q, pl.ds(slot * 2, 1), :]
            if step == 0:
                for q in range(8):
                    ref, k = (tr, q) if q < 4 else (ve, q - 4)
                    src[q, pl.ds(8, WIDTH), :] = ref[slot, k]
            for r in range(0, 144, 16):
                p0, p1 = pressure(*[src[q, pl.ds(r, 16), :] for q in range(4)])
                src[8, pl.ds(r, 16), :] = p0
                src[9, pl.ds(r, 16), :] = p1
            for r in range(0, WIDTH, EDGE):
                f = (base + (y16 + (r + 0.5))) * (2.0 / (ROWS * WIDTH))
                for level in range(2):
                    c, e, w, n, s = [], [], [], [], []
                    for i in range(5):
                        q = 2 * i + level
                        x = src[q, pl.ds(8 + r, EDGE), :]
                        edge = pltpu.roll(cols[step, pl.ds(r, EDGE), :], WIDTH - 1 - q * 8 - 2 * slot, 1)
                        c.append(x)
                        e.append(jnp.where(lane == WIDTH - 1, edge, pltpu.roll(x, WIDTH - 1, 1)))
                        w.append(jnp.where(lane == 0, edge, pltpu.roll(x, 1, 1)))
                        n.append(src[q, pl.ds(9 + r, EDGE), :])
                        s.append(src[q, pl.ds(7 + r, EDGE), :])
                    new = stencil(
                        c, e, w, n, s, oe, ow, on16 if r == WIDTH - EDGE else None, os16 if r == 0 else None, f
                    )
                    for i in range(4):
                        if step == 0:
                            xb[2 * i + level, pl.ds(8 + r, EDGE), :] = new[i]
                        else:
                            out = tr_out if i < 2 else ve_out
                            out[slot, 2 * (i % 2) + level, pl.ds(r, EDGE), :] = jnp.where(alive, new[i], 0.0)
        return carry

    for src in (xa, xb):
        for q in range(8):
            src[q, pl.ds(0, 8), :] = jnp.zeros((8, WIDTH), F32)
            src[q, pl.ds(136, 8), :] = jnp.zeros((8, WIDTH), F32)
    lax.fori_loop(0, 4, one_slot, 0)


def shape(*dims):
    return jax.ShapeDtypeStruct(dims, F32)


def permute(x, pairs):
    return lax.ppermute(x, "blk", pairs)


def column_pairs(distance):
    pairs = []
    for i in range(DEVICES):
        j = i + 16 * distance * (1 if i % 2 == 0 else -1)
        if 0 <= j < DEVICES:
            pairs.append((i, j))
    return pairs


def exchange_z(x):
    groups = [[16 * a + 2 * z + c for z in range(8)] for a in range(16) for c in range(2)]
    return lax.all_to_all(x, "blk", 0, 0, axis_index_groups=groups, tiled=True)


def per_device(tracers, velocity, block_counts, land):
    me = lax.axis_index("blk").astype(I32)
    tab = make_tables(block_counts, land, me)
    tr = tracers.reshape(4, 4, WIDTH, WIDTH)
    ve = velocity.reshape(4, 4, WIDTH, WIDTH)
    swap = [(i, i ^ 1) for i in range(DEVICES)]

    rims = pl.pallas_call(
        rims_kernel,
        out_shape=shape(4, 4, EDGE, WIDTH),
        in_specs=[VM, VM],
        out_specs=VM,
        scratch_shapes=[pltpu.VMEM((WIDTH, WIDTH), F32)],
        compiler_params=params(16),
        name="rims",
    )(tr, ve)
    rims = rims.reshape(16 * EDGE, WIDTH)
    other = permute(rims, swap)
    chip, message = pl.pallas_call(
        message_kernel,
        out_shape=(shape(32 * EDGE, WIDTH), shape(MSG, WIDTH)),
        in_specs=[SM, VM, VM],
        out_specs=(VM, VM),
        compiler_params=params(16),
        name="message",
    )(tab["message"], rims, other)
    near = [permute(message, column_pairs(d)) for d in (1, 2, 3)]
    corners = message[MSG_EDGES * EDGE :]
    far = [permute(corners, column_pairs(d)) for d in (4, 5)]
    chunks = pl.pallas_call(
        pack_kernel,
        out_shape=shape(8 * CHUNK, WIDTH),
        in_specs=[SM] + [HB] * 6,
        out_specs=VM,
        scratch_shapes=[pltpu.VMEM((4 * MSG, WIDTH), F32), pltpu.VMEM((16, WIDTH), F32), pltpu.SemaphoreType.DMA((6,))],
        compiler_params=params(16),
        name="pack",
    )(tab["picks"][:, :CAP].reshape(-1), message, *near, *far)
    got = exchange_z(chunks.reshape(8, CHUNK, WIDTH)).reshape(8 * CHUNK, WIDTH)
    own, others = pl.pallas_call(
        sort_kernel,
        out_shape=(shape(SWAP, WIDTH), shape(SWAP, WIDTH)),
        in_specs=[SM, VM],
        out_specs=(VM, VM),
        compiler_params=params(16),
        name="sort",
    )(tab["take"], got)

    def second(args):
        own, others, message, near = args
        held = jnp.concatenate([message, *near])
        rows = tab["picks"][:, CAP:, None] + jnp.arange(EDGE, dtype=I32)
        more = exchange_z(held[rows].reshape(8, MORE * EDGE, WIDTH)).reshape(8 * MORE * EDGE, WIDTH)
        late = tab["got"] & (tab["got_rank"] >= CAP)
        start = jnp.where(late, tab["got_z"] * (MORE * EDGE) + (tab["got_rank"] - CAP) * EDGE, 0)
        new = more[start[:, None] + jnp.arange(EDGE, dtype=I32)]
        old = jnp.stack([own[: 16 * EDGE], others[: 16 * EDGE]]).reshape(32, EDGE, WIDTH)
        new = jnp.where(late[:, None, None], new, old).reshape(2, 16 * EDGE, WIDTH)
        return jnp.concatenate([new[0], own[16 * EDGE :]]), jnp.concatenate([new[1], others[16 * EDGE :]])

    own, others = lax.cond(tab["overflow"], second, lambda args: (args[0], args[1]), (own, others, message, near))
    theirs = permute(others, swap)

    tr_new, ve_new = pl.pallas_call(
        steps_kernel,
        out_shape=(shape(4, 4, WIDTH, WIDTH), shape(4, 4, WIDTH, WIDTH)),
        in_specs=[SM] + [HB] * 3 + [VM] * 4,
        out_specs=(VM, VM),
        scratch_shapes=[
            pltpu.VMEM((32 * EDGE + 2 * SWAP + EDGE, WIDTH), F32),
            pltpu.VMEM((2, EDGE, 8, WIDTH), F32),
            pltpu.VMEM((2, 8, 8, WIDTH), F32),
            pltpu.VMEM((2, 8, 8, WIDTH), F32),
            pltpu.VMEM((2, 8, 8, WIDTH), F32),
            pltpu.VMEM((2, WIDTH, WIDTH), F32),
            pltpu.VMEM((10, 144, WIDTH), F32),
            pltpu.VMEM((10, 144, WIDTH), F32),
            pltpu.SemaphoreType.DMA((3,)),
        ],
        compiler_params=params(32),
        name="steps",
    )(jnp.concatenate([tab["final"], tab["top"]]), chip, own, theirs, tab["strips"], tab["faces"], tr, ve)
    return tr_new.reshape(tracers.shape), ve_new.reshape(velocity.shape)


def solution(mesh):
    spec = P("blk", None, None, None, None)
    return jax.shard_map(
        per_device,
        mesh=mesh,
        in_specs=(spec, spec, P(), P()),
        out_specs=(spec, spec),
        check_vma=False,
    )
```

time: 1270 us -> 84.7 us (0.07)
  the two profiles are of different devices: /device:TPU:3 before, /device:TPU:27 now
where the time goes in v1:
time: 84.7 us; the launch traced here: 84.2 us
  starting transfers between devices  22.1 us (26%)
  waiting for transfers between devices  19.9 us (23%)
  local copies, waits for them, and re-layouts  13.2 us (16%)
  Pallas kernels  12.7 us (15%)
  other arithmetic  11.8 us (14%)
  between operations  3.64 us (4%)
    all_to_all x1, waiting for transfers between devices, exchange_z(): return lax.all_to_all(x, 'blk', 0, 0, axis_index_groups=groups, tiled=True)  14.5 us
    ppermute x7, starting transfers between devices, permute(): return lax.ppermute(x, 'blk', pairs)  14 us
    all_to_all x1, starting transfers between devices, exchange_z(): return lax.all_to_all(x, 'blk', 0, 0, axis_index_groups=groups, tiled=True)  8.08 us
    pallas_call x1, Pallas kernels, per_device(): pl.pallas_call(steps_kernel, out_shape=(shape(4, 4, WIDTH, WIDTH), shape(...  7.76 us
    ppermute x7, waiting for transfers between devices, permute(): return lax.ppermute(x, 'blk', pairs)  5.38 us
    another operation x6, local copies, waits for them, and re-layouts, make_tables(): jnp.stack([east, west, wet[:, 1:2] * ones, wet[:, 0:1] * ones, rowf[:, No...  3.59 us
    unnamed x28, local copies, waits for them, and re-layouts  2.5 us
    pallas_call x1, Pallas kernels, per_device(): pl.pallas_call(pack_kernel, out_shape=shape(8 * CHUNK, WIDTH), in_specs=[...  2.28 us
  transfers between devices with their start and end apart: 8, of which 2 were waited for; matrix products, arithmetic and copies ran while one was open for 28% of the time, Pallas kernels for 0%

profile of v1, /device:TPU:27, one launch (start us, length us, event | category | flops | bytes accessed | tf_op | source)
XLA Modules:
  0.0 84.2 jit_solution(6951340448591408421)
XLA Ops:
  0.6 1.2 %copy-done = f32[4,2,2,128,128]{4,3,2,1,0:T(8,128)S(1)} copy-done((f32[4,2,2,128,128]{4,3,2,1,0:T(8,128)S(1)}, f32[4,2,2,128,128]{4,3,2,1,0:T(8,128)}, u32[]{:S(2)}) %copy-start) | copy-done | bytes 1048600
  1.9 1.2 %copy-done.2 = f32[4,2,2,128,128]{4,3,2,1,0:T(8,128)S(1)} copy-done((f32[4,2,2,128,128]{4,3,2,1,0:T(8,128)S(1)}, f32[4,2,2,128,128]{4,3,2,1,0:T(8,128)}, u32[]{:S(2)}) %copy-start.2) | copy-done | bytes 1048600
  3.8 0.8 collective-permute-start
  7.6 1.2 %select_reduce_fusion.1 = s32[64,8]{1,0:T(8,128)S(1)} fusion(s32[8,884]{1,0:T(8,128)S(1)} %broadcast_add_fusion, pred[64,884]{1,0:T(8,128)(4,1)S(1)} %broadcast_compare_fusion), kind=kLoop, calls=%fused_computation.17 | loop fusion | flops 904704 | bytes 86912 | tf_op jit(solution)/shard_map/reduce_sum | solution.py:82
  10.3 0.8 fusion.27
  19.3 0.8 convolution_reduce_fusion
  20.7 2.4 %collective-permute-start.1 = (f32[296,128]{1,0:T(8,128)S(1)}, f32[296,128]{1,0:T(8,128)S(1)}, u32[]{:S(2)}, u32[]{:S(2)}) collective-permute-start(f32[296,128]{1,0:T(8,128)S(1)} %get-tuple-element.45.m0), channel_id=1, source_target_pairs={{0,16},{2,18},{4,20},{6,22},{8,24},{10,26},{12,28},{14,30},{16,32}... | collective-permute-start | bytes 454664 | tf_op jit(solution)/shard_map/ppermute | solution.py:438
  23.1 2.6 %collective-permute-start.2 = (f32[296,128]{1,0:T(8,128)S(1)}, f32[296,128]{1,0:T(8,128)S(1)}, u32[]{:S(2)}, u32[]{:S(2)}) collective-permute-start(f32[296,128]{1,0:T(8,128)S(1)} %get-tuple-element.45.m0), channel_id=1, source_target_pairs={{0,32},{2,34},{4,36},{6,38},{8,40},{10,42},{12,44},{14,46},{16,48}... | collective-permute-start | bytes 454664 | tf_op jit(solution)/shard_map/ppermute | solution.py:438
  25.7 3.8 %collective-permute-start.3 = (f32[296,128]{1,0:T(8,128)S(1)}, f32[296,128]{1,0:T(8,128)S(1)}, u32[]{:S(2)}, u32[]{:S(2)}) collective-permute-start(f32[296,128]{1,0:T(8,128)S(1)} %get-tuple-element.45.m0), channel_id=1, source_target_pairs={{0,48},{2,50},{4,52},{6,54},{8,56},{10,58},{12,60},{14,62},{16,64}... | collective-permute-start | bytes 454664 | tf_op jit(solution)/shard_map/ppermute | solution.py:438
  29.5 2.0 %collective-permute-start.4 = (f32[8,128]{1,0:T(8,128)S(1)}, f32[8,128]{1,0:T(8,128)S(1)}, u32[]{:S(2)}, u32[]{:S(2)}) collective-permute-start(f32[8,128]{1,0:T(8,128)S(1)} %slice.279), channel_id=1, source_target_pairs={{0,64},{2,66},{4,68},{6,70},{8,72},{10,74},{12,76},{14,78},{16,80}... | collective-permute-start | bytes 12296 | tf_op jit(solution)/shard_map/ppermute | solution.py:438
  31.6 1.9 %collective-permute-start.5 = (f32[8,128]{1,0:T(8,128)S(1)}, f32[8,128]{1,0:T(8,128)S(1)}, u32[]{:S(2)}, u32[]{:S(2)}) collective-permute-start(f32[8,128]{1,0:T(8,128)S(1)} %slice.279), channel_id=1, source_target_pairs={{0,80},{2,82},{4,84},{6,86},{8,88},{10,90},{12,92},{14,94},{16,96}... | collective-permute-start | bytes 12296 | tf_op jit(solution)/shard_map/ppermute | solution.py:438
  34.2 5.4 %collective-permute-done.5.c5 = f32[8,128]{1,0:T(8,128)S(1)} collective-permute-done((f32[8,128]{1,0:T(8,128)S(1)}, f32[8,128]{1,0:T(8,128)S(1)}, u32[]{:S(2)}, u32[]{:S(2)}) %collective-permute-start.5) | collective-permute-done | bytes 4128 | tf_op jit(solution)/shard_map/ppermute | solution.py:438
  39.5 2.3 %pack.1 = f32[1152,128]{1,0:T(8,128)} custom-call(s32[64]{0:T(128)S(1)} %reshape.726.table, f32[296,128]{1,0:T(8,128)S(1)} %get-tuple-element.45.m0, f32[296,128]{1,0:T(8,128)S(1)} %collective-permute-done.1.m1, f32[296,128]{1,0:T(8,128)S(1)} %collective-permute-done.2.m2, f32[296,128]{1,0:T(8,128)S(1)} %collective-permute-done.3.m3, ...), custom_call_target="tpu_custom_call" | custom-call | tf_op jit(solution)/shard_map/pack/pallas_call | solution.py:484
  41.9 8.1 %all-to-all-start.1 = ((f32[8,144,128]{2,1,0:T(8,128)}), f32[8,144,128]{2,1,0:T(8,128)S(1)}, u32[]{:S(2)}, u32[]{:S(2)}) async-start(f32[8,144,128]{2,1,0:T(8,128)} %bitcast.21), calls=%async_computation.1 | async-start | bytes 1179648 | tf_op jit(solution)/shard_map/all_to_all | solution.py:452
  54.8 14.5 %all-to-all-done.1 = f32[8,144,128]{2,1,0:T(8,128)S(1)} async-done(((f32[8,144,128]{2,1,0:T(8,128)}), f32[8,144,128]{2,1,0:T(8,128)S(1)}, u32[]{:S(2)}, u32[]{:S(2)}) %all-to-all-start.1) | async-done | bytes 589856 | tf_op jit(solution)/shard_map/all_to_all | solution.py:452
  69.3 1.4 %sort.1 = (f32[264,128]{1,0:T(8,128)}, f32[264,128]{1,0:T(8,128)}) custom-call(s32[128]{0:T(128)S(1)} %pad_add_fusion.10.table, f32[1152,128]{1,0:T(8,128)S(1)} %bitcast.65), custom_call_target="tpu_custom_call" | custom-call | tf_op jit(solution)/shard_map/sort/pallas_call | solution.py:494
  71.3 0.8 pad_add_fusion.8.table
  72.1 0.7 stack.133
  72.8 0.7 stack.134
  73.5 0.7 stack.135
  74.2 0.7 stack.136
  75.0 0.7 stack.138.faces
  75.7 0.7 pad_maximum_fusion.4.strips
  76.4 7.8 %steps.1 = (f32[4,4,128,128]{3,2,1,0:T(8,128)}, f32[4,4,128,128]{3,2,1,0:T(8,128)}) custom-call(s32[25]{0:T(128)S(1)} %pad_add_fusion.8.table, f32[512,128]{1,0:T(8,128)S(1)} %get-tuple-element.44.chip, f32[264,128]{1,0:T(8,128)} %get-tuple-element.48.own, f32[264,128]{1,0:T(8,128)S(1)} %collective-permute-done.6.other, ...), custom_call_target="tpu_custom_call" | custom-call | tf_op jit(solution)/shard_map/steps/pallas_call | solution.py:518
  (184 shorter events, 17.5 us)
Async XLA Ops:
  0.6 1.2 %copy-start = (f32[4,2,2,128,128]{4,3,2,1,0:T(8,128)S(1)}, f32[4,2,2,128,128]{4,3,2,1,0:T(8,128)}, u32[]{:S(2)}) copy-start(f32[4,2,2,128,128]{4,3,2,1,0:T(8,128)} %param.10) | copy-start | bytes 3145732
  1.9 1.2 %copy-start.2 = (f32[4,2,2,128,128]{4,3,2,1,0:T(8,128)S(1)}, f32[4,2,2,128,128]{4,3,2,1,0:T(8,128)}, u32[]{:S(2)}) copy-start(f32[4,2,2,128,128]{4,3,2,1,0:T(8,128)} %param.11) | copy-start | bytes 3145732
  3.1 1.5 %copy-start.7 = (s32[26,34]{1,0:T(8,128)S(1)}, s32[26,34]{1,0:T(8,128)}, u32[]{:S(2)}) copy-start(s32[26,34]{1,0:T(8,128)} %param.13) | copy-start | bytes 10612
  3.1 1.6 %copy-start.16 = (s32[256]{0:T(256)S(1)}, s32[256]{0:T(256)}, u32[]{:S(2)}) copy-start(s32[256]{0:T(256)} %param.12) | copy-start | bytes 3076
  3.8 5.4 %copy-start.17 = (s32[4]{0:T(128)S(1)}, s32[4]{0:T(128)}, u32[]{:S(2)}) copy-start(s32[4]{0:T(128)} %constant.46) | copy-start | bytes 52
  3.8 5.4 %copy-start.18 = (s32[4]{0:T(128)S(1)}, s32[4]{0:T(128)}, u32[]{:S(2)}) copy-start(s32[4]{0:T(128)} %constant.89.clone) | copy-start | bytes 52
  3.8 5.4 %copy-start.19 = (pred[4]{0:T(512)(128)(4,1)S(1)}, pred[4]{0:T(512)(128)(4,1)}, u32[]{:S(2)}) copy-start(pred[4]{0:T(512)(128)(4,1)} %constant.32.clone) | copy-start | bytes 16
  3.8 16.3 %collective-permute-start = (f32[256,128]{1,0:T(8,128)S(1)}, f32[256,128]{1,0:T(8,128)S(1)}, u32[]{:S(2)}, u32[]{:S(2)}) collective-permute-start(f32[256,128]{1,0:T(8,128)S(1)} %bitcast.66), channel_id=1, source_target_pairs={{0,1},{1,0},{2,3},{3,2},{4,5},{5,4},{6,7},{7,6},{8,9},{9,8},{10,11... | collective-permute-start | bytes 393224 | tf_op jit(solution)/shard_map/ppermute | solution.py:438
  13.8 6.3 %copy-start.9 = (pred[32]{0:T(512)(128)(4,1)}, pred[32]{0:T(512)(128)(4,1)S(1)}, u32[]{:S(2)}) copy-start(pred[32]{0:T(512)(128)(4,1)S(1)} %reshape.721) | copy-start | bytes 100
  15.1 5.0 %copy-start.8 = (f32[4]{0:T(128)}, f32[4]{0:T(128)S(1)}, u32[]{:S(2)}) copy-start(f32[4]{0:T(128)S(1)} %get-tuple-element.177) | copy-start | bytes 52
  20.7 18.8 %collective-permute-start.1 = (f32[296,128]{1,0:T(8,128)S(1)}, f32[296,128]{1,0:T(8,128)S(1)}, u32[]{:S(2)}, u32[]{:S(2)}) collective-permute-start(f32[296,128]{1,0:T(8,128)S(1)} %get-tuple-element.45.m0), channel_id=1, source_target_pairs={{0,16},{2,18},{4,20},{6,22},{8,24},{10,26},{12,28},{14,30},{16,32}... | collective-permute-start | bytes 454664 | tf_op jit(solution)/shard_map/ppermute | solution.py:438
  23.1 16.4 %collective-permute-start.2 = (f32[296,128]{1,0:T(8,128)S(1)}, f32[296,128]{1,0:T(8,128)S(1)}, u32[]{:S(2)}, u32[]{:S(2)}) collective-permute-start(f32[296,128]{1,0:T(8,128)S(1)} %get-tuple-element.45.m0), channel_id=1, source_target_pairs={{0,32},{2,34},{4,36},{6,38},{8,40},{10,42},{12,44},{14,46},{16,48}... | collective-permute-start | bytes 454664 | tf_op jit(solution)/shard_map/ppermute | solution.py:438
  25.7 13.8 %collective-permute-start.3 = (f32[296,128]{1,0:T(8,128)S(1)}, f32[296,128]{1,0:T(8,128)S(1)}, u32[]{:S(2)}, u32[]{:S(2)}) collective-permute-start(f32[296,128]{1,0:T(8,128)S(1)} %get-tuple-element.45.m0), channel_id=1, source_target_pairs={{0,48},{2,50},{4,52},{6,54},{8,56},{10,58},{12,60},{14,62},{16,64}... | collective-permute-start | bytes 454664 | tf_op jit(solution)/shard_map/ppermute | solution.py:438
  29.5 4.6 %collective-permute-start.4 = (f32[8,128]{1,0:T(8,128)S(1)}, f32[8,128]{1,0:T(8,128)S(1)}, u32[]{:S(2)}, u32[]{:S(2)}) collective-permute-start(f32[8,128]{1,0:T(8,128)S(1)} %slice.279), channel_id=1, source_target_pairs={{0,64},{2,66},{4,68},{6,70},{8,72},{10,74},{12,76},{14,78},{16,80}... | collective-permute-start | bytes 12296 | tf_op jit(solution)/shard_map/ppermute | solution.py:438
  31.6 8.0 %collective-permute-start.5 = (f32[8,128]{1,0:T(8,128)S(1)}, f32[8,128]{1,0:T(8,128)S(1)}, u32[]{:S(2)}, u32[]{:S(2)}) collective-permute-start(f32[8,128]{1,0:T(8,128)S(1)} %slice.279), channel_id=1, source_target_pairs={{0,80},{2,82},{4,84},{6,86},{8,88},{10,90},{12,92},{14,94},{16,96}... | collective-permute-start | bytes 12296 | tf_op jit(solution)/shard_map/ppermute | solution.py:438
  39.5 2.3 %copy-start.4 = (f32[296,128]{1,0:T(8,128)}, f32[296,128]{1,0:T(8,128)S(1)}, u32[]{:S(2)}) copy-start(f32[296,128]{1,0:T(8,128)S(1)} %collective-permute-done.3.m3) | copy-start | bytes 454660
  41.8 28.8 %copy-start.10 = (pred[32]{0:T(512)(128)(4,1)S(1)}, pred[32]{0:T(512)(128)(4,1)}, u32[]{:S(2)}) copy-start(pred[32]{0:T(512)(128)(4,1)} %copy-done.9) | copy-start | bytes 100
  41.8 28.8 %copy-start.13 = (s32[32]{0:T(128)S(1)}, s32[32]{0:T(128)}, u32[]{:S(2)}) copy-start(s32[32]{0:T(128)} %get-tuple-element.110) | copy-start | bytes 388
  41.9 27.4 %all-to-all-start.1 = ((f32[8,144,128]{2,1,0:T(8,128)}), f32[8,144,128]{2,1,0:T(8,128)S(1)}, u32[]{:S(2)}, u32[]{:S(2)}) async-start(f32[8,144,128]{2,1,0:T(8,128)} %bitcast.21), calls=%async_computation.1 | async-start | bytes 1179648 | tf_op jit(solution)/shard_map/all_to_all | solution.py:452
  70.7 5.7 %copy-start.1 = (f32[4,2,2,128,128]{4,3,2,1,0:T(8,128)S(1)}, f32[4,2,2,128,128]{4,3,2,1,0:T(8,128)}, u32[]{:S(2)}) copy-start(f32[4,2,2,128,128]{4,3,2,1,0:T(8,128)} %param.10) | copy-start | bytes 3145732
  70.7 5.7 %copy-start.3 = (f32[4,2,2,128,128]{4,3,2,1,0:T(8,128)S(1)}, f32[4,2,2,128,128]{4,3,2,1,0:T(8,128)}, u32[]{:S(2)}) copy-start(f32[4,2,2,128,128]{4,3,2,1,0:T(8,128)} %param.11) | copy-start | bytes 3145732
  70.7 5.7 %collective-permute-start.6 = (f32[264,128]{1,0:T(8,128)}, f32[264,128]{1,0:T(8,128)S(1)}, u32[]{:S(2)}, u32[]{:S(2)}) collective-permute-start(f32[264,128]{1,0:T(8,128)} %get-tuple-element.49), channel_id=1, source_target_pairs={{0,1},{1,0},{2,3},{3,2},{4,5},{5,4},{6,7},{7,6},{8,9},{9,8},{10,11... | collective-permute-start | bytes 405512 | tf_op jit(solution)/shard_map/ppermute | solution.py:438

commit v2 on v1

v2 whole, which is shorter than its diff:
```python
import jax
import jax.numpy as jnp
from jax import lax
from jax.experimental import pallas as pl
from jax.experimental.pallas import tpu as pltpu
from jax.sharding import PartitionSpec as P

DEVICES = 256
ROWS, COLS = 26, 34
WIDTH = 128
CAP = 8
MORE = 10
EDGE = 16
MSG_EDGES = 18
MSG = MSG_EDGES * EDGE + 8
CHUNK = CAP * EDGE + 16
SWAP = 16 * EDGE + 8
F32 = jnp.float32
I32 = jnp.int32


def params(mib):
    return pltpu.CompilerParams(vmem_limit_bytes=mib * 1024 * 1024)


VM = pl.BlockSpec(memory_space=pltpu.VMEM)
SM = pl.BlockSpec(memory_space=pltpu.SMEM)
HB = pl.BlockSpec(memory_space=pl.ANY)


CODES = 28


def lane_iota(rows):
    return lax.broadcasted_iota(I32, (rows, WIDTH), 1)


def row_iota(rows):
    return lax.broadcasted_iota(I32, (rows, WIDTH), 0)


def exact_dot(a, b):
    return jnp.dot(a.astype(jnp.bfloat16), b.astype(jnp.bfloat16), preferred_element_type=F32)


def build_tables(me, counts, land, board, codes, mine, load):
    column, zed, core = me >> 4, (me >> 1) & 7, me & 1
    board[...] = jnp.ones((32, WIDTH), I32)
    board[pl.ds(0, ROWS), pl.ds(0, COLS)] = land[...]
    sea = board[...] == 0
    lane, row = lane_iota(32), row_iota(32)
    ones = sea.astype(F32)
    i, j = row_iota(WIDTH), lane_iota(WIDTH)
    along = exact_dot(ones, i <= j)
    totals = exact_dot(ones, i >= 0)
    li, lj = lax.broadcasted_iota(I32, (32, 32), 0), lax.broadcasted_iota(I32, (32, 32), 1)
    pos = (exact_dot(lj < li, totals) + along - ones).astype(I32)

    def device(n, carry):
        end, owner, start = carry
        for k in range(8):
            d = n * 8 + k
            end = end + counts[d]
            past = pos >= end
            owner = jnp.where(past, d + 1, owner)
            start = jnp.where(past, end, start)
        return end, owner, start

    zero = jnp.zeros((32, WIDTH), I32)
    _, owner, start = lax.fori_loop(0, DEVICES // 8, device, (jnp.int32(0), zero, zero))
    ids = jnp.where(sea, owner * 4 + pos - start, -1).astype(F32)

    def west(x):
        return jnp.where(lane == 0, pltpu.roll(x, WIDTH - COLS + 1, 1), pltpu.roll(x, 1, 1))

    def east(x):
        return jnp.where(lane == COLS - 1, pltpu.roll(x, COLS - 1, 1), pltpu.roll(x, WIDTH - 1, 1))

    mirror = (i + j == COLS - 1).astype(F32)
    folded = jnp.dot(ids, mirror, preferred_element_type=F32, precision=lax.Precision.HIGHEST)
    south = jnp.where(row == 0, -1.0, pltpu.roll(ids, 1, 0))
    north = jnp.where(row == ROWS - 1, folded, pltpu.roll(ids, 31, 0))
    near = [south, north, west(ids), east(ids), west(south), east(south), west(north), east(north)]
    pairs = [(near[2 * k] + 1.0) * 2048.0 + (near[2 * k + 1] + 1.0) for k in range(4)]
    place = (row * WIDTH + lane).astype(F32)

    chip = jnp.right_shift(ids.astype(I32), 3)
    kinds = []
    for k in range(4):
        source = jnp.right_shift(near[k].astype(I32), 3)
        away = sea & (source >= 0) & (source != chip)
        kinds.append(jnp.where(away, (source & 7) + jnp.where(source > chip, 8, 0), -1))
    kind_row = row_iota(16)
    counted = jnp.zeros((WIDTH, 16), F32)
    for r in range(ROWS):
        is_chip = (chip[r : r + 1, :] == i).astype(jnp.bfloat16)
        of_kind = sum((kinds[k][r : r + 1, :] == kind_row).astype(F32) for k in range(4)).astype(jnp.bfloat16)
        counted += lax.dot_general(is_chip, of_kind, (((1,), (1,)), ((), ())), preferred_element_type=F32)
    load[...] = jnp.broadcast_to(jnp.max(counted), (8, WIDTH)).astype(I32)

    slot = row_iota(64)
    want = (column * 64 + slot).astype(F32)
    found = [jnp.zeros((64, WIDTH), F32) for _ in range(4)] + [jnp.full((64, WIDTH), -1.0, F32)]
    for r in range(ROWS):
        hit = ids[r : r + 1, :] == want
        for k, x in enumerate(pairs + [place]):
            found[k] = jnp.where(hit, x[r : r + 1, :], found[k])
    found = [jnp.max(x, axis=1, keepdims=True).astype(I32) for x in found]
    place = found[4]
    live = place >= 0
    block_row, block_col = jnp.right_shift(place, 7), place & 127
    top = live & (block_row == ROWS - 1)
    ids8 = []
    for k in range(4):
        ids8 += [jnp.right_shift(found[k], 11) - 1, (found[k] & 2047) - 1]
    slot1 = lax.broadcasted_iota(I32, (64, 1), 0)
    here = column * 8 + jnp.right_shift(slot1, 3)
    down = core == 1
    items = {}
    for k in range(8):
        valid = ids8[k] >= 0
        source, t = jnp.right_shift(ids8[k], 3), ids8[k] & 7
        z, delta = source & 7, jnp.abs(jnp.right_shift(source, 3) - column)
        lower, same = source < here, source == here
        items[16 + k] = valid.astype(I32)
        if k < 4:
            flow = valid & ~same & (lower != down)
            if k < 2:
                edge = t if k == 0 else t + jnp.where(top & down, 10, 0)
            else:
                edge = jnp.where(down, 11 - k, 6 + k)
            at = delta * (MSG // 8) + edge * (EDGE // 8) + 1
            items[k] = jnp.where(flow & (z == zed), at, 0)
            items[4 + k] = jnp.where(flow, z, -1)
            of = (1, 0, 3, 2)[k]
            if k == 1:
                of = jnp.where(top, 1, 0)
            close = (t * 4 + of) * (EDGE // 8)
            base = jnp.where(lower != down, 4 * EDGE, 4 * EDGE + SWAP // 8)
            far = ((slot1 & 3) * 4 + k) * (EDGE // 8) + base
            items[8 + k] = jnp.where(valid, jnp.where(same, close, far), 4 * EDGE + 2 * SWAP // 8)
        else:
            flow = valid & ((lower | same) != down)
            hi = (0, 1, 0, 1)[k - 4]
            lane_at = 2 * t + hi
            if k >= 6:
                lane_at = jnp.where(top, 2 * t + 1 - hi, 16 + 2 * t + hi)
            at = z * (CHUNK // 8) + CAP * EDGE // 8 + jnp.right_shift(delta, 2)
            items[8 + k] = jnp.where(flow, at * WIDTH + 32 * (delta & 3) + lane_at, -1)
    items[24], items[25], items[26], items[27] = live.astype(I32), top.astype(I32), block_row, block_col
    lane64 = lane_iota(64)
    table = jnp.zeros((64, WIDTH), I32)
    for k in range(CODES):
        table = jnp.where(lane64 == k, items[k], table)
    codes[...] = table
    mine[...] = codes[pl.ds(pl.multiple_of(zed * 8, 8), 8), :]


def start_kernel(counts, land, tr_hbm, ve_hbm, out, codes, mine, load, board, tr, ve, turned, sem):
    copies = [pltpu.make_async_copy(tr_hbm, tr, sem.at[0]), pltpu.make_async_copy(ve_hbm, ve, sem.at[1])]
    for copy in copies:
        copy.start()
    build_tables(lax.axis_index("blk").astype(I32), counts, land, board, codes, mine, load)
    for copy in copies:
        copy.wait()
    lane = lane_iota(WIDTH) // 4
    gathered = jnp.zeros((WIDTH, WIDTH), F32)
    for slot in range(4):
        for fl in range(8):
            ref, k = (tr, fl) if fl < 4 else (ve, fl - 4)
            for depth in range(2):
                out[pl.ds((slot * 4 + 0) * EDGE + depth * 8 + fl, 1), :] = ref[slot, k, pl.ds(depth, 1), :]
                out[pl.ds((slot * 4 + 1) * EDGE + depth * 8 + fl, 1), :] = ref[slot, k, pl.ds(127 - depth, 1), :]
            tile = slot * 8 + fl
            rolled = pltpu.roll(ref[slot, k], (4 * tile + 2) % WIDTH, 1)
            gathered = jnp.where(lane == tile, rolled, gathered)
    turned[...] = gathered.T
    for slot in range(4):
        for j, (side, depth) in enumerate([(3, 1), (3, 0), (2, 0), (2, 1)]):
            out[pl.ds((slot * 4 + side) * EDGE + depth * 8, 8), :] = turned[pl.ds(slot * 32 + j, 8, stride=4), :]


def message_kernel(table, mine, other, chip, out):
    core = lax.axis_index("blk").astype(I32) & 1
    flag = core == 0
    for t in range(4):
        for side in range(4):
            at = (t * 4 + side) * EDGE
            a, b = mine[pl.ds(at, EDGE), :], other[pl.ds(at, EDGE), :]
            chip[pl.ds(at, EDGE), :] = jnp.where(flag, a, b)
            chip[pl.ds(16 * EDGE + at, EDGE), :] = jnp.where(flag, b, a)
    last, first_col, last_col = jnp.int32(0), jnp.int32(0), jnp.int32(0)
    for t in range(8):
        live, col = table[t, 24] == 1, table[t, 27]
        last = jnp.where(live, t, last)
        first_col = jnp.where(live & (col == 0), t, first_col)
        live, col = table[7 - t, 24] == 1, table[7 - t, 27]
        last_col = jnp.where(live & (col == COLS - 1), 7 - t, last_col)
    for t in range(8):
        at = pl.multiple_of(jnp.where(flag, t * 4 + 1, t * 4) * EDGE, EDGE)
        out[pl.ds(t * EDGE, EDGE), :] = chip[pl.ds(at, EDGE), :]
        out[pl.ds((10 + t) * EDGE, EDGE), :] = chip[pl.ds((t * 4 + 1) * EDGE, EDGE), :]
    for e, edge in ((8, jnp.where(flag, last * 4 + 3, 2)), (9, jnp.where(flag, first_col * 4 + 2, last_col * 4 + 3))):
        at = pl.multiple_of(edge * EDGE, EDGE)
        out[pl.ds(e * EDGE, EDGE), :] = chip[pl.ds(at, EDGE), :]
    lane = lax.broadcasted_iota(I32, (8, WIDTH), 1) // 2
    corners = jnp.zeros((8, WIDTH), F32)
    for t in range(8):
        for side, base in ((1, 0), (0, 8)):
            x = chip[pl.ds((t * 4 + side) * EDGE, 8), :]
            corners = jnp.where(lane == base + t, pltpu.roll(x, 2 * (base + t) + 1, 1), corners)
    out[pl.ds(MSG_EDGES * EDGE, 8), :] = corners


def pack_kernel(codes, m0, m1, m2, m3, c4, c5, out, held, far, table, sem):
    copies = [pltpu.make_async_copy(m, held.at[pl.ds(i * MSG, MSG)], sem.at[i]) for i, m in enumerate((m0, m1, m2, m3))]
    copies += [pltpu.make_async_copy(m, far.at[pl.ds(i * 8, 8)], sem.at[4 + i]) for i, m in enumerate((c4, c5))]
    for copy in copies:
        copy.start()
    for z in range(8):
        for r in range(CAP):
            table[z * 32 + r] = 0
        count = jnp.int32(0)
        for t in range(8):
            for side in range(4):
                code = codes[z * 8 + t, side]
                table[z * 32 + count] = code
                count += (code > 0).astype(I32)
    for copy in copies:
        copy.wait()
    lane = lax.broadcasted_iota(I32, (8, WIDTH), 1) // 32
    near_c = jnp.zeros((8, WIDTH), F32)
    for i in range(4):
        x = held[pl.ds(i * MSG + MSG_EDGES * EDGE, 8), :]
        near_c = jnp.where(lane == i, pltpu.roll(x, 32 * i, 1) if i else x, near_c)
    far_c = jnp.where(lane == 0, far[pl.ds(0, 8), :], pltpu.roll(far[pl.ds(8, 8), :], 32, 1))
    for z in range(8):
        for r in range(CAP):
            at = pl.multiple_of(jnp.maximum(table[z * 32 + r] - 1, 0) * 8, 8)
            out[pl.ds(z * CHUNK + r * EDGE, EDGE), :] = held[pl.ds(at, EDGE), :]
        out[pl.ds(z * CHUNK + CAP * EDGE, 8), :] = near_c
        out[pl.ds(z * CHUNK + CAP * EDGE + 8, 8), :] = far_c


def sort_kernel(table, got, own, other, taken, rows):
    core = lax.axis_index("blk").astype(I32) & 1
    for z in range(8):
        taken[z] = 0
    for t in range(8):
        for side in range(4):
            code = table[t, 4 + side]
            z = jnp.maximum(code, 0)
            rank = taken[z]
            taken[z] = rank + (code >= 0).astype(I32)
            rows[t * 4 + side] = z * CHUNK + jnp.minimum(rank, CAP - 1) * EDGE
    lane = lane_iota(8)
    for half, out in enumerate((own, other)):
        first = (core ^ half) * 4
        corners = jnp.zeros((8, WIDTH), F32)
        for e in range(16):
            at = pl.multiple_of(rows[first * 4 + e], 8)
            out[pl.ds(e * EDGE, EDGE), :] = got[pl.ds(at, EDGE), :]
            code = table[first + e // 4, 12 + e % 4]
            turn = (e - code) & (WIDTH - 1)
            at = pl.multiple_of(jnp.right_shift(jnp.maximum(code, 0), 7) * 8, 8)
            corners = jnp.where(lane == jnp.where(code >= 0, e, -1), pltpu.roll(got[pl.ds(at, 8), :], turn, 1), corners)
        out[pl.ds(16 * EDGE, 8), :] = corners


def pressure(t0, t1, s0, s1):
    r0 = t0 * (-0.3 - 0.08 * t0 + 0.05 * s0) + 0.6 * s0
    r1 = t1 * (-0.3 - 0.08 * t1 + 0.05 * s1) + 0.6 * s1
    return 0.25 * r0, 0.5 * r0 + 0.25 * r1


def stencil(c, e, w, n, s, oe, ow, on, os, f):
    def times(o, x):
        return x if o is None else o * x

    ue, uw = 0.025 * (c[2] + e[2]), 0.025 * (w[2] + c[2])
    vn, vs = 0.025 * (c[3] + n[3]), 0.025 * (s[3] + c[3])
    ae, be = times(oe, 0.05 - ue), times(oe, 0.05 + ue)
    aw, bw = times(ow, 0.05 + uw), times(ow, 0.05 - uw)
    an, bn = times(on, 0.05 - vn), times(on, 0.05 + vn)
    as_, bs = times(os, 0.05 + vs), times(os, 0.05 - vs)
    mid = 1.0 - ((be + bw) + (bn + bs))
    out = []
    for i in range(2):
        out.append(mid * c[i] + ((ae * e[i] + aw * w[i]) + (an * n[i] + as_ * s[i])))
    for i, (lo, hi, olo, ohi) in ((2, (w, e, ow, oe)), (3, (s, n, os, on))):
        lap = (times(oe, e[i] - c[i]) + times(ow, w[i] - c[i])) + (times(on, n[i] - c[i]) + times(os, s[i] - c[i]))
        grad = times(ohi, hi[4] - c[4]) + times(olo, c[4] - lo[4])
        turn = f * c[3] if i == 2 else -(f * c[2])
        out.append(c[i] + (0.1 * turn + 0.05 * (lap - grad)))
    return out


def steps_kernel(table, chip, own, other, tr, ve, tr_out, ve_out, held, hx, inn, crv, upd, cols, xa, xb, sem):
    sizes = (8 * 4 * EDGE, SWAP, SWAP)
    starts = (0, sizes[0], sizes[0] + SWAP)
    copies = [
        pltpu.make_async_copy(x, held.at[pl.ds(at, n)], sem.at[i]) for i, (x, at, n) in enumerate(zip((chip, own, other), starts, sizes))
    ]
    for copy in copies:
        copy.start()
    held[pl.ds(starts[2] + SWAP, EDGE), :] = jnp.zeros((EDGE, WIDTH), F32)
    for copy in copies:
        copy.wait()
    core = lax.axis_index("blk").astype(I32) & 1

    def item(slot, k):
        return table[core * 4 + slot, k]

    def factor(slot, k):
        return item(slot, k).astype(F32)

    i0 = lax.broadcasted_iota(I32, (WIDTH, WIDTH), 0)
    i1 = lax.broadcasted_iota(I32, (WIDTH, WIDTH), 1)
    mirror = (i0 + i1 == WIDTH - 1).astype(F32)
    sub16 = lax.broadcasted_iota(I32, (EDGE, WIDTH), 0)
    sign = jnp.where((sub16 & 7) >= 4, -1.0, 1.0)
    lane8 = lax.broadcasted_iota(I32, (8, WIDTH), 1)
    sub8 = lax.broadcasted_iota(I32, (8, WIDTH), 0)
    even = (sub8 & 1) == 0
    corners = held[pl.ds(starts[1] + 16 * EDGE, 8), :] + held[pl.ds(starts[2] + 16 * EDGE, 8), :]
    sign8 = jnp.where(sub8 >= 4, -1.0, 1.0)

    for slot in range(4):
        top = item(slot, 25) == 1
        for side in range(4):
            at = pl.multiple_of(item(slot, 8 + side) * 8, 8)
            x = held[pl.ds(at, EDGE), :]
            if side == 1:
                flipped = jnp.dot(x, mirror, preferred_element_type=F32, precision=lax.Precision.HIGHEST) * sign
                x = jnp.where(top, flipped, x)
            group, row = (0, 1) if side == 0 else (0, 0) if side == 1 else (1, 1) if side == 2 else (1, 0)
            row += slot * 2
            hx[group, :, row, :] = x
            inner = held[pl.ds(pl.multiple_of(core * (16 * EDGE) + (slot * 4 + side) * EDGE, 8), 8), :]
            inn[group, :, row, :] = inner
        for group, odd, lo, hi in ((0, 0, 2, 3), (0, 1, 0, 1), (1, 0, 1, 3), (1, 1, 0, 2)):
            vals = []
            for which, lane in ((lo, 0), (hi, WIDTH - 1)):
                v = pltpu.roll(corners, (lane - (slot * 4 + which)) % WIDTH, 1)
                if which >= 2:
                    v = jnp.where(top, v * sign8, v)
                vals.append(v)
            crv[group, :, slot * 2 + odd, :] = jnp.where(lane8 == 0, vals[0], vals[1])

    for group in range(2):
        low_o, high_o, cor = jnp.ones((8, WIDTH), F32), jnp.ones((8, WIDTH), F32), jnp.zeros((8, WIDTH), F32)
        for slot in range(4):
            first = factor(slot, 26) * float(WIDTH)
            for odd in range(2):
                lo, hi = ((22, 23), (20, 21))[odd] if group == 0 else ((21, 23), (20, 22))[odd]
                here = sub8 == slot * 2 + odd
                low_o = jnp.where(here & (lane8 == 0), factor(slot, lo), low_o)
                high_o = jnp.where(here & (lane8 == WIDTH - 1), factor(slot, hi), high_o)
                if group == 1:
                    y = first
                elif odd:
                    y = first - 1.0
                else:
                    y = first + jnp.where(item(slot, 25) == 1, WIDTH - 1.0, float(WIDTH))
                cor = jnp.where(here, y, cor)
        if group == 1:
            cor = cor + lane8.astype(F32)
        cor = (cor + 0.5) * (2.0 / (ROWS * WIDTH))
        at_c, at_p, at_m, at_h, at_l = [], [], [], [], []
        for q in range(8):
            c, outer, inner, k = hx[group, q], hx[group, 8 + q], inn[group, q], crv[group, q]
            at_c.append(c)
            at_p.append(jnp.where(even, outer, inner))
            at_m.append(jnp.where(even, inner, outer))
            at_h.append(jnp.where(lane8 == WIDTH - 1, k, pltpu.roll(c, WIDTH - 1, 1)))
            at_l.append(jnp.where(lane8 == 0, k, pltpu.roll(c, 1, 1)))
        five = [x + list(pressure(x[0], x[1], x[2], x[3])) for x in (at_c, at_p, at_m, at_h, at_l)]
        for level in range(2):
            c, p, m, h, l = [[x[2 * i + level] for i in range(5)] for x in five]
            if group == 0:
                new = stencil(c, h, l, p, m, high_o, low_o, None, None, cor)
            else:
                new = stencil(c, p, m, h, l, None, None, high_o, low_o, cor)
            for i in range(4):
                upd[group, 2 * i + level] = new[i]

    for step in range(2):
        parts = [(hx if step == 0 else upd)[1, q] for q in range(8)]
        parts += list(pressure(parts[0], parts[1], parts[2], parts[3]))
        parts += [jnp.zeros((WIDTH - 80, WIDTH), F32)]
        cols[step] = jnp.concatenate(parts, axis=0).T

    lane = lax.broadcasted_iota(I32, (EDGE, WIDTH), 1)
    y16 = lax.broadcasted_iota(I32, (EDGE, WIDTH), 0).astype(F32)
    at_lo, at_hi = sub16 == 0, sub16 == EDGE - 1

    def one_slot(slot, carry):
        oe = jnp.where(lane == WIDTH - 1, factor(slot, 19), 1.0)
        ow = jnp.where(lane == 0, factor(slot, 18), 1.0)
        on16 = jnp.where(at_hi, factor(slot, 17), 1.0)
        os16 = jnp.where(at_lo, factor(slot, 16), 1.0)
        base = factor(slot, 26) * float(WIDTH)
        alive = item(slot, 24) == 1
        for step in range(2):
            src = xa if step == 0 else xb
            halo = hx if step == 0 else upd
            for q in range(8):
                src[q, pl.ds(7, 1), :] = halo[0, q, pl.ds(slot * 2 + 1, 1), :]
                src[q, pl.ds(136, 1), :] = halo[0, q, pl.ds(slot * 2, 1), :]
            if step == 0:
                for q in range(8):
                    ref, k = (tr, q) if q < 4 else (ve, q - 4)
                    src[q, pl.ds(8, WIDTH), :] = ref[slot, k]
            for r in range(0, 144, 16):
                p0, p1 = pressure(*[src[q, pl.ds(r, 16), :] for q in range(4)])
                src[8, pl.ds(r, 16), :] = p0
                src[9, pl.ds(r, 16), :] = p1
            for r in range(0, WIDTH, EDGE):
                f = (base + (y16 + (r + 0.5))) * (2.0 / (ROWS * WIDTH))
                for level in range(2):
                    c, e, w, n, s = [], [], [], [], []
                    for i in range(5):
                        q = 2 * i + level
                        x = src[q, pl.ds(8 + r, EDGE), :]
                        edge = pltpu.roll(cols[step, pl.ds(r, EDGE), :], WIDTH - 1 - q * 8 - 2 * slot, 1)
                        c.append(x)
                        e.append(jnp.where(lane == WIDTH - 1, edge, pltpu.roll(x, WIDTH - 1, 1)))
                        w.append(jnp.where(lane == 0, edge, pltpu.roll(x, 1, 1)))
                        n.append(src[q, pl.ds(9 + r, EDGE), :])
                        s.append(src[q, pl.ds(7 + r, EDGE), :])
                    new = stencil(
                        c, e, w, n, s, oe, ow, on16 if r == WIDTH - EDGE else None, os16 if r == 0 else None, f
                    )
                    for i in range(4):
                        if step == 0:
                            xb[2 * i + level, pl.ds(8 + r, EDGE), :] = new[i]
                        else:
                            out = tr_out if i < 2 else ve_out
                            out[slot, 2 * (i % 2) + level, pl.ds(r, EDGE), :] = jnp.where(alive, new[i], 0.0)
        return carry

    for src in (xa, xb):
        for q in range(8):
            src[q, pl.ds(0, 8), :] = jnp.zeros((8, WIDTH), F32)
            src[q, pl.ds(136, 8), :] = jnp.zeros((8, WIDTH), F32)
    lax.fori_loop(0, 4, one_slot, 0)


def shape(*dims):
    return jax.ShapeDtypeStruct(dims, F32)


def table_shape(rows):
    return jax.ShapeDtypeStruct((rows, WIDTH), I32)


def exclusive_count(mask):
    i = jnp.arange(mask.shape[-1])
    return jnp.sum(mask[..., None, :] & (i[None, :] < i[:, None]), axis=-1).astype(I32)


def permute(x, pairs):
    return lax.ppermute(x, "blk", pairs)


def column_pairs(distance):
    return [(i, (i + 16 * distance * (1 if i % 2 == 0 else -1)) % DEVICES) for i in range(DEVICES)]


def exchange_z(x):
    groups = [[16 * a + 2 * z + c for z in range(8)] for a in range(16) for c in range(2)]
    return lax.all_to_all(x, "blk", 0, 0, axis_index_groups=groups, tiled=True)


def per_device(tracers, velocity, block_counts, land):
    tr = tracers.reshape(4, 4, WIDTH, WIDTH)
    ve = velocity.reshape(4, 4, WIDTH, WIDTH)
    swap = [(i, i ^ 1) for i in range(DEVICES)]

    rims, codes, mine, load = pl.pallas_call(
        start_kernel,
        out_shape=(shape(16 * EDGE, WIDTH), table_shape(64), table_shape(8), table_shape(8)),
        in_specs=[SM, VM, HB, HB],
        out_specs=(VM, VM, VM, VM),
        scratch_shapes=[
            pltpu.VMEM((32, WIDTH), I32),
            pltpu.VMEM((4, 4, WIDTH, WIDTH), F32),
            pltpu.VMEM((4, 4, WIDTH, WIDTH), F32),
            pltpu.VMEM((WIDTH, WIDTH), F32),
            pltpu.SemaphoreType.DMA((2,)),
        ],
        compiler_params=params(32),
        name="start",
    )(block_counts, land, tr, ve)
    other = permute(rims, swap)
    chip, message = pl.pallas_call(
        message_kernel,
        out_shape=(shape(32 * EDGE, WIDTH), shape(MSG, WIDTH)),
        in_specs=[SM, VM, VM],
        out_specs=(VM, VM),
        compiler_params=params(16),
        name="message",
    )(mine, rims, other)
    near = [permute(message, column_pairs(d)) for d in (1, 2, 3)]
    corners = message[MSG_EDGES * EDGE :]
    far = [permute(corners, column_pairs(d)) for d in (4, 5)]
    chunks = pl.pallas_call(
        pack_kernel,
        out_shape=shape(8 * CHUNK, WIDTH),
        in_specs=[SM] + [HB] * 6,
        out_specs=VM,
        scratch_shapes=[
            pltpu.VMEM((4 * MSG, WIDTH), F32),
            pltpu.VMEM((16, WIDTH), F32),
            pltpu.SMEM((8 * 32,), I32),
            pltpu.SemaphoreType.DMA((6,)),
        ],
        compiler_params=params(16),
        name="pack",
    )(codes, message, *near, *far)
    got = exchange_z(chunks.reshape(8, CHUNK, WIDTH)).reshape(8 * CHUNK, WIDTH)
    own, others = pl.pallas_call(
        sort_kernel,
        out_shape=(shape(SWAP, WIDTH), shape(SWAP, WIDTH)),
        in_specs=[SM, VM],
        out_specs=(VM, VM),
        scratch_shapes=[pltpu.SMEM((8,), I32), pltpu.SMEM((32,), I32)],
        compiler_params=params(16),
        name="sort",
    )(mine, got)

    def second(args):
        own, others, codes, mine, message, near = args
        down = (lax.axis_index("blk").astype(I32) & 1) == 1
        held = jnp.concatenate([message, *near])
        send = codes[:, :4].reshape(8, 32)
        rank = exclusive_count(send > 0)
        late = jnp.arange(CAP, CAP + MORE)
        picks = jnp.sum(jnp.where((send > 0)[:, None] & (rank[:, None] == late[None, :, None]), send[:, None] - 1, 0), axis=-1)
        rows = picks[:, :, None] * 8 + jnp.arange(EDGE, dtype=I32)
        more = exchange_z(held[rows].reshape(8, MORE * EDGE, WIDTH)).reshape(8 * MORE * EDGE, WIDTH)
        zed = mine[:, 4:8].reshape(32)
        i32 = jnp.arange(32)
        rank = jnp.sum((zed[None] >= 0) & (zed[None] == zed[:, None]) & (i32[None] < i32[:, None]), axis=1).astype(I32)
        late = (zed >= 0) & (rank >= CAP)
        start = jnp.where(late, zed * (MORE * EDGE) + (rank - CAP) * EDGE, 0)
        start, late = [jnp.where(down, jnp.concatenate([x[16:], x[:16]]), x) for x in (start, late)]
        new = more[start[:, None] + jnp.arange(EDGE, dtype=I32)]
        old = jnp.stack([own[: 16 * EDGE], others[: 16 * EDGE]]).reshape(32, EDGE, WIDTH)
        new = jnp.where(late[:, None, None], new, old).reshape(2, 16 * EDGE, WIDTH)
        return jnp.concatenate([new[0], own[16 * EDGE :]]), jnp.concatenate([new[1], others[16 * EDGE :]])

    own, others = lax.cond(
        load[0, 0] > CAP, second, lambda args: (args[0], args[1]), (own, others, codes, mine, message, near)
    )
    theirs = permute(others, swap)

    tr_new, ve_new = pl.pallas_call(
        steps_kernel,
        out_shape=(shape(4, 4, WIDTH, WIDTH), shape(4, 4, WIDTH, WIDTH)),
        in_specs=[SM] + [HB] * 3 + [VM] * 2,
        out_specs=(VM, VM),
        scratch_shapes=[
            pltpu.VMEM((32 * EDGE + 2 * SWAP + EDGE, WIDTH), F32),
            pltpu.VMEM((2, EDGE, 8, WIDTH), F32),
            pltpu.VMEM((2, 8, 8, WIDTH), F32),
            pltpu.VMEM((2, 8, 8, WIDTH), F32),
            pltpu.VMEM((2, 8, 8, WIDTH), F32),
            pltpu.VMEM((2, WIDTH, WIDTH), F32),
            pltpu.VMEM((10, 144, WIDTH), F32),
            pltpu.VMEM((10, 144, WIDTH), F32),
            pltpu.SemaphoreType.DMA((3,)),
        ],
        compiler_params=params(32),
        name="steps",
    )(mine, chip, own, theirs, tr, ve)
    return tr_new.reshape(tracers.shape), ve_new.reshape(velocity.shape)


def solution(mesh):
    spec = P("blk", None, None, None, None)
    return jax.shard_map(
        per_device,
        mesh=mesh,
        in_specs=(spec, spec, P(), P()),
        out_specs=(spec, spec),
        check_vma=False,
    )
```

time: 84.7 us -> 67.3 us (0.79)
  the two profiles are of different devices: /device:TPU:27 before, /device:TPU:1 now
where the time goes in v2:
time: 67.3 us; the launch traced here: 67 us
  waiting for transfers between devices  24.2 us (36%)
  starting transfers between devices  20 us (30%)
  Pallas kernels  17 us (25%)
  local copies, waits for them, and re-layouts  4.39 us (7%)
  between operations  1.31 us (2%)
    all_to_all x1, waiting for transfers between devices, exchange_z(): return lax.all_to_all(x, 'blk', 0, 0, axis_index_groups=groups, tiled=True)  15.4 us
    ppermute x7, starting transfers between devices, permute(): return lax.ppermute(x, 'blk', pairs)  13.3 us
    ppermute x7, waiting for transfers between devices, permute(): return lax.ppermute(x, 'blk', pairs)  8.82 us
    pallas_call x1, Pallas kernels, per_device(): pl.pallas_call(steps_kernel, out_shape=(shape(4, 4, WIDTH, WIDTH), shape(...  7.75 us
    all_to_all x1, starting transfers between devices, exchange_z(): return lax.all_to_all(x, 'blk', 0, 0, axis_index_groups=groups, tiled=True)  6.65 us
    unnamed x14, local copies, waits for them, and re-layouts  3.85 us
    pallas_call x1, Pallas kernels, per_device(): pl.pallas_call(start_kernel, out_shape=(shape(16 * EDGE, WIDTH), table_sh...  3.57 us
    pallas_call x1, Pallas kernels, per_device(): pl.pallas_call(pack_kernel, out_shape=shape(8 * CHUNK, WIDTH), in_specs=[...  3.38 us
  transfers between devices with their start and end apart: 8, of which 7 were waited for; matrix products, arithmetic and copies ran while one was open for 1% of the time, Pallas kernels for 0%

profile of v2, /device:TPU:1, one launch (start us, length us, event | category | flops | bytes accessed | tf_op | source)
XLA Modules:
  0.0 67.0 jit_solution(15251450110718037110)
XLA Ops:
  0.6 0.7 %copy-done.5 = s32[256]{0:T(256)S(1)} copy-done((s32[256]{0:T(256)S(1)}, s32[256]{0:T(256)}, u32[]{:S(2)}) %copy-start.5) | copy-done | bytes 1048
  1.3 1.2 %copy-done = f32[4,2,2,128,128]{4,3,2,1,0:T(8,128)S(1)} copy-done((f32[4,2,2,128,128]{4,3,2,1,0:T(8,128)S(1)}, f32[4,2,2,128,128]{4,3,2,1,0:T(8,128)}, u32[]{:S(2)}) %copy-start) | copy-done | bytes 1048600
  2.5 1.2 %copy-done.2 = f32[4,2,2,128,128]{4,3,2,1,0:T(8,128)S(1)} copy-done((f32[4,2,2,128,128]{4,3,2,1,0:T(8,128)S(1)}, f32[4,2,2,128,128]{4,3,2,1,0:T(8,128)}, u32[]{:S(2)}) %copy-start.2) | copy-done | bytes 1048600
  3.8 0.7 %copy-done.4 = s32[26,34]{1,0:T(8,128)S(1)} copy-done((s32[26,34]{1,0:T(8,128)S(1)}, s32[26,34]{1,0:T(8,128)}, u32[]{:S(2)}) %copy-start.4) | copy-done | bytes 3560
  4.5 3.6 %start.1 = (f32[256,128]{1,0:T(8,128)S(1)}, s32[64,128]{1,0:T(8,128)S(1)}, s32[8,128]{1,0:T(8,128)S(1)}, s32[8,128]{1,0:T(8,128)S(1)}) custom-call(s32[256]{0:T(256)S(1)} %copy-done.5, s32[26,34]{1,0:T(8,128)S(1)} %copy-done.4, f32[4,4,128,128]{3,2,1,0:T(8,128)S(1)} %bitcast.21, f32[4,4,128,128]{3,2,1,0:T(8,128)S(1)} %bitcast.23), custom_call_target="tpu_custom_call" | custom-call | tf_op jit(solution)/shard_map/start/pallas_call | solution.py:480
  8.1 3.3 %collective-permute-start = (f32[256,128]{1,0:T(8,128)S(1)}, f32[256,128]{1,0:T(8,128)S(1)}, u32[]{:S(2)}, u32[]{:S(2)}) collective-permute-start(f32[256,128]{1,0:T(8,128)S(1)} %get-tuple-element.43.mine), channel_id=1, source_target_pairs={{0,1},{1,0},{2,3},{3,2},{4,5},{5,4},{6,7},{7,6},{8,9},{9,8},{10,11... | collective-permute-start | bytes 393224 | tf_op jit(solution)/shard_map/ppermute | solution.py:463
  11.4 1.0 %collective-permute-done.other = f32[256,128]{1,0:T(8,128)S(1)} collective-permute-done((f32[256,128]{1,0:T(8,128)S(1)}, f32[256,128]{1,0:T(8,128)S(1)}, u32[]{:S(2)}, u32[]{:S(2)}) %collective-permute-start) | collective-permute-done | bytes 131104 | tf_op jit(solution)/shard_map/ppermute | solution.py:463
  12.4 0.7 %message.1 = (f32[512,128]{1,0:T(8,128)S(1)}, f32[296,128]{1,0:T(8,128)S(1)}) custom-call(s32[8,128]{1,0:T(8,128)S(1)} %get-tuple-element.42.table, f32[256,128]{1,0:T(8,128)S(1)} %get-tuple-element.43.mine, f32[256,128]{1,0:T(8,128)S(1)} %collective-permute-done.other), custom_call_target="tpu_custom_call" | custom-call | tf_op jit(solution)/shard_map/message/pallas_call | solution.py:496
  13.1 3.3 %collective-permute-start.1 = (f32[296,128]{1,0:T(8,128)S(1)}, f32[296,128]{1,0:T(8,128)S(1)}, u32[]{:S(2)}, u32[]{:S(2)}) collective-permute-start(f32[296,128]{1,0:T(8,128)S(1)} %get-tuple-element.47.m0), channel_id=1, source_target_pairs={{0,16},{1,241},{2,18},{3,243},{4,20},{5,245},{6,22},{7,247},{8,24}... | collective-permute-start | bytes 454664 | tf_op jit(solution)/shard_map/ppermute | solution.py:463
  16.4 0.4 collective-permute-start.2
  16.7 0.9 %collective-permute-start.3 = (f32[296,128]{1,0:T(8,128)S(1)}, f32[296,128]{1,0:T(8,128)S(1)}, u32[]{:S(2)}, u32[]{:S(2)}) collective-permute-start(f32[296,128]{1,0:T(8,128)S(1)} %get-tuple-element.47.m0), channel_id=1, source_target_pairs={{0,48},{1,209},{2,50},{3,211},{4,52},{5,213},{6,54},{7,215},{8,56}... | collective-permute-start | bytes 454664 | tf_op jit(solution)/shard_map/ppermute | solution.py:463
  17.9 2.0 %collective-permute-start.5 = (f32[8,128]{1,0:T(8,128)S(1)}, f32[8,128]{1,0:T(8,128)S(1)}, u32[]{:S(2)}, u32[]{:S(2)}) collective-permute-start(f32[8,128]{1,0:T(8,128)S(1)} %slice.45), channel_id=1, source_target_pairs={{0,80},{1,177},{2,82},{3,179},{4,84},{5,181},{6,86},{7,183},{8,88}... | collective-permute-start | bytes 12296 | tf_op jit(solution)/shard_map/ppermute | solution.py:463
  19.9 2.0 %collective-permute-done.4.c4 = f32[8,128]{1,0:T(8,128)S(1)} collective-permute-done((f32[8,128]{1,0:T(8,128)S(1)}, f32[8,128]{1,0:T(8,128)S(1)}, u32[]{:S(2)}, u32[]{:S(2)}) %collective-permute-start.4) | collective-permute-done | bytes 4128 | tf_op jit(solution)/shard_map/ppermute | solution.py:463
  21.9 1.0 %collective-permute-done.5.c5 = f32[8,128]{1,0:T(8,128)S(1)} collective-permute-done((f32[8,128]{1,0:T(8,128)S(1)}, f32[8,128]{1,0:T(8,128)S(1)}, u32[]{:S(2)}, u32[]{:S(2)}) %collective-permute-start.5) | collective-permute-done | bytes 4128 | tf_op jit(solution)/shard_map/ppermute | solution.py:463
  22.9 2.1 %collective-permute-done.2.m2 = f32[296,128]{1,0:T(8,128)S(1)} collective-permute-done((f32[296,128]{1,0:T(8,128)S(1)}, f32[296,128]{1,0:T(8,128)S(1)}, u32[]{:S(2)}, u32[]{:S(2)}) %collective-permute-start.2) | collective-permute-done | bytes 151584 | tf_op jit(solution)/shard_map/ppermute | solution.py:463
  25.0 1.5 %collective-permute-done.3.m3 = f32[296,128]{1,0:T(8,128)S(1)} collective-permute-done((f32[296,128]{1,0:T(8,128)S(1)}, f32[296,128]{1,0:T(8,128)S(1)}, u32[]{:S(2)}, u32[]{:S(2)}) %collective-permute-start.3) | collective-permute-done | bytes 151584 | tf_op jit(solution)/shard_map/ppermute | solution.py:463
  26.5 3.4 %pack.1 = f32[1152,128]{1,0:T(8,128)} custom-call(s32[64,128]{1,0:T(8,128)S(1)} %get-tuple-element.46.codes, f32[296,128]{1,0:T(8,128)S(1)} %get-tuple-element.47.m0, f32[296,128]{1,0:T(8,128)S(1)} %collective-permute-done.1.m1, f32[296,128]{1,0:T(8,128)S(1)} %collective-permute-done.2.m2, f32[296,128]{1,0:T(8,128)S(1)} %collective-permute-done.3.m3, ...), custom_call_target="tpu_custom_call" | custom-call | tf_op jit(solution)/shard_map/pack/pallas_call | solution.py:507
  29.9 6.7 %all-to-all-start.1 = ((f32[8,144,128]{2,1,0:T(8,128)}), f32[8,144,128]{2,1,0:T(8,128)S(1)}, u32[]{:S(2)}, u32[]{:S(2)}) async-start(f32[8,144,128]{2,1,0:T(8,128)} %bitcast.11), calls=%async_computation.1 | async-start | bytes 1179648 | tf_op jit(solution)/shard_map/all_to_all | solution.py:472
  36.6 0.5 slice.44
  37.7 15.4 %all-to-all-done.1 = f32[8,144,128]{2,1,0:T(8,128)S(1)} async-done(((f32[8,144,128]{2,1,0:T(8,128)}), f32[8,144,128]{2,1,0:T(8,128)S(1)}, u32[]{:S(2)}, u32[]{:S(2)}) %all-to-all-start.1) | async-done | bytes 589856 | tf_op jit(solution)/shard_map/all_to_all | solution.py:472
  53.2 1.6 %sort.1 = (f32[264,128]{1,0:T(8,128)}, f32[264,128]{1,0:T(8,128)}) custom-call(s32[8,128]{1,0:T(8,128)S(1)} %get-tuple-element.42.table, f32[1152,128]{1,0:T(8,128)S(1)} %bitcast.25), custom_call_target="tpu_custom_call" | custom-call | tf_op jit(solution)/shard_map/sort/pallas_call | solution.py:522
  54.8 3.2 %collective-permute-start.6 = (f32[264,128]{1,0:T(8,128)}, f32[264,128]{1,0:T(8,128)S(1)}, u32[]{:S(2)}, u32[]{:S(2)}) collective-permute-start(f32[264,128]{1,0:T(8,128)} %get-tuple-element.51), channel_id=1, source_target_pairs={{0,1},{1,0},{2,3},{3,2},{4,5},{5,4},{6,7},{7,6},{8,9},{9,8},{10,11... | collective-permute-start | bytes 405512 | tf_op jit(solution)/shard_map/ppermute | solution.py:463
  58.0 1.2 %collective-permute-done.6.other = f32[264,128]{1,0:T(8,128)S(1)} collective-permute-done((f32[264,128]{1,0:T(8,128)}, f32[264,128]{1,0:T(8,128)S(1)}, u32[]{:S(2)}, u32[]{:S(2)}) %collective-permute-start.6) | collective-permute-done | bytes 135200 | tf_op jit(solution)/shard_map/ppermute | solution.py:463
  59.2 7.7 %steps.1 = (f32[4,4,128,128]{3,2,1,0:T(8,128)}, f32[4,4,128,128]{3,2,1,0:T(8,128)}) custom-call(s32[8,128]{1,0:T(8,128)S(1)} %get-tuple-element.42.table, f32[512,128]{1,0:T(8,128)S(1)} %get-tuple-element.44.chip, f32[264,128]{1,0:T(8,128)} %get-tuple-element.50.own, f32[264,128]{1,0:T(8,128)S(1)} %collective-permute-done.6.other, ...), custom_call_target="tpu_custom_call" | custom-call | tf_op jit(solution)/shard_map/steps/pallas_call | solution.py:558
  (14 shorter events, 0.3 us)
Async XLA Ops:
  0.6 0.7 %copy-start.5 = (s32[256]{0:T(256)S(1)}, s32[256]{0:T(256)}, u32[]{:S(2)}) copy-start(s32[256]{0:T(256)} %counts.1) | copy-start | bytes 3076
  1.3 1.2 %copy-start = (f32[4,2,2,128,128]{4,3,2,1,0:T(8,128)S(1)}, f32[4,2,2,128,128]{4,3,2,1,0:T(8,128)}, u32[]{:S(2)}) copy-start(f32[4,2,2,128,128]{4,3,2,1,0:T(8,128)} %param.6) | copy-start | bytes 3145732
  2.5 1.2 %copy-start.2 = (f32[4,2,2,128,128]{4,3,2,1,0:T(8,128)S(1)}, f32[4,2,2,128,128]{4,3,2,1,0:T(8,128)}, u32[]{:S(2)}) copy-start(f32[4,2,2,128,128]{4,3,2,1,0:T(8,128)} %param.7) | copy-start | bytes 3145732
  3.8 0.7 %copy-start.4 = (s32[26,34]{1,0:T(8,128)S(1)}, s32[26,34]{1,0:T(8,128)}, u32[]{:S(2)}) copy-start(s32[26,34]{1,0:T(8,128)} %land.1) | copy-start | bytes 10612
  8.1 4.3 %collective-permute-start = (f32[256,128]{1,0:T(8,128)S(1)}, f32[256,128]{1,0:T(8,128)S(1)}, u32[]{:S(2)}, u32[]{:S(2)}) collective-permute-start(f32[256,128]{1,0:T(8,128)S(1)} %get-tuple-element.43.mine), channel_id=1, source_target_pairs={{0,1},{1,0},{2,3},{3,2},{4,5},{5,4},{6,7},{7,6},{8,9},{9,8},{10,11... | collective-permute-start | bytes 393224 | tf_op jit(solution)/shard_map/ppermute | solution.py:463
  13.1 9.8 %collective-permute-start.1 = (f32[296,128]{1,0:T(8,128)S(1)}, f32[296,128]{1,0:T(8,128)S(1)}, u32[]{:S(2)}, u32[]{:S(2)}) collective-permute-start(f32[296,128]{1,0:T(8,128)S(1)} %get-tuple-element.47.m0), channel_id=1, source_target_pairs={{0,16},{1,241},{2,18},{3,243},{4,20},{5,245},{6,22},{7,247},{8,24}... | collective-permute-start | bytes 454664 | tf_op jit(solution)/shard_map/ppermute | solution.py:463
  16.4 8.6 %collective-permute-start.2 = (f32[296,128]{1,0:T(8,128)S(1)}, f32[296,128]{1,0:T(8,128)S(1)}, u32[]{:S(2)}, u32[]{:S(2)}) collective-permute-start(f32[296,128]{1,0:T(8,128)S(1)} %get-tuple-element.47.m0), channel_id=1, source_target_pairs={{0,32},{1,225},{2,34},{3,227},{4,36},{5,229},{6,38},{7,231},{8,40}... | collective-permute-start | bytes 454664 | tf_op jit(solution)/shard_map/ppermute | solution.py:463
  16.7 9.8 %collective-permute-start.3 = (f32[296,128]{1,0:T(8,128)S(1)}, f32[296,128]{1,0:T(8,128)S(1)}, u32[]{:S(2)}, u32[]{:S(2)}) collective-permute-start(f32[296,128]{1,0:T(8,128)S(1)} %get-tuple-element.47.m0), channel_id=1, source_target_pairs={{0,48},{1,209},{2,50},{3,211},{4,52},{5,213},{6,54},{7,215},{8,56}... | collective-permute-start | bytes 454664 | tf_op jit(solution)/shard_map/ppermute | solution.py:463
  17.7 4.2 %collective-permute-start.4 = (f32[8,128]{1,0:T(8,128)S(1)}, f32[8,128]{1,0:T(8,128)S(1)}, u32[]{:S(2)}, u32[]{:S(2)}) collective-permute-start(f32[8,128]{1,0:T(8,128)S(1)} %slice.45), channel_id=1, source_target_pairs={{0,64},{1,193},{2,66},{3,195},{4,68},{5,197},{6,70},{7,199},{8,72}... | collective-permute-start | bytes 12296 | tf_op jit(solution)/shard_map/ppermute | solution.py:463
  17.9 4.9 %collective-permute-start.5 = (f32[8,128]{1,0:T(8,128)S(1)}, f32[8,128]{1,0:T(8,128)S(1)}, u32[]{:S(2)}, u32[]{:S(2)}) collective-permute-start(f32[8,128]{1,0:T(8,128)S(1)} %slice.45), channel_id=1, source_target_pairs={{0,80},{1,177},{2,82},{3,179},{4,84},{5,181},{6,86},{7,183},{8,88}... | collective-permute-start | bytes 12296 | tf_op jit(solution)/shard_map/ppermute | solution.py:463
  26.5 3.4 %copy-start.6 = (f32[296,128]{1,0:T(8,128)}, f32[296,128]{1,0:T(8,128)S(1)}, u32[]{:S(2)}) copy-start(f32[296,128]{1,0:T(8,128)S(1)} %collective-permute-done.3.m3) | copy-start | bytes 454660
  29.9 23.3 %all-to-all-start.1 = ((f32[8,144,128]{2,1,0:T(8,128)}), f32[8,144,128]{2,1,0:T(8,128)S(1)}, u32[]{:S(2)}, u32[]{:S(2)}) async-start(f32[8,144,128]{2,1,0:T(8,128)} %bitcast.11), calls=%async_computation.1 | async-start | bytes 1179648 | tf_op jit(solution)/shard_map/all_to_all | solution.py:472
  54.8 4.5 %copy-start.1 = (f32[4,2,2,128,128]{4,3,2,1,0:T(8,128)S(1)}, f32[4,2,2,128,128]{4,3,2,1,0:T(8,128)}, u32[]{:S(2)}) copy-start(f32[4,2,2,128,128]{4,3,2,1,0:T(8,128)} %param.6) | copy-start | bytes 3145732
  54.8 4.5 %copy-start.3 = (f32[4,2,2,128,128]{4,3,2,1,0:T(8,128)S(1)}, f32[4,2,2,128,128]{4,3,2,1,0:T(8,128)}, u32[]{:S(2)}) copy-start(f32[4,2,2,128,128]{4,3,2,1,0:T(8,128)} %param.7) | copy-start | bytes 3145732
  54.8 4.5 %collective-permute-start.6 = (f32[264,128]{1,0:T(8,128)}, f32[264,128]{1,0:T(8,128)S(1)}, u32[]{:S(2)}, u32[]{:S(2)}) collective-permute-start(f32[264,128]{1,0:T(8,128)} %get-tuple-element.51), channel_id=1, source_target_pairs={{0,1},{1,0},{2,3},{3,2},{4,5},{5,4},{6,7},{7,6},{8,9},{9,8},{10,11... | collective-permute-start | bytes 405512 | tf_op jit(solution)/shard_map/ppermute | solution.py:463

commit v3 on v2

--- a/solution.py
+++ b/solution.py
@@ -8,8 +8,8 @@
 DEVICES = 256
 ROWS, COLS = 26, 34
 WIDTH = 128
-CAP = 8
-MORE = 10
+CAP = 7
+MORE = 11
 EDGE = 16
 MSG_EDGES = 18
 MSG = MSG_EDGES * EDGE + 8
@@ -43,7 +43,7 @@
     return jnp.dot(a.astype(jnp.bfloat16), b.astype(jnp.bfloat16), preferred_element_type=F32)
 
 
-def build_tables(me, counts, land, board, codes, mine, load):
+def build_tables(me, counts, land, board, codes, mine, picks, load):
     column, zed, core = me >> 4, (me >> 1) & 7, me & 1
     board[...] = jnp.ones((32, WIDTH), I32)
     board[pl.ds(0, ROWS), pl.ds(0, COLS)] = land[...]
@@ -148,7 +148,20 @@
             at = z * (CHUNK // 8) + CAP * EDGE // 8 + jnp.right_shift(delta, 2)
             items[8 + k] = jnp.where(flow, at * WIDTH + 32 * (delta & 3) + lane_at, -1)
     items[24], items[25], items[26], items[27] = live.astype(I32), top.astype(I32), block_row, block_col
-    lane64 = lane_iota(64)
+    sends = [items[k] > 0 for k in range(4)]
+    lane64, slot64 = lane_iota(64), row_iota(64)
+    masks = jnp.zeros((64, WIDTH), F32)
+    for k in range(4):
+        masks = jnp.where((lane64 == k) & sends[k], 1.0, masks)
+    si, sj = lax.broadcasted_iota(I32, (64, 64), 0), lax.broadcasted_iota(I32, (64, 64), 1)
+    before = exact_dot((sj < si) & (jnp.right_shift(si, 3) == jnp.right_shift(sj, 3)), masks)
+    rank = jnp.sum(before, axis=1, keepdims=True).astype(I32)
+    placed = jnp.zeros((64, WIDTH), F32)
+    for k in range(4):
+        placed = jnp.where(sends[k] & (lane64 == rank), items[k].astype(F32), placed)
+        rank = rank + sends[k].astype(I32)
+    zi, zj = lax.broadcasted_iota(I32, (8, 64), 0), lax.broadcasted_iota(I32, (8, 64), 1)
+    picks[...] = exact_dot(jnp.right_shift(zj, 3) == zi, placed).astype(I32)
     table = jnp.zeros((64, WIDTH), I32)
     for k in range(CODES):
         table = jnp.where(lane64 == k, items[k], table)
@@ -156,11 +169,11 @@
     mine[...] = codes[pl.ds(pl.multiple_of(zed * 8, 8), 8), :]
 
 
-def start_kernel(counts, land, tr_hbm, ve_hbm, out, codes, mine, load, board, tr, ve, turned, sem):
+def start_kernel(counts, land, tr_hbm, ve_hbm, out, codes, mine, picks, load, board, tr, ve, turned, sem):
     copies = [pltpu.make_async_copy(tr_hbm, tr, sem.at[0]), pltpu.make_async_copy(ve_hbm, ve, sem.at[1])]
     for copy in copies:
         copy.start()
-    build_tables(lax.axis_index("blk").astype(I32), counts, land, board, codes, mine, load)
+    build_tables(lax.axis_index("blk").astype(I32), counts, land, board, codes, mine, picks, load)
     for copy in copies:
         copy.wait()
     lane = lane_iota(WIDTH) // 4
@@ -180,7 +193,9 @@
             out[pl.ds((slot * 4 + side) * EDGE + depth * 8, 8), :] = turned[pl.ds(slot * 32 + j, 8, stride=4), :]
 
 
-def message_kernel(table, mine, other, chip, out):
+def message_kernel(table_hbm, mine, other, chip, out, table, sem):
+    fetch = pltpu.make_async_copy(table_hbm, table, sem.at[0])
+    fetch.start()
     core = lax.axis_index("blk").astype(I32) & 1
     flag = core == 0
     for t in range(4):
@@ -189,6 +204,18 @@
             a, b = mine[pl.ds(at, EDGE), :], other[pl.ds(at, EDGE), :]
             chip[pl.ds(at, EDGE), :] = jnp.where(flag, a, b)
             chip[pl.ds(16 * EDGE + at, EDGE), :] = jnp.where(flag, b, a)
+    for t in range(8):
+        at = pl.multiple_of(jnp.where(flag, t * 4 + 1, t * 4) * EDGE, EDGE)
+        out[pl.ds(t * EDGE, EDGE), :] = chip[pl.ds(at, EDGE), :]
+        out[pl.ds((10 + t) * EDGE, EDGE), :] = chip[pl.ds((t * 4 + 1) * EDGE, EDGE), :]
+    lane = lax.broadcasted_iota(I32, (8, WIDTH), 1) // 2
+    corners = jnp.zeros((8, WIDTH), F32)
+    for t in range(8):
+        for side, base in ((1, 0), (0, 8)):
+            x = chip[pl.ds((t * 4 + side) * EDGE, 8), :]
+            corners = jnp.where(lane == base + t, pltpu.roll(x, 2 * (base + t) + 1, 1), corners)
+    out[pl.ds(MSG_EDGES * EDGE, 8), :] = corners
+    fetch.wait()
     last, first_col, last_col = jnp.int32(0), jnp.int32(0), jnp.int32(0)
     for t in range(8):
         live, col = table[t, 24] == 1, table[t, 27]
@@ -196,56 +223,62 @@
         first_col = jnp.where(live & (col == 0), t, first_col)
         live, col = table[7 - t, 24] == 1, table[7 - t, 27]
         last_col = jnp.where(live & (col == COLS - 1), 7 - t, last_col)
-    for t in range(8):
-        at = pl.multiple_of(jnp.where(flag, t * 4 + 1, t * 4) * EDGE, EDGE)
-        out[pl.ds(t * EDGE, EDGE), :] = chip[pl.ds(at, EDGE), :]
-        out[pl.ds((10 + t) * EDGE, EDGE), :] = chip[pl.ds((t * 4 + 1) * EDGE, EDGE), :]
     for e, edge in ((8, jnp.where(flag, last * 4 + 3, 2)), (9, jnp.where(flag, first_col * 4 + 2, last_col * 4 + 3))):
         at = pl.multiple_of(edge * EDGE, EDGE)
         out[pl.ds(e * EDGE, EDGE), :] = chip[pl.ds(at, EDGE), :]
-    lane = lax.broadcasted_iota(I32, (8, WIDTH), 1) // 2
-    corners = jnp.zeros((8, WIDTH), F32)
-    for t in range(8):
-        for side, base in ((1, 0), (0, 8)):
-            x = chip[pl.ds((t * 4 + side) * EDGE, 8), :]
-            corners = jnp.where(lane == base + t, pltpu.roll(x, 2 * (base + t) + 1, 1), corners)
-    out[pl.ds(MSG_EDGES * EDGE, 8), :] = corners
-
-
-def pack_kernel(codes, m0, m1, m2, m3, c4, c5, out, held, far, table, sem):
-    copies = [pltpu.make_async_copy(m, held.at[pl.ds(i * MSG, MSG)], sem.at[i]) for i, m in enumerate((m0, m1, m2, m3))]
-    copies += [pltpu.make_async_copy(m, far.at[pl.ds(i * 8, 8)], sem.at[4 + i]) for i, m in enumerate((c4, c5))]
+
+
+def pack_kernel(picks_hbm, m0, m1, m2, m3, c4, c5, out, picks, held, packed, sem, sent):
+    messages = (m0, m1, m2, m3)
+    fetch = pltpu.make_async_copy(picks_hbm, picks, sem.at[14])
+    fetch.start()
+    copies = [
+        pltpu.make_async_copy(m.at[pl.ds(MSG_EDGES * EDGE, 8)] if i < 4 else m, held.at[pl.ds(i * 8, 8)], sem.at[i])
+        for i, m in enumerate((*messages, c4, c5))
+    ]
     for copy in copies:
         copy.start()
-    for z in range(8):
-        for r in range(CAP):
-            table[z * 32 + r] = 0
-        count = jnp.int32(0)
-        for t in range(8):
-            for side in range(4):
-                code = codes[z * 8 + t, side]
-                table[z * 32 + count] = code
-                count += (code > 0).astype(I32)
+
+    def edges(wait):
+        for z in range(8):
+            for r in range(CAP):
+                code = picks[z, r]
+                for k, m in enumerate(messages):
+
+                    @pl.when((code > k * (MSG // 8)) & (code <= (k + 1) * (MSG // 8)))
+                    def _():
+                        row = pl.multiple_of((code - 1 - k * (MSG // 8)) * 8, EDGE)
+                        to = out.at[pl.ds(z * CHUNK + r * EDGE, EDGE)]
+                        copy = pltpu.make_async_copy(m.at[pl.ds(row, EDGE)], to, sent.at[0])
+                        copy.wait() if wait else copy.start()
+
+    fetch.wait()
+    edges(False)
     for copy in copies:
         copy.wait()
-    lane = lax.broadcasted_iota(I32, (8, WIDTH), 1) // 32
-    near_c = jnp.zeros((8, WIDTH), F32)
-    for i in range(4):
-        x = held[pl.ds(i * MSG + MSG_EDGES * EDGE, 8), :]
-        near_c = jnp.where(lane == i, pltpu.roll(x, 32 * i, 1) if i else x, near_c)
-    far_c = jnp.where(lane == 0, far[pl.ds(0, 8), :], pltpu.roll(far[pl.ds(8, 8), :], 32, 1))
-    for z in range(8):
-        for r in range(CAP):
-            at = pl.multiple_of(jnp.maximum(table[z * 32 + r] - 1, 0) * 8, 8)
-            out[pl.ds(z * CHUNK + r * EDGE, EDGE), :] = held[pl.ds(at, EDGE), :]
-        out[pl.ds(z * CHUNK + CAP * EDGE, 8), :] = near_c
-        out[pl.ds(z * CHUNK + CAP * EDGE + 8, 8), :] = far_c
-
-
-def sort_kernel(table, got, own, other, taken, rows):
+    lane = lane_iota(8) // 32
+    near_c = held[pl.ds(0, 8), :]
+    for i in range(1, 4):
+        near_c = jnp.where(lane == i, pltpu.roll(held[pl.ds(i * 8, 8), :], 32 * i, 1), near_c)
+    packed[pl.ds(0, 8), :] = near_c
+    packed[pl.ds(8, 8), :] = jnp.where(lane == 0, held[pl.ds(32, 8), :], pltpu.roll(held[pl.ds(40, 8), :], 32, 1))
+    copies = [
+        pltpu.make_async_copy(packed, out.at[pl.ds(z * CHUNK + CAP * EDGE, 16)], sem.at[6 + z]) for z in range(8)
+    ]
+    for copy in copies:
+        copy.start()
+    edges(True)
+    for copy in copies:
+        copy.wait()
+
+
+def sort_kernel(table_hbm, got, own, other, table, taken, rows, sem):
+    fetch = pltpu.make_async_copy(table_hbm, table, sem.at[0])
+    fetch.start()
     core = lax.axis_index("blk").astype(I32) & 1
     for z in range(8):
         taken[z] = 0
+    fetch.wait()
     for t in range(8):
         for side in range(4):
             code = table[t, 4 + side]
@@ -258,7 +291,7 @@
         first = (core ^ half) * 4
         corners = jnp.zeros((8, WIDTH), F32)
         for e in range(16):
-            at = pl.multiple_of(rows[first * 4 + e], 8)
+            at = pl.multiple_of(rows[first * 4 + e], EDGE)
             out[pl.ds(e * EDGE, EDGE), :] = got[pl.ds(at, EDGE), :]
             code = table[first + e // 4, 12 + e % 4]
             turn = (e - code) & (WIDTH - 1)
@@ -295,7 +328,78 @@
     return out
 
 
-def steps_kernel(table, chip, own, other, tr, ve, tr_out, ve_out, held, hx, inn, crv, upd, cols, xa, xb, sem):
+def inner_kernel(table, tr, ve, tr_out, ve_out, rims, xa, xb, gathered):
+    core = lax.axis_index("blk").astype(I32) & 1
+    y16 = lax.broadcasted_iota(I32, (EDGE, WIDTH), 0).astype(F32)
+    lane = lane_iota(WIDTH)
+    for src in (xa, xb):
+        for q in range(10):
+            src[q, pl.ds(0, 8), :] = jnp.zeros((8, WIDTH), F32)
+            src[q, pl.ds(136, 8), :] = jnp.zeros((8, WIDTH), F32)
+
+    def one_slot(slot, carry):
+        base = table[core * 4 + slot, 26].astype(F32) * float(WIDTH)
+        alive = table[core * 4 + slot, 24] == 1
+        for q in range(8):
+            ref, k = (tr, q) if q < 4 else (ve, q - 4)
+            xa[q, pl.ds(8, WIDTH), :] = ref[slot, k]
+        for step, src in enumerate((xa, xb)):
+            for r in range(8, 8 + WIDTH, EDGE):
+                p0, p1 = pressure(*[src[q, pl.ds(r, EDGE), :] for q in range(4)])
+                src[8, pl.ds(r, EDGE), :] = p0
+                src[9, pl.ds(r, EDGE), :] = p1
+            for r in range(0, WIDTH, EDGE):
+                f = (base + (y16 + (r + 0.5))) * (2.0 / (ROWS * WIDTH))
+                for level in range(2):
+                    c, e, w, n, s = [], [], [], [], []
+                    for i in range(5):
+                        q = 2 * i + level
+                        x = src[q, pl.ds(8 + r, EDGE), :]
+                        c.append(x)
+                        e.append(pltpu.roll(x, WIDTH - 1, 1))
+                        w.append(pltpu.roll(x, 1, 1))
+                        n.append(src[q, pl.ds(9 + r, EDGE), :])
+                        s.append(src[q, pl.ds(7 + r, EDGE), :])
+                    new = stencil(c, e, w, n, s, None, None, None, None, f)
+                    for i in range(4):
+                        if step == 0:
+                            xb[2 * i + level, pl.ds(8 + r, EDGE), :] = new[i]
+                        else:
+                            out = tr_out if i < 2 else ve_out
+                            out[slot, 2 * (i % 2) + level, pl.ds(r, EDGE), :] = jnp.where(alive, new[i], 0.0)
+        for q in range(8):
+            at = pl.multiple_of(slot * 4 * EDGE, EDGE)
+            for ring in range(2):
+                rims[pl.ds(at + ring * 8 + q, 1), :] = xb[q, pl.ds(8 + 1 + ring, 1), :]
+                rims[pl.ds(at + EDGE + ring * 8 + q, 1), :] = xb[q, pl.ds(8 + 126 - ring, 1), :]
+            tile = slot * 8 + q
+            x = xb[q, pl.ds(8, WIDTH), :]
+            a, b = pltpu.roll(x, (tile * 4 + 3) & (WIDTH - 1), 1), pltpu.roll(x, (tile * 4 + 1) & (WIDTH - 1), 1)
+            mine = jnp.right_shift(lane, 2) == tile
+            gathered[...] = jnp.where(mine, jnp.where((lane & 3) < 2, a, b), gathered[...])
+        return carry
+
+    gathered[...] = jnp.zeros((WIDTH, WIDTH), F32)
+    lax.fori_loop(0, 4, one_slot, 0)
+    gathered[...] = gathered[...].T
+    for slot in range(4):
+        for j, (side, ring) in enumerate([(3, 1), (3, 0), (2, 0), (2, 1)]):
+            rims[pl.ds((slot * 4 + side) * EDGE + ring * 8, 8), :] = gathered[pl.ds(slot * 32 + j, 8, stride=4), :]
+
+
+def lateral(x, ring):
+    even = (row_iota(8) & 1) == 0
+    up, down = pltpu.roll(x, 7, 0), pltpu.roll(x, 1, 0)
+    back = pltpu.roll(x, WIDTH - ring, 1) if ring else x
+    ahead = pltpu.roll(x, ring, 1) if ring else x
+    low = jnp.where(even, pltpu.roll(up, ring + 1, 1), back)
+    high = jnp.where(even, ahead, pltpu.roll(down, WIDTH - 1 - ring, 1))
+    return low, high
+
+
+def final_kernel(
+    table, chip, own, other, edges, rims, tr, ve, tr_out, ve_out, held, hx, inn, mid, crv, upd, first, r0, r1, turned, res_t, res_v, sem, sent
+):
     sizes = (8 * 4 * EDGE, SWAP, SWAP)
     starts = (0, sizes[0], sizes[0] + SWAP)
     copies = [
@@ -304,40 +408,40 @@
     for copy in copies:
         copy.start()
     held[pl.ds(starts[2] + SWAP, EDGE), :] = jnp.zeros((EDGE, WIDTH), F32)
+    core = lax.axis_index("blk").astype(I32) & 1
+
+    def item(slot, k):
+        return table[core * 4 + slot, k]
+
+    def factor(slot, k):
+        return item(slot, k).astype(F32)
+
+    i0, i1 = row_iota(WIDTH), lane_iota(WIDTH)
+    mirror = (i0 + i1 == WIDTH - 1).astype(F32)
+    sign = jnp.where((row_iota(EDGE) & 7) >= 4, -1.0, 1.0)
+    lane8, sub8 = lane_iota(8), row_iota(8)
+    even = (sub8 & 1) == 0
+    sign8 = jnp.where(sub8 >= 4, -1.0, 1.0)
+    where_to = ((0, 1), (0, 0), (1, 1), (1, 0))
+
+    for slot in range(4):
+        for side in range(4):
+            group, odd = where_to[side]
+            at = (slot * 4 + side) * EDGE
+            inn[group, :, slot * 2 + odd, :] = edges[pl.ds(at, EDGE), :]
+            mid[group, :, slot * 2 + odd, :] = rims[pl.ds(at, EDGE), :]
     for copy in copies:
         copy.wait()
-    core = lax.axis_index("blk").astype(I32) & 1
-
-    def item(slot, k):
-        return table[core * 4 + slot, k]
-
-    def factor(slot, k):
-        return item(slot, k).astype(F32)
-
-    i0 = lax.broadcasted_iota(I32, (WIDTH, WIDTH), 0)
-    i1 = lax.broadcasted_iota(I32, (WIDTH, WIDTH), 1)
-    mirror = (i0 + i1 == WIDTH - 1).astype(F32)
-    sub16 = lax.broadcasted_iota(I32, (EDGE, WIDTH), 0)
-    sign = jnp.where((sub16 & 7) >= 4, -1.0, 1.0)
-    lane8 = lax.broadcasted_iota(I32, (8, WIDTH), 1)
-    sub8 = lax.broadcasted_iota(I32, (8, WIDTH), 0)
-    even = (sub8 & 1) == 0
     corners = held[pl.ds(starts[1] + 16 * EDGE, 8), :] + held[pl.ds(starts[2] + 16 * EDGE, 8), :]
-    sign8 = jnp.where(sub8 >= 4, -1.0, 1.0)
-
     for slot in range(4):
         top = item(slot, 25) == 1
         for side in range(4):
-            at = pl.multiple_of(item(slot, 8 + side) * 8, 8)
-            x = held[pl.ds(at, EDGE), :]
+            group, odd = where_to[side]
+            x = held[pl.ds(pl.multiple_of(item(slot, 8 + side) * 8, 8), EDGE), :]
             if side == 1:
                 flipped = jnp.dot(x, mirror, preferred_element_type=F32, precision=lax.Precision.HIGHEST) * sign
                 x = jnp.where(top, flipped, x)
-            group, row = (0, 1) if side == 0 else (0, 0) if side == 1 else (1, 1) if side == 2 else (1, 0)
-            row += slot * 2
-            hx[group, :, row, :] = x
-            inner = held[pl.ds(pl.multiple_of(core * (16 * EDGE) + (slot * 4 + side) * EDGE, 8), 8), :]
-            inn[group, :, row, :] = inner
+            hx[group, :, slot * 2 + odd, :] = x
         for group, odd, lo, hi in ((0, 0, 2, 3), (0, 1, 0, 1), (1, 0, 1, 3), (1, 1, 0, 2)):
             vals = []
             for which, lane in ((lo, 0), (hi, WIDTH - 1)):
@@ -347,103 +451,155 @@
                 vals.append(v)
             crv[group, :, slot * 2 + odd, :] = jnp.where(lane8 == 0, vals[0], vals[1])
 
-    for group in range(2):
-        low_o, high_o, cor = jnp.ones((8, WIDTH), F32), jnp.ones((8, WIDTH), F32), jnp.zeros((8, WIDTH), F32)
-        for slot in range(4):
-            first = factor(slot, 26) * float(WIDTH)
-            for odd in range(2):
-                lo, hi = ((22, 23), (20, 21))[odd] if group == 0 else ((21, 23), (20, 22))[odd]
-                here = sub8 == slot * 2 + odd
-                low_o = jnp.where(here & (lane8 == 0), factor(slot, lo), low_o)
-                high_o = jnp.where(here & (lane8 == WIDTH - 1), factor(slot, hi), high_o)
-                if group == 1:
-                    y = first
-                elif odd:
-                    y = first - 1.0
-                else:
-                    y = first + jnp.where(item(slot, 25) == 1, WIDTH - 1.0, float(WIDTH))
-                cor = jnp.where(here, y, cor)
-        if group == 1:
-            cor = cor + lane8.astype(F32)
-        cor = (cor + 0.5) * (2.0 / (ROWS * WIDTH))
+    def strip(group, c, outer, inner, low, high, o_out, o_low, o_high, cor, out):
         at_c, at_p, at_m, at_h, at_l = [], [], [], [], []
         for q in range(8):
-            c, outer, inner, k = hx[group, q], hx[group, 8 + q], inn[group, q], crv[group, q]
-            at_c.append(c)
-            at_p.append(jnp.where(even, outer, inner))
-            at_m.append(jnp.where(even, inner, outer))
-            at_h.append(jnp.where(lane8 == WIDTH - 1, k, pltpu.roll(c, WIDTH - 1, 1)))
-            at_l.append(jnp.where(lane8 == 0, k, pltpu.roll(c, 1, 1)))
+            x = c(q)
+            at_c.append(x)
+            at_p.append(jnp.where(even, outer(q), inner(q)))
+            at_m.append(jnp.where(even, inner(q), outer(q)))
+            lo, hi = low(q), high(q)
+            at_h.append(jnp.where(lane8 == WIDTH - 1, hi, pltpu.roll(x, WIDTH - 1, 1)))
+            at_l.append(jnp.where(lane8 == 0, lo, pltpu.roll(x, 1, 1)))
         five = [x + list(pressure(x[0], x[1], x[2], x[3])) for x in (at_c, at_p, at_m, at_h, at_l)]
+        o_pos = None if o_out is None else jnp.where(even, o_out, 1.0)
+        o_neg = None if o_out is None else jnp.where(even, 1.0, o_out)
         for level in range(2):
             c, p, m, h, l = [[x[2 * i + level] for i in range(5)] for x in five]
             if group == 0:
-                new = stencil(c, h, l, p, m, high_o, low_o, None, None, cor)
+                new = stencil(c, h, l, p, m, o_high, o_low, o_pos, o_neg, cor)
             else:
-                new = stencil(c, p, m, h, l, None, None, high_o, low_o, cor)
+                new = stencil(c, p, m, h, l, o_pos, o_neg, o_high, o_low, cor)
             for i in range(4):
-                upd[group, 2 * i + level] = new[i]
-
-    for step in range(2):
-        parts = [(hx if step == 0 else upd)[1, q] for q in range(8)]
-        parts += list(pressure(parts[0], parts[1], parts[2], parts[3]))
-        parts += [jnp.zeros((WIDTH - 80, WIDTH), F32)]
-        cols[step] = jnp.concatenate(parts, axis=0).T
-
-    lane = lax.broadcasted_iota(I32, (EDGE, WIDTH), 1)
-    y16 = lax.broadcasted_iota(I32, (EDGE, WIDTH), 0).astype(F32)
-    at_lo, at_hi = sub16 == 0, sub16 == EDGE - 1
-
-    def one_slot(slot, carry):
-        oe = jnp.where(lane == WIDTH - 1, factor(slot, 19), 1.0)
-        ow = jnp.where(lane == 0, factor(slot, 18), 1.0)
-        on16 = jnp.where(at_hi, factor(slot, 17), 1.0)
-        os16 = jnp.where(at_lo, factor(slot, 16), 1.0)
-        base = factor(slot, 26) * float(WIDTH)
-        alive = item(slot, 24) == 1
-        for step in range(2):
-            src = xa if step == 0 else xb
-            halo = hx if step == 0 else upd
-            for q in range(8):
-                src[q, pl.ds(7, 1), :] = halo[0, q, pl.ds(slot * 2 + 1, 1), :]
-                src[q, pl.ds(136, 1), :] = halo[0, q, pl.ds(slot * 2, 1), :]
-            if step == 0:
-                for q in range(8):
-                    ref, k = (tr, q) if q < 4 else (ve, q - 4)
-                    src[q, pl.ds(8, WIDTH), :] = ref[slot, k]
-            for r in range(0, 144, 16):
-                p0, p1 = pressure(*[src[q, pl.ds(r, 16), :] for q in range(4)])
-                src[8, pl.ds(r, 16), :] = p0
-                src[9, pl.ds(r, 16), :] = p1
+                out[group, 2 * i + level] = new[i]
+
+    def by_row(values):
+        x = jnp.zeros((8, WIDTH), F32)
+        for slot in range(4):
+            for odd in range(2):
+                x = jnp.where(sub8 == slot * 2 + odd, values(slot, odd), x)
+        return x
+
+    def ends(x, where):
+        return jnp.where(lane8 == where, x, 1.0)
+
+    scale = 2.0 / (ROWS * WIDTH)
+    base = by_row(lambda slot, odd: factor(slot, 26) * float(WIDTH))
+    halo_row = by_row(
+        lambda slot, odd: -1.0 if odd else jnp.where(item(slot, 25) == 1, WIDTH - 1.0, float(WIDTH)),
+    )
+    across = (base + lane8.astype(F32) + 0.5) * scale
+    o_out, o_low, o_high, cor0, cor1 = [], [], [], [], []
+    for group in range(2):
+        o_out.append(by_row(lambda slot, odd: factor(slot, ((17, 16), (19, 18))[group][odd])))
+        lo, hi = ((18, 19), (16, 17))[group]
+        o_low.append(ends(by_row(lambda slot, odd: factor(slot, lo)), 0))
+        o_high.append(ends(by_row(lambda slot, odd: factor(slot, hi)), WIDTH - 1))
+        if group == 0:
+            cor0.append((base + jnp.where(even, WIDTH - 1.0, 0.0) + 0.5) * scale)
+            cor1.append((base + jnp.where(even, WIDTH - 2.0, 1.0) + 0.5) * scale)
+        else:
+            cor0.append(across)
+            cor1.append(across)
+
+    for group in range(2):
+        lo, hi = ((22, 23), (20, 21)) if group == 0 else ((21, 23), (20, 22))
+        corner_low = ends(by_row(lambda slot, odd: factor(slot, (lo, hi)[odd][0])), 0)
+        corner_high = ends(by_row(lambda slot, odd: factor(slot, (lo, hi)[odd][1])), WIDTH - 1)
+        cor = (base + halo_row + 0.5) * scale if group == 0 else across
+        strip(
+            group,
+            lambda q: hx[group, q],
+            lambda q: hx[group, 8 + q],
+            lambda q: inn[group, q],
+            lambda q: crv[group, q],
+            lambda q: crv[group, q],
+            None,
+            corner_low,
+            corner_high,
+            cor,
+            upd,
+        )
+    for group in range(2):
+        beyond = [lateral(hx[1 - group, q], 0) for q in range(8)]
+        strip(
+            group,
+            lambda q: inn[group, q],
+            lambda q: hx[group, q],
+            lambda q: inn[group, 8 + q],
+            lambda q: beyond[q][0],
+            lambda q: beyond[q][1],
+            o_out[group],
+            o_low[group],
+            o_high[group],
+            cor0[group],
+            first,
+        )
+    for group in range(2):
+        for q in range(8):
+            for ring in (1, 2):
+                low, high = lateral(first[1 - group, q], ring)
+                x = mid[group, (ring - 1) * 8 + q]
+                mid[group, (ring - 1) * 8 + q] = jnp.where(lane8 == 0, low, jnp.where(lane8 == WIDTH - 1, high, x))
+    for group in range(2):
+        beyond0 = [lateral(upd[1 - group, q], 0) for q in range(8)]
+        strip(
+            group,
+            lambda q: first[group, q],
+            lambda q: upd[group, q],
+            lambda q: mid[group, q],
+            lambda q: beyond0[q][0],
+            lambda q: beyond0[q][1],
+            o_out[group],
+            o_low[group],
+            o_high[group],
+            cor0[group],
+            r0,
+        )
+        beyond1 = [lateral(upd[1 - group, q], 1) for q in range(8)]
+        strip(
+            group,
+            lambda q: mid[group, q],
+            lambda q: first[group, q],
+            lambda q: mid[group, 8 + q],
+            lambda q: beyond1[q][0],
+            lambda q: beyond1[q][1],
+            None,
+            o_low[group],
+            o_high[group],
+            cor1[group],
+            r1,
+        )
+
+    live8 = by_row(lambda slot, odd: factor(slot, 24)) > 0.5
+    for group in range(2):
+        for q in range(8):
+            r0[group, q] = jnp.where(live8, r0[group, q], 0.0)
+            r1[group, q] = jnp.where(live8, r1[group, q], 0.0)
+    for q in range(8):
+        for slot in range(4):
+            for j, (ring, odd) in enumerate(((r1, 0), (r0, 0), (r0, 1), (r1, 1))):
+                turned[pl.ds((slot * 8 + q) * 4 + j, 1), :] = ring[1, q, pl.ds(slot * 2 + odd, 1), :]
+    turned[...] = turned[...].T
+    lane16 = lane_iota(EDGE)
+    rim = (lane16 < 2) | (lane16 >= WIDTH - 2)
+    out_copies = []
+    for slot in range(4):
+        for q in range(8):
+            src, res, k = (tr, res_t, q) if q < 4 else (ve, res_v, q - 4)
+            tile = slot * 8 + q
             for r in range(0, WIDTH, EDGE):
-                f = (base + (y16 + (r + 0.5))) * (2.0 / (ROWS * WIDTH))
-                for level in range(2):
-                    c, e, w, n, s = [], [], [], [], []
-                    for i in range(5):
-                        q = 2 * i + level
-                        x = src[q, pl.ds(8 + r, EDGE), :]
-                        edge = pltpu.roll(cols[step, pl.ds(r, EDGE), :], WIDTH - 1 - q * 8 - 2 * slot, 1)
-                        c.append(x)
-                        e.append(jnp.where(lane == WIDTH - 1, edge, pltpu.roll(x, WIDTH - 1, 1)))
-                        w.append(jnp.where(lane == 0, edge, pltpu.roll(x, 1, 1)))
-                        n.append(src[q, pl.ds(9 + r, EDGE), :])
-                        s.append(src[q, pl.ds(7 + r, EDGE), :])
-                    new = stencil(
-                        c, e, w, n, s, oe, ow, on16 if r == WIDTH - EDGE else None, os16 if r == 0 else None, f
-                    )
-                    for i in range(4):
-                        if step == 0:
-                            xb[2 * i + level, pl.ds(8 + r, EDGE), :] = new[i]
-                        else:
-                            out = tr_out if i < 2 else ve_out
-                            out[slot, 2 * (i % 2) + level, pl.ds(r, EDGE), :] = jnp.where(alive, new[i], 0.0)
-        return carry
-
-    for src in (xa, xb):
-        for q in range(8):
-            src[q, pl.ds(0, 8), :] = jnp.zeros((8, WIDTH), F32)
-            src[q, pl.ds(136, 8), :] = jnp.zeros((8, WIDTH), F32)
-    lax.fori_loop(0, 4, one_slot, 0)
+                x = pltpu.roll(turned[pl.ds(r, EDGE), :], (-(tile * 4 + 2)) % WIDTH, 1)
+                res[slot, k, pl.ds(r, EDGE), :] = jnp.where(rim, x, src[slot, k, pl.ds(r, EDGE), :])
+            for ring, rr in ((0, r0), (1, r1)):
+                res[slot, k, pl.ds(ring, 1), :] = rr[0, q, pl.ds(slot * 2 + 1, 1), :]
+                res[slot, k, pl.ds(WIDTH - 1 - ring, 1), :] = rr[0, q, pl.ds(slot * 2, 1), :]
+        for i, (res, out) in enumerate(((res_t, tr_out), (res_v, ve_out))):
+            copy = pltpu.make_async_copy(res.at[slot], out.at[slot], sent.at[slot * 2 + i])
+            copy.start()
+            out_copies.append(copy)
+    for copy in out_copies:
+        copy.wait()
 
 
 def shape(*dims):
@@ -477,11 +633,11 @@
     ve = velocity.reshape(4, 4, WIDTH, WIDTH)
     swap = [(i, i ^ 1) for i in range(DEVICES)]
 
-    rims, codes, mine, load = pl.pallas_call(
+    rims, codes, mine, picks, load = pl.pallas_call(
         start_kernel,
-        out_shape=(shape(16 * EDGE, WIDTH), table_shape(64), table_shape(8), table_shape(8)),
+        out_shape=(shape(16 * EDGE, WIDTH), table_shape(64), table_shape(8), table_shape(8), table_shape(8)),
         in_specs=[SM, VM, HB, HB],
-        out_specs=(VM, VM, VM, VM),
+        out_specs=(VM, VM, VM, VM, VM),
         scratch_shapes=[
             pltpu.VMEM((32, WIDTH), I32),
             pltpu.VMEM((4, 4, WIDTH, WIDTH), F32),
@@ -489,15 +645,16 @@
             pltpu.VMEM((WIDTH, WIDTH), F32),
             pltpu.SemaphoreType.DMA((2,)),
         ],
-        compiler_params=params(32),
+        compiler_params=params(60),
         name="start",
     )(block_counts, land, tr, ve)
     other = permute(rims, swap)
     chip, message = pl.pallas_call(
         message_kernel,
         out_shape=(shape(32 * EDGE, WIDTH), shape(MSG, WIDTH)),
-        in_specs=[SM, VM, VM],
+        in_specs=[HB, VM, VM],
         out_specs=(VM, VM),
+        scratch_shapes=[pltpu.SMEM((8, WIDTH), I32), pltpu.SemaphoreType.DMA((1,))],
         compiler_params=params(16),
         name="message",
     )(mine, rims, other)
@@ -507,24 +664,46 @@
     chunks = pl.pallas_call(
         pack_kernel,
         out_shape=shape(8 * CHUNK, WIDTH),
-        in_specs=[SM] + [HB] * 6,
-        out_specs=VM,
+        in_specs=[HB] * 7,
+        out_specs=HB,
         scratch_shapes=[
-            pltpu.VMEM((4 * MSG, WIDTH), F32),
+            pltpu.SMEM((8, WIDTH), I32),
+            pltpu.VMEM((48, WIDTH), F32),
             pltpu.VMEM((16, WIDTH), F32),
-            pltpu.SMEM((8 * 32,), I32),
-            pltpu.SemaphoreType.DMA((6,)),
+            pltpu.SemaphoreType.DMA((15,)),
+            pltpu.SemaphoreType.DMA((1,)),
         ],
         compiler_params=params(16),
         name="pack",
-    )(codes, message, *near, *far)
+    )(picks, message, *near, *far)
+    tr, ve, chunks = lax.optimization_barrier((tr, ve, chunks))
+    tr_inner, ve_inner, inner_rims = pl.pallas_call(
+        inner_kernel,
+        out_shape=(shape(4, 4, WIDTH, WIDTH), shape(4, 4, WIDTH, WIDTH), shape(16 * EDGE, WIDTH)),
+        in_specs=[SM, VM, VM],
+        out_specs=(VM, VM, VM),
+        scratch_shapes=[
+            pltpu.VMEM((10, 144, WIDTH), F32),
+            pltpu.VMEM((10, 144, WIDTH), F32),
+            pltpu.VMEM((WIDTH, WIDTH), F32),
+        ],
+        compiler_params=params(32),
+        cost_estimate=pl.CostEstimate(flops=60_000_000, bytes_accessed=8_000_000, transcendentals=0),
+        name="inner",
+    )(mine, tr, ve)
     got = exchange_z(chunks.reshape(8, CHUNK, WIDTH)).reshape(8 * CHUNK, WIDTH)
+    got, tr_inner, ve_inner, inner_rims = lax.optimization_barrier((got, tr_inner, ve_inner, inner_rims))
     own, others = pl.pallas_call(
         sort_kernel,
         out_shape=(shape(SWAP, WIDTH), shape(SWAP, WIDTH)),
-        in_specs=[SM, VM],
+        in_specs=[HB, VM],
         out_specs=(VM, VM),
-        scratch_shapes=[pltpu.SMEM((8,), I32), pltpu.SMEM((32,), I32)],
+        scratch_shapes=[
+            pltpu.SMEM((8, WIDTH), I32),
+            pltpu.SMEM((8,), I32),
+            pltpu.SMEM((32,), I32),
+            pltpu.SemaphoreType.DMA((1,)),
+        ],
         compiler_params=params(16),
         name="sort",
     )(mine, got)
@@ -556,24 +735,29 @@
     theirs = permute(others, swap)
 
     tr_new, ve_new = pl.pallas_call(
-        steps_kernel,
+        final_kernel,
         out_shape=(shape(4, 4, WIDTH, WIDTH), shape(4, 4, WIDTH, WIDTH)),
-        in_specs=[SM] + [HB] * 3 + [VM] * 2,
-        out_specs=(VM, VM),
+        in_specs=[SM] + [HB] * 3 + [VM] * 4,
+        out_specs=(HB, HB),
         scratch_shapes=[
             pltpu.VMEM((32 * EDGE + 2 * SWAP + EDGE, WIDTH), F32),
+            pltpu.VMEM((2, EDGE, 8, WIDTH), F32),
+            pltpu.VMEM((2, EDGE, 8, WIDTH), F32),
             pltpu.VMEM((2, EDGE, 8, WIDTH), F32),
             pltpu.VMEM((2, 8, 8, WIDTH), F32),
             pltpu.VMEM((2, 8, 8, WIDTH), F32),
             pltpu.VMEM((2, 8, 8, WIDTH), F32),
-            pltpu.VMEM((2, WIDTH, WIDTH), F32),
-            pltpu.VMEM((10, 144, WIDTH), F32),
-            pltpu.VMEM((10, 144, WIDTH), F32),
+            pltpu.VMEM((2, 8, 8, WIDTH), F32),
+            pltpu.VMEM((2, 8, 8, WIDTH), F32),
+            pltpu.VMEM((WIDTH, WIDTH), F32),
+            pltpu.VMEM((4, 4, WIDTH, WIDTH), F32),
+            pltpu.VMEM((4, 4, WIDTH, WIDTH), F32),
             pltpu.SemaphoreType.DMA((3,)),
+            pltpu.SemaphoreType.DMA((8,)),
         ],
         compiler_params=params(32),
-        name="steps",
-    )(mine, chip, own, theirs, tr, ve)
+        name="final",
+    )(mine, chip, own, theirs, rims, inner_rims, tr_inner, ve_inner)
     return tr_new.reshape(tracers.shape), ve_new.reshape(velocity.shape)
 
 

time: 67.3 us -> 58.9 us (0.88)
  waiting for transfers between devices: 24.2 us -> 15 us
    all_to_all x1, waiting for transfers between devices: 15.4 us -> 5.97 us  [exchange_z(): return lax.all_to_all(x, 'blk', 0, 0, axis_index_groups=groups, tiled=True)]
    pallas_call x1, Pallas kernels: 3.38 us -> 2 us  [per_device(): pl.pallas_call(pack_kernel, out_shape=shape(8 * CHUNK, WIDTH), in_specs=[...]
    pallas_call x1 -> x2, Pallas kernels: 7.75 us -> 9.02 us  [the longest x1 5.02 us: per_device(): pl.pallas_call(inner_kernel, out_shape=(shape(4, 4, WIDTH, WIDTH), shape(...]
    unnamed x14 -> x20, local copies, waits for them, and re-layouts: 3.85 us -> 2.88 us
    pallas_call x1, Pallas kernels: 3.57 us -> 4.29 us  [per_device(): pl.pallas_call(start_kernel, out_shape=(shape(16 * EDGE, WIDTH), table_sh...]
  transfers between devices with their start and end apart: 8 -> 8, of which waited for: 7 -> 7; matrix products, arithmetic and copies ran while one was open for 1% -> 2% of each run, Pallas kernels for 0% -> 9%
where the time goes in v3:
time: 58.9 us; the launch traced here: 58.6 us
  starting transfers between devices  20.5 us (35%)
  Pallas kernels  17.6 us (30%)
  waiting for transfers between devices  15 us (25%)
  local copies, waits for them, and re-layouts  4.07 us (7%)
  between operations  1.41 us (2%)
    ppermute x7, starting transfers between devices, permute(): return lax.ppermute(x, 'blk', pairs)  13.8 us
    ppermute x7, waiting for transfers between devices, permute(): return lax.ppermute(x, 'blk', pairs)  9.03 us
    all_to_all x1, starting transfers between devices, exchange_z(): return lax.all_to_all(x, 'blk', 0, 0, axis_index_groups=groups, tiled=True)  6.66 us
    all_to_all x1, waiting for transfers between devices, exchange_z(): return lax.all_to_all(x, 'blk', 0, 0, axis_index_groups=groups, tiled=True)  5.97 us
    pallas_call x1, Pallas kernels, per_device(): pl.pallas_call(inner_kernel, out_shape=(shape(4, 4, WIDTH, WIDTH), shape(...  5.02 us
    pallas_call x1, Pallas kernels, per_device(): pl.pallas_call(start_kernel, out_shape=(shape(16 * EDGE, WIDTH), table_sh...  4.29 us
    pallas_call x1, Pallas kernels, per_device(): pl.pallas_call(final_kernel, out_shape=(shape(4, 4, WIDTH, WIDTH), shape(...  4 us
    unnamed x20, local copies, waits for them, and re-layouts  2.88 us
  transfers between devices with their start and end apart: 8, of which 7 were waited for; matrix products, arithmetic and copies ran while one was open for 2% of the time, Pallas kernels for 9%

profile of v3, /device:TPU:1, one launch (start us, length us, event | category | flops | bytes accessed | tf_op | source)
XLA Modules:
  0.0 58.6 jit_solution(5153574724747224851)
XLA Ops:
  0.6 4.3 %start.1 = (f32[256,128]{1,0:T(8,128)}, s32[64,128]{1,0:T(8,128)S(1)}, s32[8,128]{1,0:T(8,128)S(1)}, s32[8,128]{1,0:T(8,128)}, s32[8,128]{1,0:T(8,128)}) custom-call(s32[256]{0:T(256)} %counts.1, s32[26,34]{1,0:T(8,128)} %land.1, f32[4,4,128,128]{3,2,1,0:T(8,128)} %bitcast.21, f32[4,4,128,128]{3,2,1,0:T(8,128)} %bitcast.23), custom_call_target="tpu_custom_call" | custom-call | tf_op jit(solution)/shard_map/start/pallas_call | solution.py:636
  4.9 3.3 %collective-permute-start = (f32[256,128]{1,0:T(8,128)}, f32[256,128]{1,0:T(8,128)S(1)}, u32[]{:S(2)}, u32[]{:S(2)}) collective-permute-start(f32[256,128]{1,0:T(8,128)} %get-tuple-element.54.mine.edges), channel_id=1, source_target_pairs={{0,1},{1,0},{2,3},{3,2},{4,5},{5,4},{6,7},{7,6},{8,9},{9,8},{10,11... | collective-permute-start | bytes 393224 | tf_op jit(solution)/shard_map/ppermute | solution.py:619
  8.3 1.2 %collective-permute-done.other = f32[256,128]{1,0:T(8,128)S(1)} collective-permute-done((f32[256,128]{1,0:T(8,128)}, f32[256,128]{1,0:T(8,128)S(1)}, u32[]{:S(2)}, u32[]{:S(2)}) %collective-permute-start) | collective-permute-done | bytes 131104 | tf_op jit(solution)/shard_map/ppermute | solution.py:619
  9.5 0.9 %copy-done.6 = f32[256,128]{1,0:T(8,128)S(1)} copy-done((f32[256,128]{1,0:T(8,128)S(1)}, f32[256,128]{1,0:T(8,128)}, u32[]{:S(2)}) %copy-start.6) | copy-done | bytes 131096
  10.4 0.7 %message.1 = (f32[512,128]{1,0:T(8,128)S(1)}, f32[296,128]{1,0:T(8,128)S(1)}) custom-call(s32[8,128]{1,0:T(8,128)S(1)} %get-tuple-element.53.table_hbm.table, f32[256,128]{1,0:T(8,128)S(1)} %copy-done.6, f32[256,128]{1,0:T(8,128)S(1)} %collective-permute-done.other), custom_call_target="tpu_custom_call" | custom-call | tf_op jit(solution)/shard_map/message/pallas_call | solution.py:652
  11.0 3.3 %collective-permute-start.1 = (f32[296,128]{1,0:T(8,128)S(1)}, f32[296,128]{1,0:T(8,128)S(1)}, u32[]{:S(2)}, u32[]{:S(2)}) collective-permute-start(f32[296,128]{1,0:T(8,128)S(1)} %get-tuple-element.58.m0), channel_id=1, source_target_pairs={{0,16},{1,241},{2,18},{3,243},{4,20},{5,245},{6,22},{7,247},{8,24}... | collective-permute-start | bytes 454664 | tf_op jit(solution)/shard_map/ppermute | solution.py:619
  14.3 0.3 collective-permute-start.2
  14.7 1.0 %collective-permute-start.3 = (f32[296,128]{1,0:T(8,128)S(1)}, f32[296,128]{1,0:T(8,128)S(1)}, u32[]{:S(2)}, u32[]{:S(2)}) collective-permute-start(f32[296,128]{1,0:T(8,128)S(1)} %get-tuple-element.58.m0), channel_id=1, source_target_pairs={{0,48},{1,209},{2,50},{3,211},{4,52},{5,213},{6,54},{7,215},{8,56}... | collective-permute-start | bytes 454664 | tf_op jit(solution)/shard_map/ppermute | solution.py:619
  15.9 2.0 %collective-permute-start.5 = (f32[8,128]{1,0:T(8,128)S(1)}, f32[8,128]{1,0:T(8,128)S(1)}, u32[]{:S(2)}, u32[]{:S(2)}) collective-permute-start(f32[8,128]{1,0:T(8,128)S(1)} %slice.45), channel_id=1, source_target_pairs={{0,80},{1,177},{2,82},{3,179},{4,84},{5,181},{6,86},{7,183},{8,88}... | collective-permute-start | bytes 12296 | tf_op jit(solution)/shard_map/ppermute | solution.py:619
  17.8 2.0 %collective-permute-done.4.c4 = f32[8,128]{1,0:T(8,128)S(1)} collective-permute-done((f32[8,128]{1,0:T(8,128)S(1)}, f32[8,128]{1,0:T(8,128)S(1)}, u32[]{:S(2)}, u32[]{:S(2)}) %collective-permute-start.4) | collective-permute-done | bytes 4128 | tf_op jit(solution)/shard_map/ppermute | solution.py:619
  19.9 1.0 %collective-permute-done.5.c5 = f32[8,128]{1,0:T(8,128)S(1)} collective-permute-done((f32[8,128]{1,0:T(8,128)S(1)}, f32[8,128]{1,0:T(8,128)S(1)}, u32[]{:S(2)}, u32[]{:S(2)}) %collective-permute-start.5) | collective-permute-done | bytes 4128 | tf_op jit(solution)/shard_map/ppermute | solution.py:619
  20.8 2.1 %collective-permute-done.2.m2 = f32[296,128]{1,0:T(8,128)S(1)} collective-permute-done((f32[296,128]{1,0:T(8,128)S(1)}, f32[296,128]{1,0:T(8,128)S(1)}, u32[]{:S(2)}, u32[]{:S(2)}) %collective-permute-start.2) | collective-permute-done | bytes 151584 | tf_op jit(solution)/shard_map/ppermute | solution.py:619
  22.9 1.5 %collective-permute-done.3.m3 = f32[296,128]{1,0:T(8,128)S(1)} collective-permute-done((f32[296,128]{1,0:T(8,128)S(1)}, f32[296,128]{1,0:T(8,128)S(1)}, u32[]{:S(2)}, u32[]{:S(2)}) %collective-permute-start.3) | collective-permute-done | bytes 151584 | tf_op jit(solution)/shard_map/ppermute | solution.py:619
  24.5 2.0 %pack.1 = f32[1024,128]{1,0:T(8,128)} custom-call(s32[8,128]{1,0:T(8,128)S(1)} %copy-done.8, f32[296,128]{1,0:T(8,128)S(1)} %get-tuple-element.58.m0, f32[296,128]{1,0:T(8,128)S(1)} %collective-permute-done.1.m1, f32[296,128]{1,0:T(8,128)S(1)} %collective-permute-done.2.m2, f32[296,128]{1,0:T(8,128)S(1)} %collective-permute-done.3.m3, ...), custom_call_target="tpu_custom_call" | custom-call | tf_op jit(solution)/shard_map/pack/pallas_call | solution.py:664
  26.5 6.7 %all-to-all-start.1 = ((f32[8,128,128]{2,1,0:T(8,128)}), f32[8,128,128]{2,1,0:T(8,128)S(1)}, u32[]{:S(2)}, u32[]{:S(2)}) async-start(f32[8,128,128]{2,1,0:T(8,128)} %bitcast.11), calls=%async_computation.1 | async-start | bytes 1048576 | tf_op jit(solution)/shard_map/all_to_all | solution.py:628
  33.2 1.2 %slice.44 = s32[1,1]{1,0:T(1,128)} slice(s32[8,128]{1,0:T(8,128)} %get-tuple-element.56), slice={[0:1], [0:1]} | slice | bytes 8 | tf_op jit(solution)/shard_map/slice | solution.py:733
  35.0 5.0 %inner.1 = (f32[4,4,128,128]{3,2,1,0:T(8,128)S(1)}, f32[4,4,128,128]{3,2,1,0:T(8,128)S(1)}, f32[256,128]{1,0:T(8,128)S(1)}) custom-call(s32[8,128]{1,0:T(8,128)S(1)} %get-tuple-element.53.table_hbm.table, f32[4,4,128,128]{3,2,1,0:T(8,128)S(1)} %bitcast.22, f32[4,4,128,128]{3,2,1,0:T(8,128)S(1)} %bitcast.24), custom_call_target="tpu_custom_call" | custom-call | flops 60000000 | bytes 8000000 | tf_op jit(solution)/shard_map/inner/pallas_call | solution.py:680
  40.1 1.0 %copy-done.2 = f32[4,4,128,128]{3,2,1,0:T(8,128)} copy-done((f32[4,4,128,128]{3,2,1,0:T(8,128)}, f32[4,4,128,128]{3,2,1,0:T(8,128)S(1)}, u32[]{:S(2)}) %copy-start.2) | copy-done | bytes 1048600
  41.0 1.0 %copy-done.4 = f32[4,4,128,128]{3,2,1,0:T(8,128)} copy-done((f32[4,4,128,128]{3,2,1,0:T(8,128)}, f32[4,4,128,128]{3,2,1,0:T(8,128)S(1)}, u32[]{:S(2)}) %copy-start.4) | copy-done | bytes 1048600
  42.0 6.0 %all-to-all-done.1 = f32[8,128,128]{2,1,0:T(8,128)S(1)} async-done(((f32[8,128,128]{2,1,0:T(8,128)}), f32[8,128,128]{2,1,0:T(8,128)S(1)}, u32[]{:S(2)}, u32[]{:S(2)}) %all-to-all-start.1) | async-done | bytes 524320 | tf_op jit(solution)/shard_map/all_to_all | solution.py:628
  48.0 1.6 %sort.1 = (f32[264,128]{1,0:T(8,128)}, f32[264,128]{1,0:T(8,128)}) custom-call(s32[8,128]{1,0:T(8,128)S(1)} %get-tuple-element.53.table_hbm.table, f32[1024,128]{1,0:T(8,128)S(1)} %bitcast.25), custom_call_target="tpu_custom_call" | custom-call | tf_op jit(solution)/shard_map/sort/pallas_call | solution.py:696
  49.7 3.7 %collective-permute-start.6 = (f32[264,128]{1,0:T(8,128)}, f32[264,128]{1,0:T(8,128)S(1)}, u32[]{:S(2)}, u32[]{:S(2)}) collective-permute-start(f32[264,128]{1,0:T(8,128)} %get-tuple-element.70), channel_id=1, source_target_pairs={{0,1},{1,0},{2,3},{3,2},{4,5},{5,4},{6,7},{7,6},{8,9},{9,8},{10,11... | collective-permute-start | bytes 405512 | tf_op jit(solution)/shard_map/ppermute | solution.py:619
  53.4 1.2 %collective-permute-done.6.other = f32[264,128]{1,0:T(8,128)S(1)} collective-permute-done((f32[264,128]{1,0:T(8,128)}, f32[264,128]{1,0:T(8,128)S(1)}, u32[]{:S(2)}, u32[]{:S(2)}) %collective-permute-start.6) | collective-permute-done | bytes 135200 | tf_op jit(solution)/shard_map/ppermute | solution.py:619
  54.6 4.0 %final.1 = (f32[4,4,128,128]{3,2,1,0:T(8,128)}, f32[4,4,128,128]{3,2,1,0:T(8,128)}) custom-call(s32[8,128]{1,0:T(8,128)S(1)} %get-tuple-element.53.table_hbm.table, f32[512,128]{1,0:T(8,128)S(1)} %get-tuple-element.55.chip, f32[264,128]{1,0:T(8,128)} %get-tuple-element.69.own, f32[264,128]{1,0:T(8,128)S(1)} %collective-permute-done.6.other, ...), custom_call_target="tpu_custom_call" | custom-call | tf_op jit(solution)/shard_map/final/pallas_call | solution.py:737
  (21 shorter events, 0.3 us)
Async XLA Ops:
  4.9 4.5 %collective-permute-start = (f32[256,128]{1,0:T(8,128)}, f32[256,128]{1,0:T(8,128)S(1)}, u32[]{:S(2)}, u32[]{:S(2)}) collective-permute-start(f32[256,128]{1,0:T(8,128)} %get-tuple-element.54.mine.edges), channel_id=1, source_target_pairs={{0,1},{1,0},{2,3},{3,2},{4,5},{5,4},{6,7},{7,6},{8,9},{9,8},{10,11... | collective-permute-start | bytes 393224 | tf_op jit(solution)/shard_map/ppermute | solution.py:619
  9.5 0.9 %copy-start.6 = (f32[256,128]{1,0:T(8,128)S(1)}, f32[256,128]{1,0:T(8,128)}, u32[]{:S(2)}) copy-start(f32[256,128]{1,0:T(8,128)} %get-tuple-element.54.mine.edges) | copy-start | bytes 393220
  11.0 13.4 %copy-start.8 = (s32[8,128]{1,0:T(8,128)S(1)}, s32[8,128]{1,0:T(8,128)}, u32[]{:S(2)}) copy-start(s32[8,128]{1,0:T(8,128)} %get-tuple-element.57.picks_hbm) | copy-start | bytes 12292
  11.0 9.8 %collective-permute-start.1 = (f32[296,128]{1,0:T(8,128)S(1)}, f32[296,128]{1,0:T(8,128)S(1)}, u32[]{:S(2)}, u32[]{:S(2)}) collective-permute-start(f32[296,128]{1,0:T(8,128)S(1)} %get-tuple-element.58.m0), channel_id=1, source_target_pairs={{0,16},{1,241},{2,18},{3,243},{4,20},{5,245},{6,22},{7,247},{8,24}... | collective-permute-start | bytes 454664 | tf_op jit(solution)/shard_map/ppermute | solution.py:619
  14.3 8.6 %collective-permute-start.2 = (f32[296,128]{1,0:T(8,128)S(1)}, f32[296,128]{1,0:T(8,128)S(1)}, u32[]{:S(2)}, u32[]{:S(2)}) collective-permute-start(f32[296,128]{1,0:T(8,128)S(1)} %get-tuple-element.58.m0), channel_id=1, source_target_pairs={{0,32},{1,225},{2,34},{3,227},{4,36},{5,229},{6,38},{7,231},{8,40}... | collective-permute-start | bytes 454664 | tf_op jit(solution)/shard_map/ppermute | solution.py:619
  14.7 9.8 %collective-permute-start.3 = (f32[296,128]{1,0:T(8,128)S(1)}, f32[296,128]{1,0:T(8,128)S(1)}, u32[]{:S(2)}, u32[]{:S(2)}) collective-permute-start(f32[296,128]{1,0:T(8,128)S(1)} %get-tuple-element.58.m0), channel_id=1, source_target_pairs={{0,48},{1,209},{2,50},{3,211},{4,52},{5,213},{6,54},{7,215},{8,56}... | collective-permute-start | bytes 454664 | tf_op jit(solution)/shard_map/ppermute | solution.py:619
  15.6 4.2 %collective-permute-start.4 = (f32[8,128]{1,0:T(8,128)S(1)}, f32[8,128]{1,0:T(8,128)S(1)}, u32[]{:S(2)}, u32[]{:S(2)}) collective-permute-start(f32[8,128]{1,0:T(8,128)S(1)} %slice.45), channel_id=1, source_target_pairs={{0,64},{1,193},{2,66},{3,195},{4,68},{5,197},{6,70},{7,199},{8,72}... | collective-permute-start | bytes 12296 | tf_op jit(solution)/shard_map/ppermute | solution.py:619
  15.9 4.9 %collective-permute-start.5 = (f32[8,128]{1,0:T(8,128)S(1)}, f32[8,128]{1,0:T(8,128)S(1)}, u32[]{:S(2)}, u32[]{:S(2)}) collective-permute-start(f32[8,128]{1,0:T(8,128)S(1)} %slice.45), channel_id=1, source_target_pairs={{0,80},{1,177},{2,82},{3,179},{4,84},{5,181},{6,86},{7,183},{8,88}... | collective-permute-start | bytes 12296 | tf_op jit(solution)/shard_map/ppermute | solution.py:619
  24.5 2.0 %copy-start.11 = (f32[296,128]{1,0:T(8,128)}, f32[296,128]{1,0:T(8,128)S(1)}, u32[]{:S(2)}) copy-start(f32[296,128]{1,0:T(8,128)S(1)} %collective-permute-done.3.m3) | copy-start | bytes 454660
  24.5 10.5 %copy-start = (f32[4,2,2,128,128]{4,3,2,1,0:T(8,128)S(1)}, f32[4,2,2,128,128]{4,3,2,1,0:T(8,128)}, u32[]{:S(2)}) copy-start(f32[4,2,2,128,128]{4,3,2,1,0:T(8,128)} %param.6) | copy-start | bytes 3145732
  24.5 10.6 %copy-start.1 = (f32[4,2,2,128,128]{4,3,2,1,0:T(8,128)S(1)}, f32[4,2,2,128,128]{4,3,2,1,0:T(8,128)}, u32[]{:S(2)}) copy-start(f32[4,2,2,128,128]{4,3,2,1,0:T(8,128)} %param.7) | copy-start | bytes 3145732
  26.5 21.5 %all-to-all-start.1 = ((f32[8,128,128]{2,1,0:T(8,128)}), f32[8,128,128]{2,1,0:T(8,128)S(1)}, u32[]{:S(2)}, u32[]{:S(2)}) async-start(f32[8,128,128]{2,1,0:T(8,128)} %bitcast.11), calls=%async_computation.1 | async-start | bytes 1048576 | tf_op jit(solution)/shard_map/all_to_all | solution.py:628
  40.1 1.0 %copy-start.2 = (f32[4,4,128,128]{3,2,1,0:T(8,128)}, f32[4,4,128,128]{3,2,1,0:T(8,128)S(1)}, u32[]{:S(2)}) copy-start(f32[4,4,128,128]{3,2,1,0:T(8,128)S(1)} %get-tuple-element.72.tr) | copy-start | bytes 3145732
  41.0 1.0 %copy-start.4 = (f32[4,4,128,128]{3,2,1,0:T(8,128)}, f32[4,4,128,128]{3,2,1,0:T(8,128)S(1)}, u32[]{:S(2)}) copy-start(f32[4,4,128,128]{3,2,1,0:T(8,128)S(1)} %get-tuple-element.73.ve) | copy-start | bytes 3145732
  49.6 5.0 %copy-start.3 = (f32[4,4,128,128]{3,2,1,0:T(8,128)S(1)}, f32[4,4,128,128]{3,2,1,0:T(8,128)}, u32[]{:S(2)}) copy-start(f32[4,4,128,128]{3,2,1,0:T(8,128)} %copy-done.2) | copy-start | bytes 3145732
  49.6 5.0 %copy-start.5 = (f32[4,4,128,128]{3,2,1,0:T(8,128)S(1)}, f32[4,4,128,128]{3,2,1,0:T(8,128)}, u32[]{:S(2)}) copy-start(f32[4,4,128,128]{3,2,1,0:T(8,128)} %copy-done.4) | copy-start | bytes 3145732
  49.6 5.0 %copy-start.7 = (f32[256,128]{1,0:T(8,128)S(1)}, f32[256,128]{1,0:T(8,128)}, u32[]{:S(2)}) copy-start(f32[256,128]{1,0:T(8,128)} %get-tuple-element.54.mine.edges) | copy-start | bytes 393220
  49.7 4.9 %collective-permute-start.6 = (f32[264,128]{1,0:T(8,128)}, f32[264,128]{1,0:T(8,128)S(1)}, u32[]{:S(2)}, u32[]{:S(2)}) collective-permute-start(f32[264,128]{1,0:T(8,128)} %get-tuple-element.70), channel_id=1, source_target_pairs={{0,1},{1,0},{2,3},{3,2},{4,5},{5,4},{6,7},{7,6},{8,9},{9,8},{10,11... | collective-permute-start | bytes 405512 | tf_op jit(solution)/shard_map/ppermute | solution.py:619

commit v4 on v3

--- a/solution.py
+++ b/solution.py
@@ -43,8 +43,13 @@
     return jnp.dot(a.astype(jnp.bfloat16), b.astype(jnp.bfloat16), preferred_element_type=F32)
 
 
-def build_tables(me, counts, land, board, codes, mine, picks, load):
-    column, zed, core = me >> 4, (me >> 1) & 7, me & 1
+def ids_kernel(counts_hbm, land_hbm, grid, marks, counts, land, board, sem):
+    copies = [pltpu.make_async_copy(counts_hbm, counts, sem.at[0]), pltpu.make_async_copy(land_hbm, land, sem.at[1])]
+    for copy in copies:
+        copy.start()
+    for copy in copies:
+        copy.wait()
+    me = lax.axis_index("blk").astype(I32)
     board[...] = jnp.ones((32, WIDTH), I32)
     board[pl.ds(0, ROWS), pl.ds(0, COLS)] = land[...]
     sea = board[...] == 0
@@ -68,7 +73,25 @@
 
     zero = jnp.zeros((32, WIDTH), I32)
     _, owner, start = lax.fori_loop(0, DEVICES // 8, device, (jnp.int32(0), zero, zero))
-    ids = jnp.where(sea, owner * 4 + pos - start, -1).astype(F32)
+    ids = jnp.where(sea, owner * 4 + pos - start, -1)
+    grid[...] = ids
+    slot = (ids & 7).astype(F32)
+    here = jnp.right_shift(ids, 3) == jnp.right_shift(me, 1)
+    last = jnp.max(jnp.where(here, slot, 0.0))
+    first_col = jnp.max(jnp.where(here & (lane == 0), slot, 0.0))
+    last_col = -jnp.max(jnp.where(here & (lane == COLS - 1), -slot, -7.0))
+    lane8 = lane_iota(8)
+    marks[...] = jnp.where(lane8 == 0, last, jnp.where(lane8 == 1, first_col, last_col)).astype(I32)
+
+
+def tables_kernel(grid, codes, mine, picks, load):
+    me = lax.axis_index("blk").astype(I32)
+    column, zed, core = me >> 4, (me >> 1) & 7, me & 1
+    ids = grid[...].astype(F32)
+    sea = ids >= 0.0
+    lane, row = lane_iota(32), row_iota(32)
+    i, j = row_iota(WIDTH), lane_iota(WIDTH)
+    zero = jnp.zeros((32, WIDTH), I32)
 
     def west(x):
         return jnp.where(lane == 0, pltpu.roll(x, WIDTH - COLS + 1, 1), pltpu.roll(x, 1, 1))
@@ -97,6 +120,19 @@
         of_kind = sum((kinds[k][r : r + 1, :] == kind_row).astype(F32) for k in range(4)).astype(jnp.bfloat16)
         counted += lax.dot_general(is_chip, of_kind, (((1,), (1,)), ((), ())), preferred_element_type=F32)
     load[...] = jnp.broadcast_to(jnp.max(counted), (8, WIDTH)).astype(I32)
+    home = jnp.right_shift(chip, 3)
+    beyond = zero
+    for x in near:
+        source = jnp.right_shift(x.astype(I32), 3)
+        column_s, z_s = jnp.right_shift(source, 3), source & 7
+        gap = home - column_s
+        reached = (gap >= -2) & (gap <= 2)
+        reached |= (gap == 3) & (column_s <= 1) & (z_s >= 6)
+        reached |= (gap == -3) & (column_s <= 4) & (z_s <= 1)
+        reached |= ((gap == 4) & (source == 0)) | ((gap == -4) & (source == 33))
+        beyond = jnp.where(sea & (source >= 0) & ~reached, 1, beyond)
+    missed = jnp.broadcast_to(jnp.max(beyond.astype(F32)), (8, WIDTH)).astype(I32)
+    load[...] = jnp.where(lane_iota(8) == 1, missed, load[...])
 
     slot = row_iota(64)
     want = (column * 64 + slot).astype(F32)
@@ -169,13 +205,7 @@
     mine[...] = codes[pl.ds(pl.multiple_of(zed * 8, 8), 8), :]
 
 
-def start_kernel(counts, land, tr_hbm, ve_hbm, out, codes, mine, picks, load, board, tr, ve, turned, sem):
-    copies = [pltpu.make_async_copy(tr_hbm, tr, sem.at[0]), pltpu.make_async_copy(ve_hbm, ve, sem.at[1])]
-    for copy in copies:
-        copy.start()
-    build_tables(lax.axis_index("blk").astype(I32), counts, land, board, codes, mine, picks, load)
-    for copy in copies:
-        copy.wait()
+def rims_kernel(tr, ve, out, turned):
     lane = lane_iota(WIDTH) // 4
     gathered = jnp.zeros((WIDTH, WIDTH), F32)
     for slot in range(4):
@@ -216,19 +246,13 @@
             corners = jnp.where(lane == base + t, pltpu.roll(x, 2 * (base + t) + 1, 1), corners)
     out[pl.ds(MSG_EDGES * EDGE, 8), :] = corners
     fetch.wait()
-    last, first_col, last_col = jnp.int32(0), jnp.int32(0), jnp.int32(0)
-    for t in range(8):
-        live, col = table[t, 24] == 1, table[t, 27]
-        last = jnp.where(live, t, last)
-        first_col = jnp.where(live & (col == 0), t, first_col)
-        live, col = table[7 - t, 24] == 1, table[7 - t, 27]
-        last_col = jnp.where(live & (col == COLS - 1), 7 - t, last_col)
+    last, first_col, last_col = table[0, 0], table[0, 1], table[0, 2]
     for e, edge in ((8, jnp.where(flag, last * 4 + 3, 2)), (9, jnp.where(flag, first_col * 4 + 2, last_col * 4 + 3))):
         at = pl.multiple_of(edge * EDGE, EDGE)
         out[pl.ds(e * EDGE, EDGE), :] = chip[pl.ds(at, EDGE), :]
 
 
-def pack_kernel(picks_hbm, m0, m1, m2, m3, c4, c5, out, picks, held, packed, sem, sent):
+def pack_kernel(picks_hbm, m0, m1, m2, m3, c4, c5, out, picks, started, held, packed, sem, sent):
     messages = (m0, m1, m2, m3)
     fetch = pltpu.make_async_copy(picks_hbm, picks, sem.at[14])
     fetch.start()
@@ -238,22 +262,27 @@
     ]
     for copy in copies:
         copy.start()
-
-    def edges(wait):
-        for z in range(8):
-            for r in range(CAP):
-                code = picks[z, r]
-                for k, m in enumerate(messages):
-
-                    @pl.when((code > k * (MSG // 8)) & (code <= (k + 1) * (MSG // 8)))
-                    def _():
-                        row = pl.multiple_of((code - 1 - k * (MSG // 8)) * 8, EDGE)
-                        to = out.at[pl.ds(z * CHUNK + r * EDGE, EDGE)]
-                        copy = pltpu.make_async_copy(m.at[pl.ds(row, EDGE)], to, sent.at[0])
-                        copy.wait() if wait else copy.start()
-
+    started[0] = 0
     fetch.wait()
-    edges(False)
+
+    def edge(k, r):
+        code = picks[k, r]
+
+        @pl.when(code > 0)
+        def _():
+            started[0] = started[0] + 1
+            for i, m in enumerate(messages):
+
+                @pl.when((code > i * (MSG // 8)) & (code <= (i + 1) * (MSG // 8)))
+                def _():
+                    row = pl.multiple_of((code - 1 - i * (MSG // 8)) * 8, EDGE)
+                    pltpu.make_async_copy(m.at[pl.ds(row, EDGE)], out.at[pl.ds(k * CHUNK + r * EDGE, EDGE)], sent.at[0]).start()
+
+            if r + 1 < CAP:
+                edge(k, r + 1)
+
+    for k in range(8):
+        edge(k, 0)
     for copy in copies:
         copy.wait()
     lane = lane_iota(8) // 32
@@ -262,19 +291,27 @@
         near_c = jnp.where(lane == i, pltpu.roll(held[pl.ds(i * 8, 8), :], 32 * i, 1), near_c)
     packed[pl.ds(0, 8), :] = near_c
     packed[pl.ds(8, 8), :] = jnp.where(lane == 0, held[pl.ds(32, 8), :], pltpu.roll(held[pl.ds(40, 8), :], 32, 1))
-    copies = [
-        pltpu.make_async_copy(packed, out.at[pl.ds(z * CHUNK + CAP * EDGE, 16)], sem.at[6 + z]) for z in range(8)
-    ]
+    copies = [pltpu.make_async_copy(packed, out.at[pl.ds(k * CHUNK + CAP * EDGE, 16)], sem.at[6 + k]) for k in range(8)]
     for copy in copies:
         copy.start()
-    edges(True)
+
+    def wait(i, carry):
+        pltpu.make_async_copy(m0.at[pl.ds(0, EDGE)], out.at[pl.ds(0, EDGE)], sent.at[0]).wait()
+        return carry
+
+    lax.fori_loop(0, started[0], wait, 0)
     for copy in copies:
         copy.wait()
 
 
-def sort_kernel(table_hbm, got, own, other, table, taken, rows, sem):
+def sort_kernel(table_hbm, got_in, own, other, table, taken, rows, got, sem):
     fetch = pltpu.make_async_copy(table_hbm, table, sem.at[0])
     fetch.start()
+    copies = [
+        pltpu.make_async_copy(got_in.at[pl.ds(z * CHUNK, CHUNK)], got.at[pl.ds(z * CHUNK, CHUNK)], sem.at[1 + z]) for z in range(8)
+    ]
+    for copy in copies:
+        copy.start()
     core = lax.axis_index("blk").astype(I32) & 1
     for z in range(8):
         taken[z] = 0
@@ -286,6 +323,8 @@
             rank = taken[z]
             taken[z] = rank + (code >= 0).astype(I32)
             rows[t * 4 + side] = z * CHUNK + jnp.minimum(rank, CAP - 1) * EDGE
+    for copy in copies:
+        copy.wait()
     lane = lane_iota(8)
     for half, out in enumerate((own, other)):
         first = (core ^ half) * 4
@@ -620,12 +659,58 @@
 
 
 def column_pairs(distance):
-    return [(i, (i + 16 * distance * (1 if i % 2 == 0 else -1)) % DEVICES) for i in range(DEVICES)]
+    pairs = []
+    for i in range(DEVICES):
+        j = i + 16 * distance * (1 if i % 2 == 0 else -1)
+        pairs.append((i, j if 0 <= j < DEVICES else i ^ 1))
+    return pairs
+
+
+NEAR_PAIRS = [(i, i + 48) for i in range(32) if i % 2 == 0 and i % 16 >= 12]
+NEAR_PAIRS += [(i, i - 48) for i in range(48, 80) if i % 2 == 1 and i % 16 < 4]
+FAR_PAIRS = [(0, 64), (67, 3)]
 
 
 def exchange_z(x):
     groups = [[16 * a + 2 * z + c for z in range(8)] for a in range(16) for c in range(2)]
     return lax.all_to_all(x, "blk", 0, 0, axis_index_groups=groups, tiled=True)
+
+
+def pack(picks, message, near, far):
+    return pl.pallas_call(
+        pack_kernel,
+        out_shape=shape(8 * CHUNK, WIDTH),
+        in_specs=[HB] * 7,
+        out_specs=HB,
+        scratch_shapes=[
+            pltpu.SMEM((8, WIDTH), I32),
+            pltpu.SMEM((1,), I32),
+            pltpu.VMEM((48, WIDTH), F32),
+            pltpu.VMEM((16, WIDTH), F32),
+            pltpu.SemaphoreType.DMA((15,)),
+            pltpu.SemaphoreType.DMA((1,)),
+        ],
+        compiler_params=params(12),
+        name="pack",
+    )(picks, message, *near, *far)
+
+
+def sort(mine, got):
+    return pl.pallas_call(
+        sort_kernel,
+        out_shape=(shape(SWAP, WIDTH), shape(SWAP, WIDTH)),
+        in_specs=[HB, HB],
+        out_specs=(VM, VM),
+        scratch_shapes=[
+            pltpu.SMEM((8, WIDTH), I32),
+            pltpu.SMEM((8,), I32),
+            pltpu.SMEM((32,), I32),
+            pltpu.VMEM((8 * CHUNK, WIDTH), F32),
+            pltpu.SemaphoreType.DMA((9,)),
+        ],
+        compiler_params=params(12),
+        name="sort",
+    )(mine, got)
 
 
 def per_device(tracers, velocity, block_counts, land):
@@ -633,21 +718,39 @@
     ve = velocity.reshape(4, 4, WIDTH, WIDTH)
     swap = [(i, i ^ 1) for i in range(DEVICES)]
 
-    rims, codes, mine, picks, load = pl.pallas_call(
-        start_kernel,
-        out_shape=(shape(16 * EDGE, WIDTH), table_shape(64), table_shape(8), table_shape(8), table_shape(8)),
-        in_specs=[SM, VM, HB, HB],
-        out_specs=(VM, VM, VM, VM, VM),
+    grid, marks = pl.pallas_call(
+        ids_kernel,
+        out_shape=(table_shape(32), table_shape(8)),
+        in_specs=[HB, HB],
+        out_specs=(VM, VM),
         scratch_shapes=[
+            pltpu.SMEM((DEVICES,), I32),
+            pltpu.VMEM((ROWS, COLS), I32),
             pltpu.VMEM((32, WIDTH), I32),
-            pltpu.VMEM((4, 4, WIDTH, WIDTH), F32),
-            pltpu.VMEM((4, 4, WIDTH, WIDTH), F32),
-            pltpu.VMEM((WIDTH, WIDTH), F32),
             pltpu.SemaphoreType.DMA((2,)),
         ],
-        compiler_params=params(60),
-        name="start",
-    )(block_counts, land, tr, ve)
+        compiler_params=params(12),
+        cost_estimate=pl.CostEstimate(flops=2_000_000, bytes_accessed=100_000, transcendentals=0),
+        name="ids",
+    )(block_counts, land)
+    rims = pl.pallas_call(
+        rims_kernel,
+        out_shape=shape(16 * EDGE, WIDTH),
+        in_specs=[VM, VM],
+        out_specs=VM,
+        scratch_shapes=[pltpu.VMEM((WIDTH, WIDTH), F32)],
+        compiler_params=params(12),
+        name="rims",
+    )(tr, ve)
+    codes, mine, picks, load = pl.pallas_call(
+        tables_kernel,
+        out_shape=(table_shape(64), table_shape(8), table_shape(8), table_shape(8)),
+        in_specs=[VM],
+        out_specs=(VM, VM, VM, VM),
+        compiler_params=params(12),
+        cost_estimate=pl.CostEstimate(flops=2_000_000, bytes_accessed=100_000, transcendentals=0),
+        name="tables",
+    )(grid)
     other = permute(rims, swap)
     chip, message = pl.pallas_call(
         message_kernel,
@@ -655,27 +758,14 @@
         in_specs=[HB, VM, VM],
         out_specs=(VM, VM),
         scratch_shapes=[pltpu.SMEM((8, WIDTH), I32), pltpu.SemaphoreType.DMA((1,))],
-        compiler_params=params(16),
+        compiler_params=params(12),
         name="message",
-    )(mine, rims, other)
-    near = [permute(message, column_pairs(d)) for d in (1, 2, 3)]
+    )(marks, rims, other)
     corners = message[MSG_EDGES * EDGE :]
-    far = [permute(corners, column_pairs(d)) for d in (4, 5)]
-    chunks = pl.pallas_call(
-        pack_kernel,
-        out_shape=shape(8 * CHUNK, WIDTH),
-        in_specs=[HB] * 7,
-        out_specs=HB,
-        scratch_shapes=[
-            pltpu.SMEM((8, WIDTH), I32),
-            pltpu.VMEM((48, WIDTH), F32),
-            pltpu.VMEM((16, WIDTH), F32),
-            pltpu.SemaphoreType.DMA((15,)),
-            pltpu.SemaphoreType.DMA((1,)),
-        ],
-        compiler_params=params(16),
-        name="pack",
-    )(picks, message, *near, *far)
+    far = permute(corners, FAR_PAIRS)
+    near = [permute(message, NEAR_PAIRS), *[permute(message, column_pairs(d)) for d in (1, 2)]]
+    near = [near[1], near[2], near[0]]
+    chunks = pack(picks, message, near, (far, far))
     tr, ve, chunks = lax.optimization_barrier((tr, ve, chunks))
     tr_inner, ve_inner, inner_rims = pl.pallas_call(
         inner_kernel,
@@ -687,36 +777,28 @@
             pltpu.VMEM((10, 144, WIDTH), F32),
             pltpu.VMEM((WIDTH, WIDTH), F32),
         ],
-        compiler_params=params(32),
+        compiler_params=params(12),
         cost_estimate=pl.CostEstimate(flops=60_000_000, bytes_accessed=8_000_000, transcendentals=0),
         name="inner",
     )(mine, tr, ve)
     got = exchange_z(chunks.reshape(8, CHUNK, WIDTH)).reshape(8 * CHUNK, WIDTH)
     got, tr_inner, ve_inner, inner_rims = lax.optimization_barrier((got, tr_inner, ve_inner, inner_rims))
-    own, others = pl.pallas_call(
-        sort_kernel,
-        out_shape=(shape(SWAP, WIDTH), shape(SWAP, WIDTH)),
-        in_specs=[HB, VM],
-        out_specs=(VM, VM),
-        scratch_shapes=[
-            pltpu.SMEM((8, WIDTH), I32),
-            pltpu.SMEM((8,), I32),
-            pltpu.SMEM((32,), I32),
-            pltpu.SemaphoreType.DMA((1,)),
-        ],
-        compiler_params=params(16),
-        name="sort",
-    )(mine, got)
-
-    def second(args):
-        own, others, codes, mine, message, near = args
+    own, others = sort(mine, got)
+
+    def general(args):
+        _, _, codes, mine, picks, message, near = args
+        corners = message[MSG_EDGES * EDGE :]
+        near = [near[0], near[1], permute(message, column_pairs(3))]
+        chunks = pack(picks, message, near, [permute(corners, column_pairs(d)) for d in (4, 5)])
+        got = exchange_z(chunks.reshape(8, CHUNK, WIDTH)).reshape(8 * CHUNK, WIDTH)
+        own, others = sort(mine, got)
         down = (lax.axis_index("blk").astype(I32) & 1) == 1
         held = jnp.concatenate([message, *near])
         send = codes[:, :4].reshape(8, 32)
         rank = exclusive_count(send > 0)
         late = jnp.arange(CAP, CAP + MORE)
-        picks = jnp.sum(jnp.where((send > 0)[:, None] & (rank[:, None] == late[None, :, None]), send[:, None] - 1, 0), axis=-1)
-        rows = picks[:, :, None] * 8 + jnp.arange(EDGE, dtype=I32)
+        more = jnp.sum(jnp.where((send > 0)[:, None] & (rank[:, None] == late[None, :, None]), send[:, None] - 1, 0), axis=-1)
+        rows = more[:, :, None] * 8 + jnp.arange(EDGE, dtype=I32)
         more = exchange_z(held[rows].reshape(8, MORE * EDGE, WIDTH)).reshape(8 * MORE * EDGE, WIDTH)
         zed = mine[:, 4:8].reshape(32)
         i32 = jnp.arange(32)
@@ -730,7 +812,10 @@
         return jnp.concatenate([new[0], own[16 * EDGE :]]), jnp.concatenate([new[1], others[16 * EDGE :]])
 
     own, others = lax.cond(
-        load[0, 0] > CAP, second, lambda args: (args[0], args[1]), (own, others, codes, mine, message, near)
+        (load[0, 0] > CAP) | (load[0, 1] > 0),
+        general,
+        lambda args: (args[0], args[1]),
+        (own, others, codes, mine, picks, message, near),
     )
     theirs = permute(others, swap)
 
@@ -755,7 +840,7 @@
             pltpu.SemaphoreType.DMA((3,)),
             pltpu.SemaphoreType.DMA((8,)),
         ],
-        compiler_params=params(32),
+        compiler_params=params(12),
         name="final",
     )(mine, chip, own, theirs, rims, inner_rims, tr_inner, ve_inner)
     return tr_new.reshape(tracers.shape), ve_new.reshape(velocity.shape)

time: 58.9 us -> 52.8 us (0.90)
  the two profiles are of different devices: /device:TPU:1 before, /device:TPU:3 now
where the time goes in v4:
time: 52.8 us; the launch traced here: 52.5 us
  starting transfers between devices  17.3 us (33%)
  Pallas kernels  16.8 us (32%)
  waiting for transfers between devices  11.3 us (21%)
  local copies, waits for them, and re-layouts  5.01 us (9%)
  between operations  2.14 us (4%)
    ppermute x6, starting transfers between devices, permute(): return lax.ppermute(x, 'blk', pairs)  9.1 us
    all_to_all x1, starting transfers between devices, exchange_z(): return lax.all_to_all(x, 'blk', 0, 0, axis_index_groups=groups, tiled=True)  8.17 us
    all_to_all x1, waiting for transfers between devices, exchange_z(): return lax.all_to_all(x, 'blk', 0, 0, axis_index_groups=groups, tiled=True)  7.13 us
    pallas_call x1, Pallas kernels, per_device(): pl.pallas_call(inner_kernel, out_shape=(shape(4, 4, WIDTH, WIDTH), shape(...  5.02 us
    unnamed x28, local copies, waits for them, and re-layouts  4.43 us
    ppermute x6, waiting for transfers between devices, permute(): return lax.ppermute(x, 'blk', pairs)  4.17 us
    pallas_call x1, Pallas kernels, per_device(): pl.pallas_call(final_kernel, out_shape=(shape(4, 4, WIDTH, WIDTH), shape(...  4 us
    pallas_call x1, Pallas kernels, sort(): pl.pallas_call(sort_kernel, out_shape=(shape(SWAP, WIDTH), shape(SWAP, WI...  1.79 us
  transfers between devices with their start and end apart: 7, of which 3 were waited for; matrix products, arithmetic and copies ran while one was open for 1% of the time, Pallas kernels for 15%

profile of v4, /device:TPU:3, one launch (start us, length us, event | category | flops | bytes accessed | tf_op | source)
XLA Modules:
  0.0 52.5 jit_solution(3644565858585151357)
XLA Ops:
  0.6 0.0 copy-start
  0.6 1.2 %copy-done = f32[4,2,2,128,128]{4,3,2,1,0:T(8,128)S(1)} copy-done((f32[4,2,2,128,128]{4,3,2,1,0:T(8,128)S(1)}, f32[4,2,2,128,128]{4,3,2,1,0:T(8,128)}, u32[]{:S(2)}) %copy-start) | copy-done | bytes 1048600
  1.9 1.2 %copy-done.2 = f32[4,2,2,128,128]{4,3,2,1,0:T(8,128)S(1)} copy-done((f32[4,2,2,128,128]{4,3,2,1,0:T(8,128)S(1)}, f32[4,2,2,128,128]{4,3,2,1,0:T(8,128)}, u32[]{:S(2)}) %copy-start.2) | copy-done | bytes 1048600
  3.1 0.7 %rims.1.mine.edges = f32[256,128]{1,0:T(8,128)S(1)} custom-call(f32[4,4,128,128]{3,2,1,0:T(8,128)S(1)} %bitcast.23, f32[4,4,128,128]{3,2,1,0:T(8,128)S(1)} %bitcast.25), custom_call_target="tpu_custom_call" | custom-call | tf_op jit(solution)/shard_map/rims/pallas_call | solution.py:736
  3.8 0.8 %collective-permute-start.3 = (f32[256,128]{1,0:T(8,128)S(1)}, f32[256,128]{1,0:T(8,128)S(1)}, u32[]{:S(2)}, u32[]{:S(2)}) collective-permute-start(f32[256,128]{1,0:T(8,128)S(1)} %rims.1.mine.edges), channel_id=1, source_target_pairs={{0,1},{1,0},{2,3},{3,2},{4,5},{5,4},{6,7},{7,6},{8,9},{9,8},{10,11... | collective-permute-start | bytes 393224 | tf_op jit(solution)/shard_map/ppermute | solution.py:658
  4.5 1.6 %ids.1 = (s32[32,128]{1,0:T(8,128)S(1)}, s32[8,128]{1,0:T(8,128)S(1)}) custom-call(s32[256]{0:T(256)S(1)} %copy-done.9, s32[26,34]{1,0:T(8,128)S(1)} %copy-done.8), custom_call_target="tpu_custom_call" | custom-call | flops 2000000 | bytes 100000 | tf_op jit(solution)/shard_map/ids/pallas_call | solution.py:721
  6.2 0.6 %message.1 = (f32[512,128]{1,0:T(8,128)S(1)}, f32[296,128]{1,0:T(8,128)S(1)}) custom-call(s32[8,128]{1,0:T(8,128)S(1)} %get-tuple-element.50.table_hbm, f32[256,128]{1,0:T(8,128)S(1)} %rims.1.mine.edges, f32[256,128]{1,0:T(8,128)S(1)} %collective-permute-done.3.other), custom_call_target="tpu_custom_call" | custom-call | tf_op jit(solution)/shard_map/message/pallas_call | solution.py:755
  6.8 2.8 %collective-permute-start.4 = (f32[296,128]{1,0:T(8,128)S(1)}, f32[296,128]{1,0:T(8,128)S(1)}, u32[]{:S(2)}, u32[]{:S(2)}) collective-permute-start(f32[296,128]{1,0:T(8,128)S(1)} %get-tuple-element.54.m0), channel_id=1, source_target_pairs={{0,16},{1,0},{2,18},{3,2},{4,20},{5,4},{6,22},{7,6},{8,24},{9,8},{... | collective-permute-start | bytes 454664 | tf_op jit(solution)/shard_map/ppermute | solution.py:658
  9.6 0.4 collective-permute-start.5
  10.0 2.0 %collective-permute-start.6 = (f32[296,128]{1,0:T(8,128)S(1)}, f32[296,128]{1,0:T(8,128)S(1)}, u32[]{:S(2)}, u32[]{:S(2)}) collective-permute-start(f32[296,128]{1,0:T(8,128)S(1)} %get-tuple-element.54.m0), channel_id=1, source_target_pairs={{12,60},{14,62},{28,76},{30,78},{49,1},{51,3},{65,17},{67,19}} | collective-permute-start | bytes 454664 | tf_op jit(solution)/shard_map/ppermute | solution.py:658
  12.0 0.7 %collective-permute-start.7 = (f32[8,128]{1,0:T(8,128)S(1)}, f32[8,128]{1,0:T(8,128)S(1)}, u32[]{:S(2)}, u32[]{:S(2)}) collective-permute-start(f32[8,128]{1,0:T(8,128)S(1)} %slice.52), channel_id=1, source_target_pairs={{0,64},{67,3}} | collective-permute-start | bytes 12296 | tf_op jit(solution)/shard_map/ppermute | solution.py:658
  12.7 1.5 %tables.1 = (s32[64,128]{1,0:T(8,128)S(1)}, s32[8,128]{1,0:T(8,128)S(1)}, s32[8,128]{1,0:T(8,128)S(1)}, s32[8,128]{1,0:T(8,128)S(1)}) custom-call(s32[32,128]{1,0:T(8,128)S(1)} %get-tuple-element.48.grid), custom_call_target="tpu_custom_call" | custom-call | flops 2000000 | bytes 100000 | tf_op jit(solution)/shard_map/tables/pallas_call | solution.py:745
  14.2 3.0 %collective-permute-done.5.m2 = f32[296,128]{1,0:T(8,128)S(1)} collective-permute-done((f32[296,128]{1,0:T(8,128)S(1)}, f32[296,128]{1,0:T(8,128)S(1)}, u32[]{:S(2)}, u32[]{:S(2)}) %collective-permute-start.5) | collective-permute-done | bytes 151584 | tf_op jit(solution)/shard_map/ppermute | solution.py:658
  17.1 1.6 %pack.3 = f32[1024,128]{1,0:T(8,128)} custom-call(s32[8,128]{1,0:T(8,128)S(1)} %get-tuple-element.53.picks_hbm, f32[296,128]{1,0:T(8,128)S(1)} %get-tuple-element.54.m0, f32[296,128]{1,0:T(8,128)S(1)} %collective-permute-done.4.m1, f32[296,128]{1,0:T(8,128)S(1)} %collective-permute-done.5.m2, f32[296,128]{1,0:T(8,128)S(1)} %collective-permute-done.6.m3, ...), custom_call_target="tpu_custom_call" | custom-call | tf_op jit(solution)/shard_map/pack/pallas_call | solution.py:680
  18.8 8.2 %all-to-all-start.2 = ((f32[8,128,128]{2,1,0:T(8,128)}), f32[8,128,128]{2,1,0:T(8,128)S(1)}, u32[]{:S(2)}, u32[]{:S(2)}) async-start(f32[8,128,128]{2,1,0:T(8,128)} %bitcast.13), calls=%async_computation.2 | async-start | bytes 1048576 | tf_op jit(solution)/shard_map/all_to_all | solution.py:676
  26.9 0.6 %fusion.3 = (s32[1,1]{1,0:T(1,128)}, s32[1,1]{1,0:T(1,128)}) fusion(s32[8,128]{1,0:T(8,128)S(1)} %get-tuple-element.52), kind=kLoop, calls=%fused_computation.29 | loop fusion | bytes 16 | tf_op jit(solution)/shard_map/slice | solution.py:815
  28.8 5.0 %inner.1 = (f32[4,4,128,128]{3,2,1,0:T(8,128)S(1)}, f32[4,4,128,128]{3,2,1,0:T(8,128)S(1)}, f32[256,128]{1,0:T(8,128)S(1)}) custom-call(s32[8,128]{1,0:T(8,128)S(1)} %get-tuple-element.49.table.table_hbm, f32[4,4,128,128]{3,2,1,0:T(8,128)S(1)} %bitcast.24, f32[4,4,128,128]{3,2,1,0:T(8,128)S(1)} %bitcast.26), custom_call_target="tpu_custom_call" | custom-call | flops 60000000 | bytes 8000000 | tf_op jit(solution)/shard_map/inner/pallas_call | solution.py:770
  33.9 1.0 %copy-done.4 = f32[4,4,128,128]{3,2,1,0:T(8,128)} copy-done((f32[4,4,128,128]{3,2,1,0:T(8,128)}, f32[4,4,128,128]{3,2,1,0:T(8,128)S(1)}, u32[]{:S(2)}) %copy-start.4) | copy-done | bytes 1048600
  34.9 1.0 %copy-done.6 = f32[4,4,128,128]{3,2,1,0:T(8,128)} copy-done((f32[4,4,128,128]{3,2,1,0:T(8,128)}, f32[4,4,128,128]{3,2,1,0:T(8,128)S(1)}, u32[]{:S(2)}) %copy-start.6) | copy-done | bytes 1048600
  35.8 7.1 %all-to-all-done.2 = f32[8,128,128]{2,1,0:T(8,128)S(1)} async-done(((f32[8,128,128]{2,1,0:T(8,128)}), f32[8,128,128]{2,1,0:T(8,128)S(1)}, u32[]{:S(2)}, u32[]{:S(2)}) %all-to-all-start.2) | async-done | bytes 524320 | tf_op jit(solution)/shard_map/all_to_all | solution.py:676
  43.0 1.8 %sort.3 = (f32[264,128]{1,0:T(8,128)}, f32[264,128]{1,0:T(8,128)}) custom-call(s32[8,128]{1,0:T(8,128)S(1)} %get-tuple-element.49.table.table_hbm, f32[1024,128]{1,0:T(8,128)S(1)} %bitcast.28), custom_call_target="tpu_custom_call" | custom-call | tf_op jit(solution)/shard_map/sort/pallas_call | solution.py:699
  44.8 2.5 %collective-permute-start.8 = (f32[264,128]{1,0:T(8,128)}, f32[264,128]{1,0:T(8,128)S(1)}, u32[]{:S(2)}, u32[]{:S(2)}) collective-permute-start(f32[264,128]{1,0:T(8,128)} %get-tuple-element.64), channel_id=1, source_target_pairs={{0,1},{1,0},{2,3},{3,2},{4,5},{5,4},{6,7},{7,6},{8,9},{9,8},{10,11... | collective-permute-start | bytes 405512 | tf_op jit(solution)/shard_map/ppermute | solution.py:658
  47.3 1.2 %collective-permute-done.8.other = f32[264,128]{1,0:T(8,128)S(1)} collective-permute-done((f32[264,128]{1,0:T(8,128)}, f32[264,128]{1,0:T(8,128)S(1)}, u32[]{:S(2)}, u32[]{:S(2)}) %collective-permute-start.8) | collective-permute-done | bytes 135200 | tf_op jit(solution)/shard_map/ppermute | solution.py:658
  48.5 4.0 %final.1 = (f32[4,4,128,128]{3,2,1,0:T(8,128)}, f32[4,4,128,128]{3,2,1,0:T(8,128)}) custom-call(s32[8,128]{1,0:T(8,128)S(1)} %get-tuple-element.49.table.table_hbm, f32[512,128]{1,0:T(8,128)S(1)} %get-tuple-element.51.chip, f32[264,128]{1,0:T(8,128)} %get-tuple-element.63.own, f32[264,128]{1,0:T(8,128)S(1)} %collective-permute-done.8.other, ...), custom_call_target="tpu_custom_call" | custom-call | tf_op jit(solution)/shard_map/final/pallas_call | solution.py:822
  (29 shorter events, 0.1 us)
Async XLA Ops:
  0.6 1.2 %copy-start = (f32[4,2,2,128,128]{4,3,2,1,0:T(8,128)S(1)}, f32[4,2,2,128,128]{4,3,2,1,0:T(8,128)}, u32[]{:S(2)}) copy-start(f32[4,2,2,128,128]{4,3,2,1,0:T(8,128)} %param.6) | copy-start | bytes 3145732
  1.9 1.2 %copy-start.2 = (f32[4,2,2,128,128]{4,3,2,1,0:T(8,128)S(1)}, f32[4,2,2,128,128]{4,3,2,1,0:T(8,128)}, u32[]{:S(2)}) copy-start(f32[4,2,2,128,128]{4,3,2,1,0:T(8,128)} %param.7) | copy-start | bytes 3145732
  3.1 1.5 %copy-start.8 = (s32[26,34]{1,0:T(8,128)S(1)}, s32[26,34]{1,0:T(8,128)}, u32[]{:S(2)}) copy-start(s32[26,34]{1,0:T(8,128)} %land_hbm.1) | copy-start | bytes 10612
  3.1 1.5 %copy-start.9 = (s32[256]{0:T(256)S(1)}, s32[256]{0:T(256)}, u32[]{:S(2)}) copy-start(s32[256]{0:T(256)} %counts_hbm.1) | copy-start | bytes 3076
  3.8 2.4 %collective-permute-start.3 = (f32[256,128]{1,0:T(8,128)S(1)}, f32[256,128]{1,0:T(8,128)S(1)}, u32[]{:S(2)}, u32[]{:S(2)}) collective-permute-start(f32[256,128]{1,0:T(8,128)S(1)} %rims.1.mine.edges), channel_id=1, source_target_pairs={{0,1},{1,0},{2,3},{3,2},{4,5},{5,4},{6,7},{7,6},{8,9},{9,8},{10,11... | collective-permute-start | bytes 393224 | tf_op jit(solution)/shard_map/ppermute | solution.py:658
  6.8 7.3 %collective-permute-start.4 = (f32[296,128]{1,0:T(8,128)S(1)}, f32[296,128]{1,0:T(8,128)S(1)}, u32[]{:S(2)}, u32[]{:S(2)}) collective-permute-start(f32[296,128]{1,0:T(8,128)S(1)} %get-tuple-element.54.m0), channel_id=1, source_target_pairs={{0,16},{1,0},{2,18},{3,2},{4,20},{5,4},{6,22},{7,6},{8,24},{9,8},{... | collective-permute-start | bytes 454664 | tf_op jit(solution)/shard_map/ppermute | solution.py:658
  9.6 7.5 %collective-permute-start.5 = (f32[296,128]{1,0:T(8,128)S(1)}, f32[296,128]{1,0:T(8,128)S(1)}, u32[]{:S(2)}, u32[]{:S(2)}) collective-permute-start(f32[296,128]{1,0:T(8,128)S(1)} %get-tuple-element.54.m0), channel_id=1, source_target_pairs={{0,32},{1,0},{2,34},{3,2},{4,36},{5,4},{6,38},{7,6},{8,40},{9,8},{... | collective-permute-start | bytes 454664 | tf_op jit(solution)/shard_map/ppermute | solution.py:658
  10.0 7.2 %collective-permute-start.6 = (f32[296,128]{1,0:T(8,128)S(1)}, f32[296,128]{1,0:T(8,128)S(1)}, u32[]{:S(2)}, u32[]{:S(2)}) collective-permute-start(f32[296,128]{1,0:T(8,128)S(1)} %get-tuple-element.54.m0), channel_id=1, source_target_pairs={{12,60},{14,62},{28,76},{30,78},{49,1},{51,3},{65,17},{67,19}} | collective-permute-start | bytes 454664 | tf_op jit(solution)/shard_map/ppermute | solution.py:658
  12.0 2.1 %collective-permute-start.7 = (f32[8,128]{1,0:T(8,128)S(1)}, f32[8,128]{1,0:T(8,128)S(1)}, u32[]{:S(2)}, u32[]{:S(2)}) collective-permute-start(f32[8,128]{1,0:T(8,128)S(1)} %slice.52), channel_id=1, source_target_pairs={{0,64},{67,3}} | collective-permute-start | bytes 12296 | tf_op jit(solution)/shard_map/ppermute | solution.py:658
  14.2 4.6 %copy-start.10 = (f32[296,128]{1,0:T(8,128)}, f32[296,128]{1,0:T(8,128)S(1)}, u32[]{:S(2)}) copy-start(f32[296,128]{1,0:T(8,128)S(1)} %collective-permute-done.4.m1) | copy-start | bytes 454660
  17.1 1.6 %copy-start.13 = (f32[296,128]{1,0:T(8,128)}, f32[296,128]{1,0:T(8,128)S(1)}, u32[]{:S(2)}) copy-start(f32[296,128]{1,0:T(8,128)S(1)} %collective-permute-done.5.m2) | copy-start | bytes 454660
  17.1 11.7 %copy-start.1 = (f32[4,2,2,128,128]{4,3,2,1,0:T(8,128)S(1)}, f32[4,2,2,128,128]{4,3,2,1,0:T(8,128)}, u32[]{:S(2)}) copy-start(f32[4,2,2,128,128]{4,3,2,1,0:T(8,128)} %param.6) | copy-start | bytes 3145732
  17.1 11.7 %copy-start.3 = (f32[4,2,2,128,128]{4,3,2,1,0:T(8,128)S(1)}, f32[4,2,2,128,128]{4,3,2,1,0:T(8,128)}, u32[]{:S(2)}) copy-start(f32[4,2,2,128,128]{4,3,2,1,0:T(8,128)} %param.7) | copy-start | bytes 3145732
  18.8 24.2 %all-to-all-start.2 = ((f32[8,128,128]{2,1,0:T(8,128)}), f32[8,128,128]{2,1,0:T(8,128)S(1)}, u32[]{:S(2)}, u32[]{:S(2)}) async-start(f32[8,128,128]{2,1,0:T(8,128)} %bitcast.13), calls=%async_computation.2 | async-start | bytes 1048576 | tf_op jit(solution)/shard_map/all_to_all | solution.py:676
  33.9 1.0 %copy-start.4 = (f32[4,4,128,128]{3,2,1,0:T(8,128)}, f32[4,4,128,128]{3,2,1,0:T(8,128)S(1)}, u32[]{:S(2)}) copy-start(f32[4,4,128,128]{3,2,1,0:T(8,128)S(1)} %get-tuple-element.66.tr) | copy-start | bytes 3145732
  34.8 1.0 %copy-start.6 = (f32[4,4,128,128]{3,2,1,0:T(8,128)}, f32[4,4,128,128]{3,2,1,0:T(8,128)S(1)}, u32[]{:S(2)}) copy-start(f32[4,4,128,128]{3,2,1,0:T(8,128)S(1)} %get-tuple-element.67.ve) | copy-start | bytes 3145732
  43.0 1.8 %copy-start.11 = (f32[296,128]{1,0:T(8,128)S(1)}, f32[296,128]{1,0:T(8,128)}, u32[]{:S(2)}) copy-start(f32[296,128]{1,0:T(8,128)} %copy-done.10) | copy-start | bytes 454660
  43.0 1.8 %copy-start.14 = (f32[296,128]{1,0:T(8,128)S(1)}, f32[296,128]{1,0:T(8,128)}, u32[]{:S(2)}) copy-start(f32[296,128]{1,0:T(8,128)} %copy-done.13) | copy-start | bytes 454660
  44.8 3.8 %copy-start.5 = (f32[4,4,128,128]{3,2,1,0:T(8,128)S(1)}, f32[4,4,128,128]{3,2,1,0:T(8,128)}, u32[]{:S(2)}) copy-start(f32[4,4,128,128]{3,2,1,0:T(8,128)} %copy-done.4) | copy-start | bytes 3145732
  44.8 3.8 %copy-start.7 = (f32[4,4,128,128]{3,2,1,0:T(8,128)S(1)}, f32[4,4,128,128]{3,2,1,0:T(8,128)}, u32[]{:S(2)}) copy-start(f32[4,4,128,128]{3,2,1,0:T(8,128)} %copy-done.6) | copy-start | bytes 3145732
  44.8 3.7 %collective-permute-start.8 = (f32[264,128]{1,0:T(8,128)}, f32[264,128]{1,0:T(8,128)S(1)}, u32[]{:S(2)}, u32[]{:S(2)}) collective-permute-start(f32[264,128]{1,0:T(8,128)} %get-tuple-element.64), channel_id=1, source_target_pairs={{0,1},{1,0},{2,3},{3,2},{4,5},{5,4},{6,7},{7,6},{8,9},{9,8},{10,11... | collective-permute-start | bytes 405512 | tf_op jit(solution)/shard_map/ppermute | solution.py:658

commit v5 on v4

--- a/solution.py
+++ b/solution.py
@@ -84,7 +84,7 @@
     marks[...] = jnp.where(lane8 == 0, last, jnp.where(lane8 == 1, first_col, last_col)).astype(I32)
 
 
-def tables_kernel(grid, codes, mine, picks, load):
+def tables_kernel(grid, codes, mine, picks, enough):
     me = lax.axis_index("blk").astype(I32)
     column, zed, core = me >> 4, (me >> 1) & 7, me & 1
     ids = grid[...].astype(F32)
@@ -119,7 +119,6 @@
         is_chip = (chip[r : r + 1, :] == i).astype(jnp.bfloat16)
         of_kind = sum((kinds[k][r : r + 1, :] == kind_row).astype(F32) for k in range(4)).astype(jnp.bfloat16)
         counted += lax.dot_general(is_chip, of_kind, (((1,), (1,)), ((), ())), preferred_element_type=F32)
-    load[...] = jnp.broadcast_to(jnp.max(counted), (8, WIDTH)).astype(I32)
     home = jnp.right_shift(chip, 3)
     beyond = zero
     for x in near:
@@ -131,8 +130,7 @@
         reached |= (gap == -3) & (column_s <= 4) & (z_s <= 1)
         reached |= ((gap == 4) & (source == 0)) | ((gap == -4) & (source == 33))
         beyond = jnp.where(sea & (source >= 0) & ~reached, 1, beyond)
-    missed = jnp.broadcast_to(jnp.max(beyond.astype(F32)), (8, WIDTH)).astype(I32)
-    load[...] = jnp.where(lane_iota(8) == 1, missed, load[...])
+    enough[0] = ((jnp.max(counted) < CAP + 0.5) & (jnp.max(beyond.astype(F32)) < 0.5)).astype(I32)
 
     slot = row_iota(64)
     want = (column * 64 + slot).astype(F32)
@@ -713,7 +711,28 @@
     )(mine, got)
 
 
-def per_device(tracers, velocity, block_counts, land):
+def second_round(own, others, codes, mine, message, near):
+    down = (lax.axis_index("blk").astype(I32) & 1) == 1
+    held = jnp.concatenate([message, *near])
+    send = codes[:, :4].reshape(8, 32)
+    rank = exclusive_count(send > 0)
+    late = jnp.arange(CAP, CAP + MORE)
+    more = jnp.sum(jnp.where((send > 0)[:, None] & (rank[:, None] == late[None, :, None]), send[:, None] - 1, 0), axis=-1)
+    rows = more[:, :, None] * 8 + jnp.arange(EDGE, dtype=I32)
+    more = exchange_z(held[rows].reshape(8, MORE * EDGE, WIDTH)).reshape(8 * MORE * EDGE, WIDTH)
+    zed = mine[:, 4:8].reshape(32)
+    i32 = jnp.arange(32)
+    rank = jnp.sum((zed[None] >= 0) & (zed[None] == zed[:, None]) & (i32[None] < i32[:, None]), axis=1).astype(I32)
+    late = (zed >= 0) & (rank >= CAP)
+    start = jnp.where(late, zed * (MORE * EDGE) + (rank - CAP) * EDGE, 0)
+    start, late = [jnp.where(down, jnp.concatenate([x[16:], x[:16]]), x) for x in (start, late)]
+    new = more[start[:, None] + jnp.arange(EDGE, dtype=I32)]
+    old = jnp.stack([own[: 16 * EDGE], others[: 16 * EDGE]]).reshape(32, EDGE, WIDTH)
+    new = jnp.where(late[:, None, None], new, old).reshape(2, 16 * EDGE, WIDTH)
+    return jnp.concatenate([new[0], own[16 * EDGE :]]), jnp.concatenate([new[1], others[16 * EDGE :]])
+
+
+def run(tracers, velocity, block_counts, land, usual):
     tr = tracers.reshape(4, 4, WIDTH, WIDTH)
     ve = velocity.reshape(4, 4, WIDTH, WIDTH)
     swap = [(i, i ^ 1) for i in range(DEVICES)]
@@ -742,11 +761,11 @@
         compiler_params=params(12),
         name="rims",
     )(tr, ve)
-    codes, mine, picks, load = pl.pallas_call(
+    codes, mine, picks, enough = pl.pallas_call(
         tables_kernel,
-        out_shape=(table_shape(64), table_shape(8), table_shape(8), table_shape(8)),
+        out_shape=(table_shape(64), table_shape(8), table_shape(8), jax.ShapeDtypeStruct((1,), I32)),
         in_specs=[VM],
-        out_specs=(VM, VM, VM, VM),
+        out_specs=(VM, VM, VM, SM),
         compiler_params=params(12),
         cost_estimate=pl.CostEstimate(flops=2_000_000, bytes_accessed=100_000, transcendentals=0),
         name="tables",
@@ -762,10 +781,15 @@
         name="message",
     )(marks, rims, other)
     corners = message[MSG_EDGES * EDGE :]
-    far = permute(corners, FAR_PAIRS)
-    near = [permute(message, NEAR_PAIRS), *[permute(message, column_pairs(d)) for d in (1, 2)]]
-    near = [near[1], near[2], near[0]]
-    chunks = pack(picks, message, near, (far, far))
+    if usual:
+        far = permute(corners, FAR_PAIRS)
+        far = (far, far)
+        near = [permute(message, NEAR_PAIRS), *[permute(message, column_pairs(d)) for d in (1, 2)]]
+        near = [near[1], near[2], near[0]]
+    else:
+        far = [permute(corners, column_pairs(d)) for d in (4, 5)]
+        near = [permute(message, column_pairs(d)) for d in (1, 2, 3)]
+    chunks = pack(picks, message, near, far)
     tr, ve, chunks = lax.optimization_barrier((tr, ve, chunks))
     tr_inner, ve_inner, inner_rims = pl.pallas_call(
         inner_kernel,
@@ -784,39 +808,8 @@
     got = exchange_z(chunks.reshape(8, CHUNK, WIDTH)).reshape(8 * CHUNK, WIDTH)
     got, tr_inner, ve_inner, inner_rims = lax.optimization_barrier((got, tr_inner, ve_inner, inner_rims))
     own, others = sort(mine, got)
-
-    def general(args):
-        _, _, codes, mine, picks, message, near = args
-        corners = message[MSG_EDGES * EDGE :]
-        near = [near[0], near[1], permute(message, column_pairs(3))]
-        chunks = pack(picks, message, near, [permute(corners, column_pairs(d)) for d in (4, 5)])
-        got = exchange_z(chunks.reshape(8, CHUNK, WIDTH)).reshape(8 * CHUNK, WIDTH)
-        own, others = sort(mine, got)
-        down = (lax.axis_index("blk").astype(I32) & 1) == 1
-        held = jnp.concatenate([message, *near])
-        send = codes[:, :4].reshape(8, 32)
-        rank = exclusive_count(send > 0)
-        late = jnp.arange(CAP, CAP + MORE)
-        more = jnp.sum(jnp.where((send > 0)[:, None] & (rank[:, None] == late[None, :, None]), send[:, None] - 1, 0), axis=-1)
-        rows = more[:, :, None] * 8 + jnp.arange(EDGE, dtype=I32)
-        more = exchange_z(held[rows].reshape(8, MORE * EDGE, WIDTH)).reshape(8 * MORE * EDGE, WIDTH)
-        zed = mine[:, 4:8].reshape(32)
-        i32 = jnp.arange(32)
-        rank = jnp.sum((zed[None] >= 0) & (zed[None] == zed[:, None]) & (i32[None] < i32[:, None]), axis=1).astype(I32)
-        late = (zed >= 0) & (rank >= CAP)
-        start = jnp.where(late, zed * (MORE * EDGE) + (rank - CAP) * EDGE, 0)
-        start, late = [jnp.where(down, jnp.concatenate([x[16:], x[:16]]), x) for x in (start, late)]
-        new = more[start[:, None] + jnp.arange(EDGE, dtype=I32)]
-        old = jnp.stack([own[: 16 * EDGE], others[: 16 * EDGE]]).reshape(32, EDGE, WIDTH)
-        new = jnp.where(late[:, None, None], new, old).reshape(2, 16 * EDGE, WIDTH)
-        return jnp.concatenate([new[0], own[16 * EDGE :]]), jnp.concatenate([new[1], others[16 * EDGE :]])
-
-    own, others = lax.cond(
-        (load[0, 0] > CAP) | (load[0, 1] > 0),
-        general,
-        lambda args: (args[0], args[1]),
-        (own, others, codes, mine, picks, message, near),
-    )
+    if not usual:
+        own, others = second_round(own, others, codes, mine, message, near)
     theirs = permute(others, swap)
 
     tr_new, ve_new = pl.pallas_call(
@@ -843,7 +836,16 @@
         compiler_params=params(12),
         name="final",
     )(mine, chip, own, theirs, rims, inner_rims, tr_inner, ve_inner)
-    return tr_new.reshape(tracers.shape), ve_new.reshape(velocity.shape)
+    return enough[0] != 0, tr_new.reshape(tracers.shape), ve_new.reshape(velocity.shape)
+
+
+def per_device(tracers, velocity, block_counts, land):
+    enough, *out = run(tracers, velocity, block_counts, land, True)
+
+    def again(out, args):
+        return run(*args, False)[1:]
+
+    return lax.cond(enough, lambda out, args: tuple(out), again, tuple(out), (tracers, velocity, block_counts, land))
 
 
 def solution(mesh):

time: 52.8 us -> 51.8 us (0.981)
  local copies, waits for them, and re-layouts: 5.01 us -> 0.02 us
  waiting for transfers between devices: 11.3 us -> 14 us
  Pallas kernels: 16.8 us -> 18.8 us
  between operations: 2.14 us -> 1.6 us
    all_to_all x1, waiting for transfers between devices: 7.13 us -> 11.9 us  [exchange_z(): return lax.all_to_all(x, 'blk', 0, 0, axis_index_groups=groups, tiled=True)]
    unnamed x28 -> x8, local copies, waits for them, and re-layouts: 4.43 us -> 0.02 us
    pallas_call x6, Pallas kernels: 13.4 us -> 16.2 us  [the longest x1 6.02 us: run(): pl.pallas_call(inner_kernel, out_shape=(shape(4, 4, WIDTH, WIDTH), shape(...]
    ppermute x6, waiting for transfers between devices: 4.17 us -> 2.03 us  [permute(): return lax.ppermute(x, 'blk', pairs)]
    pallas_call x1, Pallas kernels: 1.79 us -> 1.08 us  [sort(): pl.pallas_call(sort_kernel, out_shape=(shape(SWAP, WIDTH), shape(SWAP, WI...]
    ppermute x6, starting transfers between devices: 9.1 us -> 8.45 us  [permute(): return lax.ppermute(x, 'blk', pairs)]
    slice x2 -> x1, local copies, waits for them, and re-layouts: 0.58 us -> 0.01 us  [run(): corners = message[MSG_EDGES * EDGE:]]
  transfers between devices with their start and end apart: 7 -> 7, of which waited for: 3 -> 3; matrix products, arithmetic and copies ran while one was open for 1% -> 0% of each run, Pallas kernels for 15% -> 19%
where the time goes in v5:
time: 51.8 us; the launch traced here: 51.6 us
  Pallas kernels  18.8 us (36%)
  starting transfers between devices  16.9 us (33%)
  waiting for transfers between devices  14 us (27%)
  between operations  1.6 us (3%)
    all_to_all x1, waiting for transfers between devices, exchange_z(): return lax.all_to_all(x, 'blk', 0, 0, axis_index_groups=groups, tiled=True)  11.9 us
    ppermute x6, starting transfers between devices, permute(): return lax.ppermute(x, 'blk', pairs)  8.45 us
    all_to_all x1, starting transfers between devices, exchange_z(): return lax.all_to_all(x, 'blk', 0, 0, axis_index_groups=groups, tiled=True)  8.45 us
    pallas_call x1, Pallas kernels, run(): pl.pallas_call(inner_kernel, out_shape=(shape(4, 4, WIDTH, WIDTH), shape(...  6.02 us
    pallas_call x1, Pallas kernels, run(): pl.pallas_call(final_kernel, out_shape=(shape(4, 4, WIDTH, WIDTH), shape(...  3.6 us
    pallas_call x1, Pallas kernels, run(): pl.pallas_call(rims_kernel, out_shape=shape(16 * EDGE, WIDTH), in_specs=[...  2.29 us
    pallas_call x1, Pallas kernels, run(): pl.pallas_call(tables_kernel, out_shape=(table_shape(64), table_shape(8),...  2.08 us
    ppermute x6, waiting for transfers between devices, permute(): return lax.ppermute(x, 'blk', pairs)  2.03 us
  transfers between devices with their start and end apart: 7, of which 3 were waited for; matrix products, arithmetic and copies ran while one was open for 0% of the time, Pallas kernels for 19%

profile of v5, /device:TPU:3, one launch (start us, length us, event | category | flops | bytes accessed | tf_op | source)
XLA Modules:
  0.0 51.6 jit_solution(1096022172448367618)
XLA Ops:
  0.6 0.0 copy-start.4
  0.6 2.3 %rims.3.mine.edges = f32[256,128]{1,0:T(8,128)S(1)} custom-call(f32[4,4,128,128]{3,2,1,0:T(8,128)} %bitcast.27, f32[4,4,128,128]{3,2,1,0:T(8,128)} %bitcast.31), custom_call_target="tpu_custom_call" | custom-call | tf_op jit(solution)/shard_map/rims/pallas_call | solution.py:755
  2.9 0.8 %collective-permute-start.7 = (f32[256,128]{1,0:T(8,128)S(1)}, f32[256,128]{1,0:T(8,128)S(1)}, u32[]{:S(2)}, u32[]{:S(2)}) collective-permute-start(f32[256,128]{1,0:T(8,128)S(1)} %rims.3.mine.edges), channel_id=1, source_target_pairs={{0,1},{1,0},{2,3},{3,2},{4,5},{5,4},{6,7},{7,6},{8,9},{9,8},{10,11... | collective-permute-start | bytes 393224 | tf_op jit(solution)/shard_map/ppermute | solution.py:656
  3.7 1.6 %ids.3 = (s32[32,128]{1,0:T(8,128)S(1)}, s32[8,128]{1,0:T(8,128)S(1)}) custom-call(s32[256]{0:T(256)S(1)} %copy-done.5, s32[26,34]{1,0:T(8,128)S(1)} %copy-done.4), custom_call_target="tpu_custom_call" | custom-call | flops 2000000 | bytes 100000 | tf_op jit(solution)/shard_map/ids/pallas_call | solution.py:740
  5.3 0.0 collective-permute-done.7.other
  5.3 0.6 %message.3 = (f32[512,128]{1,0:T(8,128)S(1)}, f32[296,128]{1,0:T(8,128)S(1)}) custom-call(s32[8,128]{1,0:T(8,128)S(1)} %get-tuple-element.67.table_hbm, f32[256,128]{1,0:T(8,128)S(1)} %rims.3.mine.edges, f32[256,128]{1,0:T(8,128)S(1)} %collective-permute-done.7.other), custom_call_target="tpu_custom_call" | custom-call | tf_op jit(solution)/shard_map/message/pallas_call | solution.py:774
  6.0 3.2 %collective-permute-start.10 = (f32[296,128]{1,0:T(8,128)S(1)}, f32[296,128]{1,0:T(8,128)S(1)}, u32[]{:S(2)}, u32[]{:S(2)}) collective-permute-start(f32[296,128]{1,0:T(8,128)S(1)} %get-tuple-element.70.m0), channel_id=1, source_target_pairs={{12,60},{14,62},{28,76},{30,78},{49,1},{51,3},{65,17},{67,19}} | collective-permute-start | bytes 454664 | tf_op jit(solution)/shard_map/ppermute | solution.py:656
  9.2 0.5 collective-permute-start.9
  9.6 2.8 %collective-permute-start.8 = (f32[296,128]{1,0:T(8,128)S(1)}, f32[296,128]{1,0:T(8,128)S(1)}, u32[]{:S(2)}, u32[]{:S(2)}) collective-permute-start(f32[296,128]{1,0:T(8,128)S(1)} %get-tuple-element.70.m0), channel_id=1, source_target_pairs={{0,16},{1,0},{2,18},{3,2},{4,20},{5,4},{6,22},{7,6},{8,24},{9,8},{... | collective-permute-start | bytes 454664 | tf_op jit(solution)/shard_map/ppermute | solution.py:656
  12.5 0.6 %collective-permute-start.11 = (f32[8,128]{1,0:T(8,128)S(1)}, f32[8,128]{1,0:T(8,128)S(1)}, u32[]{:S(2)}, u32[]{:S(2)}) collective-permute-start(f32[8,128]{1,0:T(8,128)S(1)} %slice.44), channel_id=1, source_target_pairs={{0,64},{67,3}} | collective-permute-start | bytes 12296 | tf_op jit(solution)/shard_map/ppermute | solution.py:656
  13.1 2.1 %tables.3 = (s32[64,128]{1,0:T(8,128)}, s32[8,128]{1,0:T(8,128)S(1)}, s32[8,128]{1,0:T(8,128)S(1)}, s32[1]{0:T(128)}) custom-call(s32[32,128]{1,0:T(8,128)S(1)} %get-tuple-element.64.grid), custom_call_target="tpu_custom_call" | custom-call | flops 2000000 | bytes 100000 | tf_op jit(solution)/shard_map/tables/pallas_call | solution.py:764
  15.2 0.0 collective-permute-done.11.c4.c5
  15.2 0.0 collective-permute-done.10.m3
  15.2 1.7 %collective-permute-done.9.m2 = f32[296,128]{1,0:T(8,128)S(1)} collective-permute-done((f32[296,128]{1,0:T(8,128)S(1)}, f32[296,128]{1,0:T(8,128)S(1)}, u32[]{:S(2)}, u32[]{:S(2)}) %collective-permute-start.9) | collective-permute-done | bytes 151584 | tf_op jit(solution)/shard_map/ppermute | solution.py:656
  16.9 0.0 collective-permute-done.8.m1
  16.9 1.5 %pack.3 = f32[1024,128]{1,0:T(8,128)} custom-call(s32[8,128]{1,0:T(8,128)S(1)} %get-tuple-element.69.picks_hbm, f32[296,128]{1,0:T(8,128)S(1)} %get-tuple-element.70.m0, f32[296,128]{1,0:T(8,128)S(1)} %collective-permute-done.8.m1, f32[296,128]{1,0:T(8,128)S(1)} %collective-permute-done.9.m2, f32[296,128]{1,0:T(8,128)S(1)} %collective-permute-done.10.m3, ...), custom_call_target="tpu_custom_call" | custom-call | tf_op jit(solution)/shard_map/pack/pallas_call | solution.py:678
  18.4 8.4 %all-to-all-start.2 = ((f32[8,128,128]{2,1,0:T(8,128)}), f32[8,128,128]{2,1,0:T(8,128)S(1)}, u32[]{:S(2)}, u32[]{:S(2)}) async-start(f32[8,128,128]{2,1,0:T(8,128)} %bitcast.15), calls=%async_computation.2 | async-start | bytes 1048576 | tf_op jit(solution)/shard_map/all_to_all | solution.py:674
  26.9 6.0 %inner.3 = (f32[4,4,128,128]{3,2,1,0:T(8,128)S(1)}, f32[4,4,128,128]{3,2,1,0:T(8,128)S(1)}, f32[256,128]{1,0:T(8,128)S(1)}) custom-call(s32[8,128]{1,0:T(8,128)S(1)} %get-tuple-element.66.table.table_hbm, f32[4,4,128,128]{3,2,1,0:T(8,128)} %bitcast.28, f32[4,4,128,128]{3,2,1,0:T(8,128)} %bitcast.32), custom_call_target="tpu_custom_call" | custom-call | flops 60000000 | bytes 8000000 | tf_op jit(solution)/shard_map/inner/pallas_call | solution.py:794
  32.9 11.9 %all-to-all-done.2 = f32[8,128,128]{2,1,0:T(8,128)S(1)} async-done(((f32[8,128,128]{2,1,0:T(8,128)}), f32[8,128,128]{2,1,0:T(8,128)S(1)}, u32[]{:S(2)}, u32[]{:S(2)}) %all-to-all-start.2) | async-done | bytes 524320 | tf_op jit(solution)/shard_map/all_to_all | solution.py:674
  44.8 1.1 %sort.3 = (f32[264,128]{1,0:T(8,128)S(1)}, f32[264,128]{1,0:T(8,128)S(1)}) custom-call(s32[8,128]{1,0:T(8,128)S(1)} %get-tuple-element.66.table.table_hbm, f32[1024,128]{1,0:T(8,128)S(1)} %bitcast.26), custom_call_target="tpu_custom_call" | custom-call | tf_op jit(solution)/shard_map/sort/pallas_call | solution.py:697
  45.9 0.6 %collective-permute-start.12 = (f32[264,128]{1,0:T(8,128)S(1)}, f32[264,128]{1,0:T(8,128)S(1)}, u32[]{:S(2)}, u32[]{:S(2)}) collective-permute-start(f32[264,128]{1,0:T(8,128)S(1)} %get-tuple-element.79), channel_id=1, source_target_pairs={{0,1},{1,0},{2,3},{3,2},{4,5},{5,4},{6,7},{7,6},{8,9},{9,8},{10,11... | collective-permute-start | bytes 405512 | tf_op jit(solution)/shard_map/ppermute | solution.py:656
  47.2 0.3 collective-permute-done.12.other
  47.5 3.6 %final.3 = (f32[4,4,128,128]{3,2,1,0:T(8,128)}, f32[4,4,128,128]{3,2,1,0:T(8,128)}) custom-call(s32[8,128]{1,0:T(8,128)S(1)} %get-tuple-element.66.table.table_hbm, f32[512,128]{1,0:T(8,128)S(1)} %get-tuple-element.68.chip, f32[264,128]{1,0:T(8,128)S(1)} %get-tuple-element.78.own, f32[264,128]{1,0:T(8,128)S(1)} %collective-permute-done.12.other, ...), custom_call_target="tpu_custom_call" | custom-call | tf_op jit(solution)/shard_map/final/pallas_call | solution.py:815
  51.1 0.2 conditional.1
  (8 shorter events, 0.0 us)
Async XLA Ops:
  0.6 3.1 %copy-start.4 = (s32[26,34]{1,0:T(8,128)S(1)}, s32[26,34]{1,0:T(8,128)}, u32[]{:S(2)}) copy-start(s32[26,34]{1,0:T(8,128)} %land_hbm.1) | copy-start | bytes 10612
  0.6 3.1 %copy-start.5 = (s32[256]{0:T(256)S(1)}, s32[256]{0:T(256)}, u32[]{:S(2)}) copy-start(s32[256]{0:T(256)} %counts_hbm.1) | copy-start | bytes 3076
  2.9 2.4 %collective-permute-start.7 = (f32[256,128]{1,0:T(8,128)S(1)}, f32[256,128]{1,0:T(8,128)S(1)}, u32[]{:S(2)}, u32[]{:S(2)}) collective-permute-start(f32[256,128]{1,0:T(8,128)S(1)} %rims.3.mine.edges), channel_id=1, source_target_pairs={{0,1},{1,0},{2,3},{3,2},{4,5},{5,4},{6,7},{7,6},{8,9},{9,8},{10,11... | collective-permute-start | bytes 393224 | tf_op jit(solution)/shard_map/ppermute | solution.py:656
  6.0 9.2 %collective-permute-start.10 = (f32[296,128]{1,0:T(8,128)S(1)}, f32[296,128]{1,0:T(8,128)S(1)}, u32[]{:S(2)}, u32[]{:S(2)}) collective-permute-start(f32[296,128]{1,0:T(8,128)S(1)} %get-tuple-element.70.m0), channel_id=1, source_target_pairs={{12,60},{14,62},{28,76},{30,78},{49,1},{51,3},{65,17},{67,19}} | collective-permute-start | bytes 454664 | tf_op jit(solution)/shard_map/ppermute | solution.py:656
  9.2 7.7 %collective-permute-start.9 = (f32[296,128]{1,0:T(8,128)S(1)}, f32[296,128]{1,0:T(8,128)S(1)}, u32[]{:S(2)}, u32[]{:S(2)}) collective-permute-start(f32[296,128]{1,0:T(8,128)S(1)} %get-tuple-element.70.m0), channel_id=1, source_target_pairs={{0,32},{1,0},{2,34},{3,2},{4,36},{5,4},{6,38},{7,6},{8,40},{9,8},{... | collective-permute-start | bytes 454664 | tf_op jit(solution)/shard_map/ppermute | solution.py:656
  9.6 7.3 %collective-permute-start.8 = (f32[296,128]{1,0:T(8,128)S(1)}, f32[296,128]{1,0:T(8,128)S(1)}, u32[]{:S(2)}, u32[]{:S(2)}) collective-permute-start(f32[296,128]{1,0:T(8,128)S(1)} %get-tuple-element.70.m0), channel_id=1, source_target_pairs={{0,16},{1,0},{2,18},{3,2},{4,20},{5,4},{6,22},{7,6},{8,24},{9,8},{... | collective-permute-start | bytes 454664 | tf_op jit(solution)/shard_map/ppermute | solution.py:656
  12.5 2.7 %collective-permute-start.11 = (f32[8,128]{1,0:T(8,128)S(1)}, f32[8,128]{1,0:T(8,128)S(1)}, u32[]{:S(2)}, u32[]{:S(2)}) collective-permute-start(f32[8,128]{1,0:T(8,128)S(1)} %slice.44), channel_id=1, source_target_pairs={{0,64},{67,3}} | collective-permute-start | bytes 12296 | tf_op jit(solution)/shard_map/ppermute | solution.py:656
  18.4 26.4 %all-to-all-start.2 = ((f32[8,128,128]{2,1,0:T(8,128)}), f32[8,128,128]{2,1,0:T(8,128)S(1)}, u32[]{:S(2)}, u32[]{:S(2)}) async-start(f32[8,128,128]{2,1,0:T(8,128)} %bitcast.15), calls=%async_computation.2 | async-start | bytes 1048576 | tf_op jit(solution)/shard_map/all_to_all | solution.py:674
  45.9 1.6 %collective-permute-start.12 = (f32[264,128]{1,0:T(8,128)S(1)}, f32[264,128]{1,0:T(8,128)S(1)}, u32[]{:S(2)}, u32[]{:S(2)}) collective-permute-start(f32[264,128]{1,0:T(8,128)S(1)} %get-tuple-element.79), channel_id=1, source_target_pairs={{0,1},{1,0},{2,3},{3,2},{4,5},{5,4},{6,7},{7,6},{8,9},{9,8},{10,11... | collective-permute-start | bytes 405512 | tf_op jit(solution)/shard_map/ppermute | solution.py:656
  47.5 3.6 %copy-start = (f32[4,2,2,128,128]{4,3,2,1,0:T(8,128)S(1)}, f32[4,2,2,128,128]{4,3,2,1,0:T(8,128)}, u32[]{:S(2)}) copy-start(f32[4,2,2,128,128]{4,3,2,1,0:T(8,128)} %param.6) | copy-start | bytes 3145732
  47.5 3.6 %copy-start.2 = (f32[4,2,2,128,128]{4,3,2,1,0:T(8,128)S(1)}, f32[4,2,2,128,128]{4,3,2,1,0:T(8,128)}, u32[]{:S(2)}) copy-start(f32[4,2,2,128,128]{4,3,2,1,0:T(8,128)} %param.7) | copy-start | bytes 3145732

commit v6 on v5

--- a/solution.py
+++ b/solution.py
@@ -631,10 +631,11 @@
             for ring, rr in ((0, r0), (1, r1)):
                 res[slot, k, pl.ds(ring, 1), :] = rr[0, q, pl.ds(slot * 2 + 1, 1), :]
                 res[slot, k, pl.ds(WIDTH - 1 - ring, 1), :] = rr[0, q, pl.ds(slot * 2, 1), :]
-        for i, (res, out) in enumerate(((res_t, tr_out), (res_v, ve_out))):
-            copy = pltpu.make_async_copy(res.at[slot], out.at[slot], sent.at[slot * 2 + i])
-            copy.start()
-            out_copies.append(copy)
+            if k == 3:
+                out = tr_out if q < 4 else ve_out
+                copy = pltpu.make_async_copy(res.at[slot], out.at[slot], sent.at[slot * 2 + q // 4])
+                copy.start()
+                out_copies.append(copy)
     for copy in out_copies:
         copy.wait()
 

time: 51.8 us -> 51.8 us (level)
  no operation moved by 1% of the time
where the time goes in v6:
time: 51.8 us; the launch traced here: 51.5 us
  Pallas kernels  18.9 us (36%)
  starting transfers between devices  16.8 us (32%)
  waiting for transfers between devices  14 us (27%)
  between operations  1.6 us (3%)
    all_to_all x1, waiting for transfers between devices, exchange_z(): return lax.all_to_all(x, 'blk', 0, 0, axis_index_groups=groups, tiled=True)  11.9 us
    ppermute x6, starting transfers between devices, permute(): return lax.ppermute(x, 'blk', pairs)  8.45 us
    all_to_all x1, starting transfers between devices, exchange_z(): return lax.all_to_all(x, 'blk', 0, 0, axis_index_groups=groups, tiled=True)  8.38 us
    pallas_call x1, Pallas kernels, run(): pl.pallas_call(inner_kernel, out_shape=(shape(4, 4, WIDTH, WIDTH), shape(...  6.02 us
    pallas_call x1, Pallas kernels, run(): pl.pallas_call(final_kernel, out_shape=(shape(4, 4, WIDTH, WIDTH), shape(...  3.6 us
    pallas_call x1, Pallas kernels, run(): pl.pallas_call(rims_kernel, out_shape=shape(16 * EDGE, WIDTH), in_specs=[...  2.29 us
    pallas_call x1, Pallas kernels, run(): pl.pallas_call(tables_kernel, out_shape=(table_shape(64), table_shape(8),...  2.08 us
    ppermute x6, waiting for transfers between devices, permute(): return lax.ppermute(x, 'blk', pairs)  2.03 us
  transfers between devices with their start and end apart: 7, of which 3 were waited for; matrix products, arithmetic and copies ran while one was open for 0% of the time, Pallas kernels for 19%

profile of v6, /device:TPU:3, one launch (start us, length us, event | category | flops | bytes accessed | tf_op | source)
XLA Modules:
  0.0 51.5 jit_solution(1096022172448367618)
XLA Ops:
  0.6 0.0 copy-start.4
  0.6 2.3 %rims.3.mine.edges = f32[256,128]{1,0:T(8,128)S(1)} custom-call(f32[4,4,128,128]{3,2,1,0:T(8,128)} %bitcast.27, f32[4,4,128,128]{3,2,1,0:T(8,128)} %bitcast.31), custom_call_target="tpu_custom_call" | custom-call | tf_op jit(solution)/shard_map/rims/pallas_call | solution.py:756
  2.9 0.8 %collective-permute-start.7 = (f32[256,128]{1,0:T(8,128)S(1)}, f32[256,128]{1,0:T(8,128)S(1)}, u32[]{:S(2)}, u32[]{:S(2)}) collective-permute-start(f32[256,128]{1,0:T(8,128)S(1)} %rims.3.mine.edges), channel_id=1, source_target_pairs={{0,1},{1,0},{2,3},{3,2},{4,5},{5,4},{6,7},{7,6},{8,9},{9,8},{10,11... | collective-permute-start | bytes 393224 | tf_op jit(solution)/shard_map/ppermute | solution.py:657
  3.7 1.6 %ids.3 = (s32[32,128]{1,0:T(8,128)S(1)}, s32[8,128]{1,0:T(8,128)S(1)}) custom-call(s32[256]{0:T(256)S(1)} %copy-done.5, s32[26,34]{1,0:T(8,128)S(1)} %copy-done.4), custom_call_target="tpu_custom_call" | custom-call | flops 2000000 | bytes 100000 | tf_op jit(solution)/shard_map/ids/pallas_call | solution.py:741
  5.3 0.0 collective-permute-done.7.other
  5.3 0.6 %message.3 = (f32[512,128]{1,0:T(8,128)S(1)}, f32[296,128]{1,0:T(8,128)S(1)}) custom-call(s32[8,128]{1,0:T(8,128)S(1)} %get-tuple-element.67.table_hbm, f32[256,128]{1,0:T(8,128)S(1)} %rims.3.mine.edges, f32[256,128]{1,0:T(8,128)S(1)} %collective-permute-done.7.other), custom_call_target="tpu_custom_call" | custom-call | tf_op jit(solution)/shard_map/message/pallas_call | solution.py:775
  6.0 3.2 %collective-permute-start.10 = (f32[296,128]{1,0:T(8,128)S(1)}, f32[296,128]{1,0:T(8,128)S(1)}, u32[]{:S(2)}, u32[]{:S(2)}) collective-permute-start(f32[296,128]{1,0:T(8,128)S(1)} %get-tuple-element.70.m0), channel_id=1, source_target_pairs={{12,60},{14,62},{28,76},{30,78},{49,1},{51,3},{65,17},{67,19}} | collective-permute-start | bytes 454664 | tf_op jit(solution)/shard_map/ppermute | solution.py:657
  9.2 0.5 collective-permute-start.9
  9.6 2.8 %collective-permute-start.8 = (f32[296,128]{1,0:T(8,128)S(1)}, f32[296,128]{1,0:T(8,128)S(1)}, u32[]{:S(2)}, u32[]{:S(2)}) collective-permute-start(f32[296,128]{1,0:T(8,128)S(1)} %get-tuple-element.70.m0), channel_id=1, source_target_pairs={{0,16},{1,0},{2,18},{3,2},{4,20},{5,4},{6,22},{7,6},{8,24},{9,8},{... | collective-permute-start | bytes 454664 | tf_op jit(solution)/shard_map/ppermute | solution.py:657
  12.5 0.6 %collective-permute-start.11 = (f32[8,128]{1,0:T(8,128)S(1)}, f32[8,128]{1,0:T(8,128)S(1)}, u32[]{:S(2)}, u32[]{:S(2)}) collective-permute-start(f32[8,128]{1,0:T(8,128)S(1)} %slice.44), channel_id=1, source_target_pairs={{0,64},{67,3}} | collective-permute-start | bytes 12296 | tf_op jit(solution)/shard_map/ppermute | solution.py:657
  13.1 2.1 %tables.3 = (s32[64,128]{1,0:T(8,128)}, s32[8,128]{1,0:T(8,128)S(1)}, s32[8,128]{1,0:T(8,128)S(1)}, s32[1]{0:T(128)}) custom-call(s32[32,128]{1,0:T(8,128)S(1)} %get-tuple-element.64.grid), custom_call_target="tpu_custom_call" | custom-call | flops 2000000 | bytes 100000 | tf_op jit(solution)/shard_map/tables/pallas_call | solution.py:765
  15.2 0.0 collective-permute-done.11.c4.c5
  15.2 0.0 collective-permute-done.10.m3
  15.2 1.7 %collective-permute-done.9.m2 = f32[296,128]{1,0:T(8,128)S(1)} collective-permute-done((f32[296,128]{1,0:T(8,128)S(1)}, f32[296,128]{1,0:T(8,128)S(1)}, u32[]{:S(2)}, u32[]{:S(2)}) %collective-permute-start.9) | collective-permute-done | bytes 151584 | tf_op jit(solution)/shard_map/ppermute | solution.py:657
  16.9 0.0 collective-permute-done.8.m1
  16.9 1.6 %pack.3 = f32[1024,128]{1,0:T(8,128)} custom-call(s32[8,128]{1,0:T(8,128)S(1)} %get-tuple-element.69.picks_hbm, f32[296,128]{1,0:T(8,128)S(1)} %get-tuple-element.70.m0, f32[296,128]{1,0:T(8,128)S(1)} %collective-permute-done.8.m1, f32[296,128]{1,0:T(8,128)S(1)} %collective-permute-done.9.m2, f32[296,128]{1,0:T(8,128)S(1)} %collective-permute-done.10.m3, ...), custom_call_target="tpu_custom_call" | custom-call | tf_op jit(solution)/shard_map/pack/pallas_call | solution.py:679
  18.5 8.4 %all-to-all-start.2 = ((f32[8,128,128]{2,1,0:T(8,128)}), f32[8,128,128]{2,1,0:T(8,128)S(1)}, u32[]{:S(2)}, u32[]{:S(2)}) async-start(f32[8,128,128]{2,1,0:T(8,128)} %bitcast.15), calls=%async_computation.2 | async-start | bytes 1048576 | tf_op jit(solution)/shard_map/all_to_all | solution.py:675
  26.9 6.0 %inner.3 = (f32[4,4,128,128]{3,2,1,0:T(8,128)S(1)}, f32[4,4,128,128]{3,2,1,0:T(8,128)S(1)}, f32[256,128]{1,0:T(8,128)S(1)}) custom-call(s32[8,128]{1,0:T(8,128)S(1)} %get-tuple-element.66.table.table_hbm, f32[4,4,128,128]{3,2,1,0:T(8,128)} %bitcast.28, f32[4,4,128,128]{3,2,1,0:T(8,128)} %bitcast.32), custom_call_target="tpu_custom_call" | custom-call | flops 60000000 | bytes 8000000 | tf_op jit(solution)/shard_map/inner/pallas_call | solution.py:795
  32.9 11.9 %all-to-all-done.2 = f32[8,128,128]{2,1,0:T(8,128)S(1)} async-done(((f32[8,128,128]{2,1,0:T(8,128)}), f32[8,128,128]{2,1,0:T(8,128)S(1)}, u32[]{:S(2)}, u32[]{:S(2)}) %all-to-all-start.2) | async-done | bytes 524320 | tf_op jit(solution)/shard_map/all_to_all | solution.py:675
  44.8 1.1 %sort.3 = (f32[264,128]{1,0:T(8,128)S(1)}, f32[264,128]{1,0:T(8,128)S(1)}) custom-call(s32[8,128]{1,0:T(8,128)S(1)} %get-tuple-element.66.table.table_hbm, f32[1024,128]{1,0:T(8,128)S(1)} %bitcast.26), custom_call_target="tpu_custom_call" | custom-call | tf_op jit(solution)/shard_map/sort/pallas_call | solution.py:698
  45.9 0.6 %collective-permute-start.12 = (f32[264,128]{1,0:T(8,128)S(1)}, f32[264,128]{1,0:T(8,128)S(1)}, u32[]{:S(2)}, u32[]{:S(2)}) collective-permute-start(f32[264,128]{1,0:T(8,128)S(1)} %get-tuple-element.79), channel_id=1, source_target_pairs={{0,1},{1,0},{2,3},{3,2},{4,5},{5,4},{6,7},{7,6},{8,9},{9,8},{10,11... | collective-permute-start | bytes 405512 | tf_op jit(solution)/shard_map/ppermute | solution.py:657
  47.1 0.3 collective-permute-done.12.other
  47.5 3.6 %final.3 = (f32[4,4,128,128]{3,2,1,0:T(8,128)}, f32[4,4,128,128]{3,2,1,0:T(8,128)}) custom-call(s32[8,128]{1,0:T(8,128)S(1)} %get-tuple-element.66.table.table_hbm, f32[512,128]{1,0:T(8,128)S(1)} %get-tuple-element.68.chip, f32[264,128]{1,0:T(8,128)S(1)} %get-tuple-element.78.own, f32[264,128]{1,0:T(8,128)S(1)} %collective-permute-done.12.other, ...), custom_call_target="tpu_custom_call" | custom-call | tf_op jit(solution)/shard_map/final/pallas_call | solution.py:816
  51.1 0.2 conditional.1
  (8 shorter events, 0.0 us)
Async XLA Ops:
  0.6 3.1 %copy-start.4 = (s32[26,34]{1,0:T(8,128)S(1)}, s32[26,34]{1,0:T(8,128)}, u32[]{:S(2)}) copy-start(s32[26,34]{1,0:T(8,128)} %land_hbm.1) | copy-start | bytes 10612
  0.6 3.1 %copy-start.5 = (s32[256]{0:T(256)S(1)}, s32[256]{0:T(256)}, u32[]{:S(2)}) copy-start(s32[256]{0:T(256)} %counts_hbm.1) | copy-start | bytes 3076
  2.9 2.4 %collective-permute-start.7 = (f32[256,128]{1,0:T(8,128)S(1)}, f32[256,128]{1,0:T(8,128)S(1)}, u32[]{:S(2)}, u32[]{:S(2)}) collective-permute-start(f32[256,128]{1,0:T(8,128)S(1)} %rims.3.mine.edges), channel_id=1, source_target_pairs={{0,1},{1,0},{2,3},{3,2},{4,5},{5,4},{6,7},{7,6},{8,9},{9,8},{10,11... | collective-permute-start | bytes 393224 | tf_op jit(solution)/shard_map/ppermute | solution.py:657
  6.0 9.2 %collective-permute-start.10 = (f32[296,128]{1,0:T(8,128)S(1)}, f32[296,128]{1,0:T(8,128)S(1)}, u32[]{:S(2)}, u32[]{:S(2)}) collective-permute-start(f32[296,128]{1,0:T(8,128)S(1)} %get-tuple-element.70.m0), channel_id=1, source_target_pairs={{12,60},{14,62},{28,76},{30,78},{49,1},{51,3},{65,17},{67,19}} | collective-permute-start | bytes 454664 | tf_op jit(solution)/shard_map/ppermute | solution.py:657
  9.2 7.7 %collective-permute-start.9 = (f32[296,128]{1,0:T(8,128)S(1)}, f32[296,128]{1,0:T(8,128)S(1)}, u32[]{:S(2)}, u32[]{:S(2)}) collective-permute-start(f32[296,128]{1,0:T(8,128)S(1)} %get-tuple-element.70.m0), channel_id=1, source_target_pairs={{0,32},{1,0},{2,34},{3,2},{4,36},{5,4},{6,38},{7,6},{8,40},{9,8},{... | collective-permute-start | bytes 454664 | tf_op jit(solution)/shard_map/ppermute | solution.py:657
  9.6 7.3 %collective-permute-start.8 = (f32[296,128]{1,0:T(8,128)S(1)}, f32[296,128]{1,0:T(8,128)S(1)}, u32[]{:S(2)}, u32[]{:S(2)}) collective-permute-start(f32[296,128]{1,0:T(8,128)S(1)} %get-tuple-element.70.m0), channel_id=1, source_target_pairs={{0,16},{1,0},{2,18},{3,2},{4,20},{5,4},{6,22},{7,6},{8,24},{9,8},{... | collective-permute-start | bytes 454664 | tf_op jit(solution)/shard_map/ppermute | solution.py:657
  12.5 2.7 %collective-permute-start.11 = (f32[8,128]{1,0:T(8,128)S(1)}, f32[8,128]{1,0:T(8,128)S(1)}, u32[]{:S(2)}, u32[]{:S(2)}) collective-permute-start(f32[8,128]{1,0:T(8,128)S(1)} %slice.44), channel_id=1, source_target_pairs={{0,64},{67,3}} | collective-permute-start | bytes 12296 | tf_op jit(solution)/shard_map/ppermute | solution.py:657
  18.5 26.3 %all-to-all-start.2 = ((f32[8,128,128]{2,1,0:T(8,128)}), f32[8,128,128]{2,1,0:T(8,128)S(1)}, u32[]{:S(2)}, u32[]{:S(2)}) async-start(f32[8,128,128]{2,1,0:T(8,128)} %bitcast.15), calls=%async_computation.2 | async-start | bytes 1048576 | tf_op jit(solution)/shard_map/all_to_all | solution.py:675
  45.9 1.6 %collective-permute-start.12 = (f32[264,128]{1,0:T(8,128)S(1)}, f32[264,128]{1,0:T(8,128)S(1)}, u32[]{:S(2)}, u32[]{:S(2)}) collective-permute-start(f32[264,128]{1,0:T(8,128)S(1)} %get-tuple-element.79), channel_id=1, source_target_pairs={{0,1},{1,0},{2,3},{3,2},{4,5},{5,4},{6,7},{7,6},{8,9},{9,8},{10,11... | collective-permute-start | bytes 405512 | tf_op jit(solution)/shard_map/ppermute | solution.py:657
  47.5 3.6 %copy-start = (f32[4,2,2,128,128]{4,3,2,1,0:T(8,128)S(1)}, f32[4,2,2,128,128]{4,3,2,1,0:T(8,128)}, u32[]{:S(2)}) copy-start(f32[4,2,2,128,128]{4,3,2,1,0:T(8,128)} %param.6) | copy-start | bytes 3145732
  47.5 3.6 %copy-start.2 = (f32[4,2,2,128,128]{4,3,2,1,0:T(8,128)S(1)}, f32[4,2,2,128,128]{4,3,2,1,0:T(8,128)}, u32[]{:S(2)}) copy-start(f32[4,2,2,128,128]{4,3,2,1,0:T(8,128)} %param.7) | copy-start | bytes 3145732
